TPU v7x, 512 devices: a whole 4x4x16 slice. The times are simulated.
512 devices in a mesh: grp: 16 (over z), pen: 32 (over x, y, core).
Axes of the slice: x: 4, y: 4, z: 16, core: 2. Of those that a mesh axis runs over, the one named last changes fastest.
Arguments:
- residual: float32 [512, 512, 512], P('grp', 'pen'), may hold values from -53 to 53
- direction: float32 [512, 512, 512], P('grp', 'pen'), may hold values from -74 to 74
- material: int32 [512, 512, 512], P('grp', 'pen'), may hold values 0 or 1
Outputs:
- new_residual: float32 [512, 512, 512], P('grp', 'pen')
- new_direction: float32 [512, 512, 512], P('grp', 'pen')
All inputs are finite; a program needn't handle non-finite values. No bound on the sum of `material` on one device may be relied on, other than what follows from the above.
Results may differ from a plain program's by a relative error of at most 0.000076.
Values sent between devices are 32-bit elements; how exact they have to be, the bound alone decides.
No kernel may reach another device: no remote copies, remote signals or barrier semaphores. Data moves between devices by JAX's collectives and lax.ppermute only.
A program may use at most 128 MiB of HBM per device.

v0:
```python
import math

import jax
import jax.numpy as jnp
from jax import lax
from jax.sharding import PartitionSpec as P

absorption = 0.02
mean_conduct = 5.0


def extended(block, sides, width):
    for axis, dim in sides:
        count = lax.axis_size(axis)
        forward = [(i, i + 1) for i in range(count - 1)]
        backward = [(target, source) for source, target in forward]
        low = lax.ppermute(
            lax.slice_in_dim(block, block.shape[dim] - width, None, axis=dim), axis, forward
        )
        high = lax.ppermute(lax.slice_in_dim(block, 0, width, axis=dim), axis, backward)
        block = jnp.concatenate([low, block, high], axis=dim)
    return block


def dct_matrix(length):
    degree = jnp.arange(length, dtype=jnp.int32)[:, None]
    sample = jnp.arange(length, dtype=jnp.int32)[None, :]
    phases = degree * (2 * sample + 1) % (4 * length)
    weight = jnp.where(degree == 0, math.sqrt(1.0 / length), math.sqrt(2.0 / length))
    return weight * jnp.cos(math.pi * phases.astype(jnp.float32) / (2.0 * length))


def eigen_values(modes, length):
    return 4.0 * jnp.sin(math.pi * modes.astype(jnp.float32) / (2.0 * length)) ** 2


def apply_operator(direction, stiffness):
    scaled = stiffness * direction
    padded = extended(scaled, (("grp", 0), ("pen", 1)), 1)
    beside = padded[2:, 1:-1] + padded[:-2, 1:-1] + padded[1:-1, 2:] + padded[1:-1, :-2]
    flat_zero = jnp.zeros_like(scaled[:, :, :1])
    beside = beside + jnp.concatenate([scaled[:, :, 1:], flat_zero], 2)
    beside = beside + jnp.concatenate([flat_zero, scaled[:, :, :-1]], 2)
    return absorption * direction + stiffness * (6.0 * scaled - beside)


def divide_modes(partial_x, along_y, depth_index, depth_len, full_x, full_y):
    highest = lax.Precision.HIGHEST
    spectrum = jnp.einsum("lapy,bpy->lab", partial_x, along_y, precision=highest)
    eigen_x = eigen_values(jnp.arange(full_x, dtype=jnp.int32), full_x)
    eigen_y = eigen_values(jnp.arange(full_y, dtype=jnp.int32), full_y)
    eigen_z = eigen_values(depth_index, depth_len)
    spectrum = spectrum / (
        absorption
        + mean_conduct * (eigen_z[:, None, None] + eigen_x[None, :, None] + eigen_y[None, None, :])
    )
    return jnp.einsum("lab,bpy->lapy", spectrum, along_y, precision=highest)


def precondition(fields):
    highest = lax.Precision.HIGHEST
    cells_x, cells_y, depth_len = fields[0].shape
    groups = lax.axis_size("grp")
    pencils = lax.axis_size("pen")
    planes_dev = depth_len // (groups * pencils)
    full_x = cells_x * groups
    full_y = cells_y * pencils
    along_z = dct_matrix(depth_len)
    along_x = dct_matrix(full_x).reshape(full_x, groups, cells_x)
    along_y = dct_matrix(full_y).reshape(full_y, pencils, cells_y)
    spectra = tuple(
        (
            jnp.einsum("xyz,kz->kxy", one_field, along_z, precision=highest).reshape(
                depth_len, cells_x * cells_y
            )
            for one_field in fields
        )
    )
    layers = jnp.arange(planes_dev, dtype=jnp.int32)
    outward = []
    planes = lax.all_to_all(
        lax.all_to_all(spectra, "pen", split_axis=0, concat_axis=1, tiled=True),
        "grp",
        split_axis=0,
        concat_axis=1,
        tiled=True,
    )
    depth_index = (
        lax.axis_index("pen") * (depth_len // pencils) + lax.axis_index("grp") * planes_dev + layers
    )
    for one_plane in planes:
        grouped = one_plane.reshape(planes_dev, groups, pencils, cells_x, cells_y)
        partial_x = jnp.einsum("lgpxy,agx->lapy", grouped, along_x, precision=highest)
        solved = divide_modes(partial_x, along_y, depth_index, depth_len, full_x, full_y)
        outward.append(
            jnp.einsum("lapy,agx->lgpxy", solved, along_x, precision=highest).reshape(
                planes_dev, groups * pencils * cells_x * cells_y
            )
        )
    bricks = lax.all_to_all(
        lax.all_to_all(tuple(outward), "grp", split_axis=1, concat_axis=0, tiled=True),
        "pen",
        split_axis=1,
        concat_axis=0,
        tiled=True,
    )
    return tuple(
        (
            jnp.einsum(
                "kxy,kz->xyz",
                one_brick.reshape(depth_len, cells_x, cells_y),
                along_z,
                precision=highest,
            )
            for one_brick in bricks
        )
    )


def on_device(residual, direction, material):
    stiffness = jnp.sqrt(1.0 + 29.0 * material.astype(jnp.float32))
    operated = apply_operator(direction, stiffness)
    curvature, projection = lax.psum(
        (jnp.sum(direction * operated), jnp.sum(residual * direction)), ("grp", "pen")
    )
    step_size = projection / curvature
    new_residual = residual - step_size * operated
    smoothed = precondition((new_residual,))[0]
    conjugacy = lax.psum(jnp.sum(smoothed * operated), ("grp", "pen"))
    new_direction = smoothed - conjugacy / curvature * direction
    return (new_residual, new_direction)


def solution(mesh):
    placed = (P("grp", "pen", None), P("grp", "pen", None), P("grp", "pen", None))
    return jax.shard_map(
        on_device,
        mesh=mesh,
        in_specs=placed,
        out_specs=(P("grp", "pen", None), P("grp", "pen", None)),
        check_vma=False,
    )
```

profile of v0, /device:TPU:1, one launch (start us, length us, event | category | flops | bytes accessed | tf_op | source)
XLA Modules:
  0.0 525.8 jit_solution(4276732010022580109)
XLA Ops:
  0.7 2.1 fusion.59
  2.7 1.3 collective-permute-start
  4.0 5.0 collective-permute-start.1
  10.2 8.9 %collective-permute-start.2 = (f32[34,1,512]{2,1,0:T(1,128)S(1)}, f32[34,1,512]{2,1,0:T(1,128)S(1)}, u32[]{:S(2)}, u32[]{:S(2)}) collective-permute-start(f32[34,1,512]{2,1,0:T(1,128)S(1)} %get-tuple-element.7), channel_id=1, source_target_pairs={{1,0},{2,1},{3,2},{4,3},{5,4},{6,5},{7,6},{8,7},{9,8},{10,9},{11,1... | collective-permute-start | bytes 208904 | tf_op jit(solution)/shard_map/ppermute | solution.py:20
  19.1 1.9 collective-permute-start.3
  21.0 1.3 collective-permute-done.3
  22.4 1.8 multiply_reduce_fusion.1
  24.2 109.5 %all-reduce.2 = (f32[]{:T(128)}, f32[]{:T(128)}) all-reduce(f32[]{:T(128)} %get-tuple-element.3, f32[]{:T(128)} %get-tuple-element.2), channel_id=1, replica_groups=mesh['grp'=16,'pen'=32] {'grp','pen'}, use_global_device_ids=true, to_apply=%region_1.0 | all-reduce | flops 2 | bytes 16 | tf_op jit(solution)/shard_map/psum | solution.py:123
  136.2 6.2 %fusion.39 = f32[512,32,16]{0,1,2:T(8,128)S(1)} fusion(f32[32,16,512]{2,1,0:T(8,128)S(1)} %multiply_subtract_fusion.1, s32[512]{0:T(512)S(1)} %multiply_add_fusion.2, f32[512]{0:T(512)S(1)} %fusion.85), kind=kOutput, calls=%fused_computation.62 | convolution fusion | flops 1614544896 | bytes 2101248 | tf_op jit(solution)/shard_map/xyz,kz->kxy/dot_general | solution.py:73
  142.5 7.5 %copy.13 = f32[512,32,16]{2,1,0:T(8,128)} copy(f32[512,32,16]{0,1,2:T(8,128)S(1)} %fusion.39) | data formatting | bytes 2097152 | tf_op jit(solution)/shard_map/xyz,kz->kxy/dot_general | solution.py:73
  150.0 7.6 %all_to_all.44 = f32[32,16,512]{2,1,0:T(8,128)S(1)} reshape(f32[512,32,16]{2,1,0:T(8,128)} %copy.13) | data formatting | bytes 2097152 | tf_op jit(solution)/shard_map/all_to_all | solution.py:82
  157.6 21.2 %all_to_all.60 = f32[32,16,512]{2,1,0:T(8,128)S(1)} all-to-all(f32[32,16,512]{2,1,0:T(8,128)S(1)} %all_to_all.44), channel_id=1, replica_groups=mesh['grp'=16,'pen'=32] {'pen'}, dimensions={0} | all-to-all | bytes 2097152 | tf_op jit(solution)/shard_map/all_to_all | solution.py:82
  179.3 2.3 all_to_all.54
  181.6 7.5 %all-to-all-start.1 = ((f32[16,1,16384]{2,1,0:T(1,128)}), f32[16,1,16384]{2,1,0:T(1,128)}, u32[]{:S(2)}, u32[]{:S(2)}) async-start(f32[16,1,16384]{2,1,0:T(1,128)} %all_to_all.54), calls=%async_computation.1 | async-start | bytes 2097152 | tf_op jit(solution)/shard_map/all_to_all | solution.py:81
  189.3 4.9 fusion.28
  194.2 41.3 %all-to-all-done.1 = f32[16,1,16384]{2,1,0:T(1,128)} async-done(((f32[16,1,16384]{2,1,0:T(1,128)}), f32[16,1,16384]{2,1,0:T(1,128)}, u32[]{:S(2)}, u32[]{:S(2)}) %all-to-all-start.1) | async-done | bytes 1048608 | tf_op jit(solution)/shard_map/all_to_all | solution.py:81
  235.5 3.8 reduce
  239.2 4.8 reshape.208
  244.0 9.0 %copy.22 = f32[16,32,32,16]{1,2,0,3:T(8,128)} copy(f32[16,32,32,16]{3,2,1,0:T(8,128)} %reshape.208) | data formatting | bytes 2097152 | tf_op jit(solution)/shard_map/reshape.3
  253.1 13.2 %convolution_bitcast_fusion.3 = f32[512,32,16]{0,1,2:T(8,128)S(1)} fusion(f32[16,32,32,16]{1,2,0,3:T(8,128)} %copy.22, s32[16,32]{1,0:T(8,128)S(1)} %multiply_add_fusion.1, f32[512]{0:T(512)S(1)} %fusion.85), kind=kOutput, calls=%fused_computation.17 | convolution fusion | flops 1614544896 | bytes 2101248 | tf_op jit(solution)/shard_map/lgpxy,agx->lapy/dot_general | solution.py:93
  266.3 3.1 fusion.3
  269.4 5.9 %convolution_bitcast_fusion.1 = f32[512,32,16,1]{0,1,2,3:T(8,128)S(1)} fusion(f32[512,512,1]{1,0,2:T(8,128)S(1)} %fusion.3, s32[32,16]{0,1:T(8,128)S(1)} %multiply_add_fusion, f32[512]{0:T(512)S(1)} %fusion.85), kind=kOutput, calls=%fused_computation.15 | convolution fusion | flops 1614544896 | bytes 2101248 | tf_op jit(solution)/shard_map/lab,bpy->lapy/dot_general | solution.py:57
  275.4 12.1 %convolution_bitcast_fusion = f32[1,16,32,32,16]{2,3,4,1,0:T(8,128)} fusion(f32[512,32,16,1]{0,1,2,3:T(8,128)S(1)} %convolution_bitcast_fusion.1, s32[16,32]{1,0:T(8,128)S(1)} %multiply_add_fusion.1, f32[512]{0:T(512)S(1)} %fusion.85), kind=kOutput, calls=%fused_computation.2 | convolution fusion | flops 1614544896 | bytes 2101248 | tf_op jit(solution)/shard_map/lapy,agx->lgpxy/dot_general | solution.py:96
  287.5 9.1 %copy.18 = f32[1,16,32,32,16]{4,3,2,1,0:T(8,128)} copy(f32[1,16,32,32,16]{2,3,4,1,0:T(8,128)} %convolution_bitcast_fusion) | data formatting | bytes 2097152 | tf_op jit(solution)/shard_map/lapy,agx->lgpxy/transpose | solution.py:96
  296.6 6.3 %all_to_all.55 = f32[1,16,16384]{2,0,1:T(1,128)S(1)} reshape(f32[1,16,32,32,16]{4,3,2,1,0:T(8,128)} %copy.18) | data formatting | bytes 2097152 | tf_op jit(solution)/shard_map/all_to_all | solution.py:101
  303.0 57.0 %all_to_all.61 = f32[1,16,16384]{2,0,1:T(1,128)} all-to-all(f32[1,16,16384]{2,0,1:T(1,128)S(1)} %all_to_all.55), channel_id=1, replica_groups=mesh['grp'=16,'pen'=32] {'grp'}, dimensions={1} | all-to-all | bytes 2097152 | tf_op jit(solution)/shard_map/all_to_all | solution.py:101
  360.0 3.8 reduce.1
  363.8 27.4 %all_to_all.62 = f32[16,32,512]{2,0,1:T(8,128)S(1)} all-to-all(f32[16,32,512]{2,0,1:T(8,128)S(1)} %bitcast.46), channel_id=1, replica_groups=mesh['grp'=16,'pen'=32] {'pen'}, dimensions={1} | all-to-all | bytes 2097152 | tf_op jit(solution)/shard_map/all_to_all | solution.py:100
  391.2 5.0 reshape.209
  396.3 24.7 %multiply_reduce_fusion = (f32[]{:T(128)}, f32[32,16,512]{2,1,0:T(8,128)S(1)}) fusion(f32[32,16,512]{2,1,0:T(8,128)S(1)} %get-tuple-element.6, s32[512]{0:T(512)S(1)} %multiply_add_fusion.2, f32[512]{0:T(512)S(1)} %fusion.85, f32[512,32,16]{2,1,0:T(8,128)} %reshape.209), kind=kOutput, calls=%fused_computation.65 | convolution fusion | flops 1615069184 | bytes 3149828 | tf_op jit(solution)/shard_map/kxy,kz->xyz/dot_general | solution.py:109
  421.0 102.1 %psum.23 = f32[]{:T(128)} all-reduce(f32[]{:T(128)} %get-tuple-element.13), channel_id=1, replica_groups=mesh['grp'=16,'pen'=32] {'grp','pen'}, use_global_device_ids=true, to_apply=%region_5.6 | all-reduce | flops 1 | bytes 8 | tf_op jit(solution)/shard_map/psum | solution.py:129
  524.3 1.2 multiply_subtract_fusion
  (24 shorter events, 3.1 us)
Async XLA Ops:
  0.6 21.7 %copy-start = (f32[32,16,512]{2,1,0:T(8,128)S(1)}, f32[32,16,512]{2,1,0:T(8,128)}, u32[]{:S(2)}) copy-start(f32[32,16,512]{2,1,0:T(8,128)} %param.4) | copy-start | bytes 3145732
  0.6 21.7 %copy-start.1 = (s32[32,16,512]{2,1,0:T(8,128)S(1)}, s32[32,16,512]{2,1,0:T(8,128)}, u32[]{:S(2)}) copy-start(s32[32,16,512]{2,1,0:T(8,128)} %param.5) | copy-start | bytes 3145732
  0.6 21.7 %copy-start.2 = (f32[32,16,512]{2,1,0:T(8,128)S(1)}, f32[32,16,512]{2,1,0:T(8,128)}, u32[]{:S(2)}) copy-start(f32[32,16,512]{2,1,0:T(8,128)} %param.3) | copy-start | bytes 3145732
  2.7 6.7 %collective-permute-start = (f32[1,16,512]{2,1,0:T(8,128)S(1)}, f32[1,16,512]{2,1,0:T(8,128)S(1)}, u32[]{:S(2)}, u32[]{:S(2)}) collective-permute-start(f32[1,16,512]{2,1,0:T(8,128)S(1)} %get-tuple-element.10), channel_id=1, source_target_pairs={{32,0},{64,32},{96,64},{128,96},{160,128},{192,160},{224,192},{256... | collective-permute-start | bytes 98312 | tf_op jit(solution)/shard_map/ppermute | solution.py:20
  4.0 6.0 %collective-permute-start.1 = (f32[1,16,512]{2,1,0:T(8,128)S(1)}, f32[1,16,512]{2,1,0:T(8,128)S(1)}, u32[]{:S(2)}, u32[]{:S(2)}) collective-permute-start(f32[1,16,512]{2,1,0:T(8,128)S(1)} %get-tuple-element.9), channel_id=1, source_target_pairs={{0,32},{32,64},{64,96},{96,128},{128,160},{160,192},{192,224},{224... | collective-permute-start | bytes 98312 | tf_op jit(solution)/shard_map/ppermute | solution.py:17
  10.2 10.9 %collective-permute-start.2 = (f32[34,1,512]{2,1,0:T(1,128)S(1)}, f32[34,1,512]{2,1,0:T(1,128)S(1)}, u32[]{:S(2)}, u32[]{:S(2)}) collective-permute-start(f32[34,1,512]{2,1,0:T(1,128)S(1)} %get-tuple-element.7), channel_id=1, source_target_pairs={{1,0},{2,1},{3,2},{4,3},{5,4},{6,5},{7,6},{8,7},{9,8},{10,9},{11,1... | collective-permute-start | bytes 208904 | tf_op jit(solution)/shard_map/ppermute | solution.py:20
  19.1 3.3 collective-permute-start.3
  135.3 1.0 copy-start.3
  181.6 53.9 %all-to-all-start.1 = ((f32[16,1,16384]{2,1,0:T(1,128)}), f32[16,1,16384]{2,1,0:T(1,128)}, u32[]{:S(2)}, u32[]{:S(2)}) async-start(f32[16,1,16384]{2,1,0:T(1,128)} %all_to_all.54), calls=%async_computation.1 | async-start | bytes 2097152 | tf_op jit(solution)/shard_map/all_to_all | solution.py:81
  244.0 22.3 %copy-start.4 = (f32[512,32,16]{0,1,2:T(8,128)S(1)}, f32[512,32,16]{0,1,2:T(8,128)}, u32[]{:S(2)}) copy-start(f32[512,32,16]{0,1,2:T(8,128)} %fusion.28) | copy-start | bytes 3145732
where the time goes:
time: 529 us; the launch traced here: 526 us
  blocking collectives  317 us (60%)
  matrix products  65.3 us (12%)
  local copies, waits for them, and re-layouts  53.8 us (10%)
  waiting for transfers between devices  43.2 us (8%)
  starting transfers between devices  24.6 us (5%)
  other arithmetic  17.9 us (3%)
    psum x1, blocking collectives, on_device(): lax.psum((jnp.sum(direction * operated), jnp.sum(residual * direction)),...  110 us
    psum x1, blocking collectives, on_device(): conjugacy = lax.psum(jnp.sum(smoothed * operated), ('grp', 'pen'))  102 us
    all_to_all x1, blocking collectives, precondition(): lax.all_to_all(tuple(outward), 'grp', split_axis=1, concat_axis=0, tiled=...  57 us
    all_to_all x1, waiting for transfers between devices, precondition(): lax.all_to_all(lax.all_to_all(spectra, 'pen', split_axis=0, concat_axis=1...  41.3 us
    all_to_all x1, blocking collectives, precondition(): lax.all_to_all(lax.all_to_all(tuple(outward), 'grp', split_axis=1, concat...  27.4 us
    dot_general x1, matrix products, precondition(): jnp.einsum('kxy,kz->xyz', one_brick.reshape(depth_len, cells_x, cells_y),...  24.7 us
    all_to_all x1, blocking collectives, precondition(): lax.all_to_all(spectra, 'pen', split_axis=0, concat_axis=1, tiled=True)  21.2 us
    another operation x2, local copies, waits for them, and re-layouts  13.8 us
  transfers between devices with their start and end apart: 5, of which 3 were waited for; matrix products, arithmetic and copies ran while one was open for 1% of the time, Pallas kernels for 0%

commit v1 on v0

v1 whole, which is shorter than its diff:
```python
import functools
import math

import jax
import jax.numpy as jnp
import numpy as np
from jax import lax
from jax.experimental import pallas as pl
from jax.experimental.pallas import tpu as pltpu
from jax.sharding import PartitionSpec as P

N = 512
GRP = 16
PEN = 32
BX = N // GRP
BY = N // PEN
BK = N // PEN
ABSORPTION = 0.02
CONDUCT = 5.0
SOLID = math.sqrt(30.0)
F32 = jnp.float32
VMEM = pl.BlockSpec(memory_space=pltpu.VMEM)
SMEM = pl.BlockSpec(memory_space=pltpu.SMEM)
PARAMS = pltpu.CompilerParams(vmem_limit_bytes=48 * 1024 * 1024)


def dct_matrix():
    k = np.arange(N)[:, None]
    n = np.arange(N)[None, :]
    weight = np.where(k == 0, math.sqrt(1.0 / N), math.sqrt(2.0 / N))
    return (weight * np.cos(math.pi * (k * (2 * n + 1) % (4 * N)) / (2.0 * N))).astype(np.float32)


def eigen_values():
    return (4.0 * np.sin(math.pi * np.arange(N) / (2.0 * N)) ** 2).astype(np.float32)


def matmul(a, b, dims):
    return lax.dot_general(
        a, b, (dims, ((), ())), precision=lax.Precision.HIGHEST, preferred_element_type=F32
    )


def decay(shift):
    rho = 2.0 / (2.0 + shift + jnp.sqrt(shift * (shift + 4.0)))
    return rho, rho / (CONDUCT * (1.0 - rho * rho))


def swap_units(rows):
    rows = list(rows)
    unit = lax.broadcasted_iota(jnp.int32, rows[0].shape, 1) // 16
    for d in (4, 2, 1):
        keep = (unit & d) == 0
        for i in range(8):
            if i & d == 0:
                a, b = rows[i], rows[i + d]
                rows[i] = jnp.where(keep, a, pltpu.roll(b, 16 * d, 1))
                rows[i + d] = jnp.where(keep, pltpu.roll(a, 128 - 16 * d, 1), b)
    return rows


def to_tile(x):
    x = x[:8] + x[8:]
    return x[:, 0:128] + x[:, 128:256] + x[:, 256:384] + x[:, 384:512]


def fold(x, step):
    return x + pltpu.roll(x, step, 0)


def stiffness_of(material):
    return jnp.where(material == 1, jnp.float32(SOLID), jnp.float32(1.0))


def faces_kernel(d_ref, m_ref, xlo_ref, xhi_ref, ylo_ref, yhi_ref):
    xlo_ref[0] = stiffness_of(m_ref[0]) * d_ref[0]
    xhi_ref[0] = stiffness_of(m_ref[BX - 1]) * d_ref[BX - 1]
    ylo_ref[...] = stiffness_of(m_ref[:, 0, :]) * d_ref[:, 0, :]
    yhi_ref[...] = stiffness_of(m_ref[:, BY - 1, :]) * d_ref[:, BY - 1, :]


def forward_kernel(r_ref, d_ref, m_ref, xl_ref, xh_ref, yl_ref, yh_ref, c_ref, q_ref, send_ref, u_ref):
    u_ref[0] = xl_ref[0]
    u_ref[BX + 1] = xh_ref[0]

    def scale(x, _):
        u_ref[x + 1] = stiffness_of(m_ref[x]) * d_ref[x]
        return 0

    lax.fori_loop(0, BX, scale, 0)
    row = lax.broadcasted_iota(jnp.int32, (BY, N), 0)
    lane = lax.broadcasted_iota(jnp.int32, (BY, N), 1)

    def stencil(x, sums):
        u = u_ref[x + 1]
        d = d_ref[x]
        beside = u_ref[x] + u_ref[x + 2]
        beside += jnp.where(row == 0, yl_ref[pl.ds(x, 1), :], pltpu.roll(u, 1, 0))
        beside += jnp.where(row == BY - 1, yh_ref[pl.ds(x, 1), :], pltpu.roll(u, BY - 1, 0))
        beside += jnp.where(lane == 0, 0.0, pltpu.roll(u, 1, 1))
        beside += jnp.where(lane == N - 1, 0.0, pltpu.roll(u, N - 1, 1))
        q = ABSORPTION * d + stiffness_of(m_ref[x]) * (6.0 * u - beside)
        q_ref[x] = q
        return sums[0] + to_tile(d * q), sums[1] + to_tile(r_ref[x] * d)

    zero = jnp.zeros((8, 128), F32)
    curvature, projection = lax.fori_loop(0, BX, stencil, (zero, zero))
    half = lax.broadcasted_iota(jnp.int32, (8, 128), 0) < 4
    sums = jnp.where(half, fold(curvature, 4), fold(projection, 4))
    for field, ref in enumerate((r_ref, q_ref)):
        modes = matmul(c_ref[...], ref[...].reshape(BX * BY, N), ((1,), (1,)))
        for b in range(4):
            part = modes[:, 128 * b : 128 * b + 128].reshape(PEN, 2, 8, 128)
            for a in range(2):
                send_ref[:, 8 * field + 4 * a + b] = part[:, a]
    for j in range(PEN):
        send_ref[j, 16] = sums


def blocks_kernel(recv_ref, c_ref, ez_ref, ey_ref, fr_ref, fq_ref, send_ref, y_ref):
    for field, out_ref in enumerate((fr_ref, fq_ref)):
        for b in range(4):
            for s in range(4):
                for a in range(2):
                    t = 8 * field + 4 * a + b
                    rows = swap_units([recv_ref[8 * s + i, t] for i in range(8)])
                    for i in range(8):
                        y_ref[8 * b + i, 8 * a : 8 * a + 8, 128 * s : 128 * s + 128] = rows[i]
        out_ref[...] = matmul(y_ref[...].reshape(BX * BK, N), c_ref[...], ((1,), (1,))).reshape(BX, BK, N)

    dots = [jnp.zeros((8, 128), F32), jnp.zeros((8, 128), F32)]
    k0 = lax.axis_index("pen") * BK
    for h in range(2):
        rows = pl.ds(8 * h, 8)
        ez = jnp.concatenate(
            [jnp.full((1, N), ez_ref[k0 + 8 * h + i], F32) for i in range(8)], axis=0
        )
        rho, factor = decay(ABSORPTION / CONDUCT + ez + ey_ref[...])

        def sweep(x, carry):
            power, vr, vq, wr, wq, rq, qq = carry
            r = fr_ref[x, rows]
            q = fq_ref[x, rows]
            vr = r + rho * vr
            vq = q + rho * vq
            wr = wr + power * r
            wq = wq + power * q
            rq = rq + (vr * q + vq * r - r * q)
            qq = qq + (2.0 * vq - q) * q
            return power * rho, vr, vq, wr, wq, rq, qq

        zero = jnp.zeros((8, N), F32)
        carry = lax.fori_loop(0, BX, sweep, (jnp.ones((8, N), F32),) + (zero,) * 6)
        _, vr, vq, wr, wq, rq, qq = carry
        for t, parts in enumerate(((vr, wr), (vq, wq))):
            for side, x in enumerate(parts):
                for b in range(4):
                    for i in range(8):
                        send_ref[8 * h + i, t, 4 * side + b : 4 * side + b + 1, :] = x[
                            i : i + 1, 128 * b : 128 * b + 128
                        ]
        for i, x in enumerate((rq, qq)):
            x = factor * x
            dots[i] += x[:, 0:128] + x[:, 128:256] + x[:, 256:384] + x[:, 384:512]

    sums = recv_ref[0, 16]
    for j in range(1, PEN):
        sums = sums + recv_ref[j, 16]
    row = lax.broadcasted_iota(jnp.int32, (8, 128), 0)
    sums = fold(sums, 6)
    rq = fold(fold(dots[0], 4), 2)
    qq = fold(fold(dots[1], 4), 2)
    sums = jnp.where(
        row < 2, sums, jnp.where(row < 4, pltpu.roll(sums, 6, 0), jnp.where(row < 6, rq, qq))
    )
    for j in range(GRP):
        send_ref[j, 2] = sums


def interface_kernel(recv_ref, ez_ref, ey_ref, send_ref, control_ref):
    row = lax.broadcasted_iota(jnp.int32, (8, 128), 0)
    sums = recv_ref[0, 2]
    for p in range(1, GRP):
        sums = sums + recv_ref[p, 2]

    def total(low):
        return jnp.full((8, 128), jnp.sum(jnp.where((row >= low) & (row < low + 2), sums, 0.0)), F32)

    curvature, projection, rq, qq = total(0), total(2), total(4), total(6)
    step = projection / curvature
    ez = ez_ref[lax.axis_index("pen") * BK + lax.axis_index("grp")]
    rho, factor = decay(ABSORPTION / CONDUCT + ez + ey_ref[...])
    across = rho
    for _ in range(5):
        across = across * across
    tiles = [recv_ref[p, 0] - step * recv_ref[p, 1] for p in range(GRP)]
    zero = jnp.zeros((8, 128), F32)
    rising = [zero]
    for p in range(GRP):
        rising.append(tiles[p] + across * rising[-1])
    falling = [zero]
    for p in reversed(range(GRP)):
        falling.append(tiles[p] + across * falling[-1])
    lower = row < 4
    ends = jnp.where(lower, rising[GRP], falling[GRP])
    powers = [jnp.ones((8, 128), F32)]
    for p in range(GRP):
        powers.append(powers[-1] * across)
    whole = powers[GRP]
    images = (pltpu.roll(ends, 4, 0) + whole * ends) / (1.0 - whole * whole)
    dots = zero
    for p in range(GRP):
        state = jnp.where(
            lower,
            rising[p] + powers[p] * images,
            falling[GRP - 1 - p] + powers[GRP - 1 - p] * images,
        )
        send_ref[p, 0] = state
        dots = dots + state * pltpu.roll(recv_ref[p, 1], 4, 0)
    dots = rho * factor * dots
    for p in range(GRP):
        send_ref[p, 1] = dots
    control_ref[0] = step
    control_ref[1] = curvature
    control_ref[2] = rq - step * qq


def solve_kernel(fr_ref, fq_ref, recv_ref, control_ref, c_ref, ez_ref, ey_ref, send_ref, f_ref, u_ref, y_ref):
    step = control_ref[0, 0:1, 0:1]
    k0 = lax.axis_index("pen") * BK
    for h in range(2):
        rows = pl.ds(8 * h, 8)
        ez = jnp.concatenate(
            [jnp.full((1, N), ez_ref[k0 + 8 * h + i], F32) for i in range(8)], axis=0
        )
        rho, factor = decay(ABSORPTION / CONDUCT + ez + ey_ref[...])

        def state(side):
            return jnp.concatenate(
                [
                    jnp.concatenate(
                        [recv_ref[8 * h + i, 0, 4 * side + b : 4 * side + b + 1, :] for i in range(8)],
                        axis=0,
                    )
                    for b in range(4)
                ],
                axis=1,
            )

        def rise(x, carry):
            f = fr_ref[x, rows] - step * fq_ref[x, rows]
            carry = f + rho * carry
            f_ref[x] = f
            u_ref[x, rows] = carry
            return carry

        def fall(i, carry):
            x = BX - 1 - i
            f = f_ref[x]
            u_ref[x, rows] = factor * (u_ref[x, rows] + rho * carry)
            return f + rho * carry

        lax.fori_loop(0, BX, rise, state(0))
        lax.fori_loop(0, BX, fall, state(1))

    y_ref[...] = matmul(u_ref[...].reshape(BX * BK, N), c_ref[...], ((1,), (0,))).reshape(BX, BK, N)
    for b in range(4):
        for s in range(4):
            for a in range(2):
                rows = swap_units(
                    [y_ref[8 * b + i, 8 * a : 8 * a + 8, 128 * s : 128 * s + 128] for i in range(8)]
                )
                for i in range(8):
                    send_ref[8 * s + i, 4 * a + b] = rows[i]
    sums = recv_ref[0, 1]
    for p in range(1, GRP):
        sums = sums + recv_ref[p, 1]
    first = (lax.broadcasted_iota(jnp.int32, (8, 128), 0) == 0) & (
        lax.broadcasted_iota(jnp.int32, (8, 128), 1) == 0
    )
    sums = sums + jnp.where(first, control_ref[2], 0.0)
    for j in range(PEN):
        send_ref[j, 8] = sums


def finish_kernel(recv_ref, r_ref, d_ref, q_ref, control_ref, c_ref, nr_ref, nd_ref, g_ref):
    for b in range(4):
        for a in range(2):
            g_ref[:, a, :, 128 * b : 128 * b + 128] = recv_ref[:, 4 * a + b]
    sums = recv_ref[0, 8]
    for j in range(1, PEN):
        sums = sums + recv_ref[j, 8]
    step = control_ref[0, 0:1, 0:1]
    conjugacy = jnp.full((8, 128), jnp.sum(sums), F32)
    ratio = (conjugacy / control_ref[1])[0:1, 0:1]
    smoothed = matmul(g_ref[...].reshape(N, BX * BY), c_ref[...], ((0,), (0,)))
    nd_ref[...] = smoothed.reshape(BX, BY, N) - ratio * d_ref[...]
    nr_ref[...] = r_ref[...] - step * q_ref[...]


def shape(*dims):
    return jax.ShapeDtypeStruct(dims, F32)


def call(kernel, ins, outs, scratch=()):
    return pl.pallas_call(
        kernel,
        in_specs=ins,
        out_specs=[VMEM] * len(outs),
        out_shape=outs,
        scratch_shapes=[pltpu.VMEM(s, F32) for s in scratch],
        compiler_params=PARAMS,
    )


def exchange(x, axis):
    return lax.all_to_all(x, axis, 0, 0)


def on_device(residual, direction, material):
    matrix = jnp.asarray(dct_matrix())
    eigen = eigen_values()
    ez = jnp.asarray(eigen)
    ey_row = jnp.asarray(eigen[None, :])
    ey_tile = jnp.asarray(np.concatenate([eigen.reshape(4, 128)] * 2, 0))
    block = shape(BX, BY, N)

    xlo, xhi, ylo, yhi = call(
        faces_kernel, [VMEM] * 2, [shape(1, BY, N), shape(1, BY, N), shape(BX, N), shape(BX, N)]
    )(direction, material)

    def up(x, axis, count):
        return lax.ppermute(x, axis, [(i, i + 1) for i in range(count - 1)])

    def down(x, axis, count):
        return lax.ppermute(x, axis, [(i + 1, i) for i in range(count - 1)])

    xl, xh = up(xhi, "grp", GRP), down(xlo, "grp", GRP)
    yl, yh = up(yhi, "pen", PEN), down(ylo, "pen", PEN)

    operated, send = call(
        forward_kernel, [VMEM] * 8, [block, shape(PEN, 17, 8, 128)], [(BX + 2, BY, N)]
    )(residual, direction, material, xl, xh, yl, yh, matrix)

    recv = exchange(send, "pen")
    field_r, field_q, send = call(
        blocks_kernel, [VMEM, VMEM, SMEM, VMEM], [block, block, shape(GRP, 3, 8, 128)], [(BX, BK, N)]
    )(recv, matrix, ez, ey_row)

    recv = exchange(send, "grp")
    send, control = call(
        interface_kernel, [VMEM, SMEM, VMEM], [shape(GRP, 2, 8, 128), shape(3, 8, 128)]
    )(recv, ez, ey_tile)

    recv = exchange(send, "grp")
    (send,) = call(
        solve_kernel,
        [VMEM] * 5 + [SMEM, VMEM],
        [shape(PEN, 9, 8, 128)],
        [(BX, 8, N), (BX, BK, N), (BX, BK, N)],
    )(field_r, field_q, recv, control, matrix, ez, ey_row)

    recv = exchange(send, "pen")
    return tuple(
        call(finish_kernel, [VMEM] * 6, [block, block], [(PEN, 2, 8, BX * BY)])(
            recv, residual, direction, operated, control, matrix
        )
    )


def solution(mesh):
    placed = P("grp", "pen", None)
    return jax.shard_map(
        on_device,
        mesh=mesh,
        in_specs=(placed, placed, placed),
        out_specs=(placed, placed),
        check_vma=False,
    )
```

time: 529 us -> 155 us (0.29)
  blocking collectives: 317 us -> 111 us
  matrix products: 65.3 us -> 0 us
  local copies, waits for them, and re-layouts: 53.8 us -> 2.56 us
  waiting for transfers between devices: 43.2 us -> 3.69 us
  Pallas kernels: 0 us -> 23.3 us
  other arithmetic: 17.9 us -> 0 us
  starting transfers between devices: 24.6 us -> 12.8 us
    psum x2 -> x0, blocking collectives: 212 us -> none  [the longest x1 110 us: on_device(): lax.psum((jnp.sum(direction * operated), jnp.sum(residual * direction)),...]
    dot_general x6 -> x0, matrix products: 65.3 us -> none  [the longest x1 24.7 us: precondition(): jnp.einsum('kxy,kz->xyz', one_brick.reshape(depth_len, cells_x, cells_y),...]
    all_to_all x1 -> x0, waiting for transfers between devices: 41.3 us -> none  [precondition(): lax.all_to_all(lax.all_to_all(spectra, 'pen', split_axis=0, concat_axis=1...]
    pallas_call x0 -> x6, Pallas kernels: none -> 23.3 us  [the longest x1 8.38 us: on_device(): call(forward_kernel, [VMEM] * 8, [block, shape(PEN, 17, 8, 128)], [(BX +...]
    all_to_all x5 -> x0, local copies, waits for them, and re-layouts: 16.9 us -> none  [the longest x2 8.21 us: precondition(): lax.all_to_all(spectra, 'pen', split_axis=0, concat_axis=1, tiled=True)]
    another operation x2 -> x0, local copies, waits for them, and re-layouts: 13.8 us -> none
    transpose x1 -> x0, local copies, waits for them, and re-layouts: 9.13 us -> none  [precondition(): jnp.einsum('lapy,agx->lgpxy', solved, along_x, precision=highest)]
    dot_general x1 -> x0, local copies, waits for them, and re-layouts: 7.5 us -> none  [precondition(): jnp.einsum('xyz,kz->kxy', one_field, along_z, precision=highest)]
  transfers between devices with their start and end apart: 5 -> 4, of which waited for: 3 -> 1; matrix products, arithmetic and copies ran while one was open for 1% -> 0% of each run, Pallas kernels for 0% -> 0%
where the time goes in v1:
time: 155 us; the launch traced here: 154 us
  blocking collectives  111 us (72%)
  Pallas kernels  23.3 us (15%)
  starting transfers between devices  12.8 us (8%)
  waiting for transfers between devices  3.69 us (2%)
  local copies, waits for them, and re-layouts  2.56 us (2%)
    all_to_all x4, blocking collectives, exchange(): return lax.all_to_all(x, axis, 0, 0)  111 us
    pallas_call x1, Pallas kernels, on_device(): call(forward_kernel, [VMEM] * 8, [block, shape(PEN, 17, 8, 128)], [(BX +...  8.38 us
    ppermute x2, starting transfers between devices, down(): return lax.ppermute(x, axis, [(i + 1, i) for i in range(count - 1)])  6.78 us
    ppermute x2, starting transfers between devices, up(): return lax.ppermute(x, axis, [(i, i + 1) for i in range(count - 1)])  6.02 us
    pallas_call x1, Pallas kernels, on_device(): call(blocks_kernel, [VMEM, VMEM, SMEM, VMEM], [block, block, shape(GRP, 3...  5.66 us
    pallas_call x1, Pallas kernels, on_device(): call(solve_kernel, [VMEM] * 5 + [SMEM, VMEM], [shape(PEN, 9, 8, 128)], [(...  5.14 us
    ppermute x2, waiting for transfers between devices, down(): return lax.ppermute(x, axis, [(i + 1, i) for i in range(count - 1)])  3.68 us
    pallas_call x1, Pallas kernels, on_device(): call(finish_kernel, [VMEM] * 6, [block, block], [(PEN, 2, 8, BX * BY)])  3.27 us
  transfers between devices with their start and end apart: 4, of which 1 were waited for; matrix products, arithmetic and copies ran while one was open for 0% of the time, Pallas kernels for 0%

profile of v1, /device:TPU:1, one launch (start us, length us, event | category | flops | bytes accessed | tf_op | source)
XLA Modules:
  0.0 154.3 jit_solution(7909271531959356546)
XLA Ops:
  0.6 0.0 copy-start
  0.6 0.0 copy-start.1
  0.7 1.3 copy-done.1
  2.0 0.0 copy-start.3
  2.0 1.2 copy-done.3
  3.2 0.0 copy-start.4
  3.2 0.1 shard_map.86
  3.3 4.7 %collective-permute-start.2 = (f32[32,512]{1,0:T(8,128)S(1)}, f32[32,512]{1,0:T(8,128)S(1)}, u32[]{:S(2)}, u32[]{:S(2)}) collective-permute-start(f32[32,512]{1,0:T(8,128)S(1)} %get-tuple-element.15), channel_id=1, source_target_pairs={{0,1},{1,2},{2,3},{3,4},{4,5},{5,6},{6,7},{7,8},{8,9},{9,10},{10,1... | collective-permute-start | bytes 196616 | tf_op jit(solution)/shard_map/ppermute | solution.py:333
  8.0 5.5 %collective-permute-start.3 = (f32[32,512]{1,0:T(8,128)S(1)}, f32[32,512]{1,0:T(8,128)S(1)}, u32[]{:S(2)}, u32[]{:S(2)}) collective-permute-start(f32[32,512]{1,0:T(8,128)S(1)} %get-tuple-element.16), channel_id=1, source_target_pairs={{1,0},{2,1},{3,2},{4,3},{5,4},{6,5},{7,6},{8,7},{9,8},{10,9},{11,1... | collective-permute-start | bytes 196616 | tf_op jit(solution)/shard_map/ppermute | solution.py:336
  13.5 1.3 collective-permute-start
  14.8 1.3 collective-permute-start.1
  16.1 0.0 collective-permute-done.xl_ref
  16.1 3.7 %collective-permute-done.1.xh_ref = f32[1,16,512]{2,1,0:T(8,128)S(1)} collective-permute-done((f32[1,16,512]{2,1,0:T(8,128)S(1)}, f32[1,16,512]{2,1,0:T(8,128)S(1)}, u32[]{:S(2)}, u32[]{:S(2)}) %collective-permute-start.1) | collective-permute-done | bytes 32800 | tf_op jit(solution)/shard_map/ppermute | solution.py:336
  19.8 0.0 collective-permute-done.2.yl_ref
  19.8 0.0 collective-permute-done.3.yh_ref
  19.8 0.0 copy-done
  19.8 0.0 copy-done.4
  19.8 8.4 %shard_map.87 = (f32[32,16,512]{2,1,0:T(8,128)S(1)}, f32[32,17,8,128]{3,2,1,0:T(8,128)}) custom-call(f32[32,16,512]{2,1,0:T(8,128)S(1)} %copy-done.4, f32[32,16,512]{2,1,0:T(8,128)S(1)} %copy-done.1, s32[32,16,512]{2,1,0:T(8,128)S(1)} %copy-done.3, f32[1,16,512]{2,1,0:T(8,128)S(1)} %collective-permute-done.xl_ref, ...), custom_call_target="tpu_custom_call" | custom-call | tf_op jit(solution)/shard_map/pallas_call | solution.py:341
  28.2 0.0 copy-start.5
  28.2 37.7 %all_to_all.20.recv_ref = f32[32,17,8,128]{3,2,1,0:T(8,128)S(1)} all-to-all(f32[32,17,8,128]{3,2,1,0:T(8,128)} %get-tuple-element.17), channel_id=1, replica_groups=mesh['grp'=16,'pen'=32] {'pen'}, dimensions={0} | all-to-all | bytes 4456448 | tf_op jit(solution)/shard_map/all_to_all | solution.py:317
  65.9 0.0 copy-done.5
  65.9 0.0 copy-done.6
  65.9 5.7 %shard_map.88 = (f32[32,16,512]{2,1,0:T(8,128)S(1)}, f32[32,16,512]{2,1,0:T(8,128)S(1)}, f32[16,3,8,128]{3,2,1,0:T(8,128)S(1)}) custom-call(f32[32,17,8,128]{3,2,1,0:T(8,128)S(1)} %all_to_all.20.recv_ref, f32[512,512]{1,0:T(8,128)S(1)} %copy-done, f32[512]{0:T(512)S(1)} %copy-done.5, f32[1,512]{1,0:T(1,128)S(1)} %copy-done.6), custom_call_target="tpu_custom_call" | custom-call | tf_op jit(solution)/shard_map/pallas_call | solution.py:346
  71.6 27.4 %all_to_all.21.recv_ref = f32[16,3,8,128]{3,2,1,0:T(8,128)S(1)} all-to-all(f32[16,3,8,128]{3,2,1,0:T(8,128)S(1)} %get-tuple-element.20), channel_id=1, replica_groups=mesh['grp'=16,'pen'=32] {'grp'}, dimensions={0} | all-to-all | bytes 393216 | tf_op jit(solution)/shard_map/all_to_all | solution.py:317
  99.0 0.0 copy-done.7
  99.0 0.8 shard_map.89
  99.8 20.3 %all_to_all.22.recv_ref = f32[16,2,8,128]{3,2,1,0:T(8,128)S(1)} all-to-all(f32[16,2,8,128]{3,2,1,0:T(8,128)S(1)} %get-tuple-element.21), channel_id=1, replica_groups=mesh['grp'=16,'pen'=32] {'grp'}, dimensions={0} | all-to-all | bytes 262144 | tf_op jit(solution)/shard_map/all_to_all | solution.py:317
  120.1 5.1 %shard_map.90 = f32[32,9,8,128]{3,2,1,0:T(8,128)S(1)} custom-call(f32[32,16,512]{2,1,0:T(8,128)S(1)} %get-tuple-element.18.fr_ref, f32[32,16,512]{2,1,0:T(8,128)S(1)} %get-tuple-element.19.fq_ref, f32[16,2,8,128]{3,2,1,0:T(8,128)S(1)} %all_to_all.22.recv_ref, f32[3,8,128]{2,1,0:T(8,128)S(1)} %get-tuple-element.22.control_ref, f32[512,512]{1,0:T(8,128)S(1)} %copy-done, ...), custom_call_target="tpu_custom_call" | custom-call | tf_op jit(solution)/shard_map/pallas_call | solution.py:356
  125.2 0.0 copy-start.2
  125.2 25.8 %all_to_all.23.recv_ref = f32[32,9,8,128]{3,2,1,0:T(8,128)S(1)} all-to-all(f32[32,9,8,128]{3,2,1,0:T(8,128)S(1)} %shard_map.90), channel_id=1, replica_groups=mesh['grp'=16,'pen'=32] {'pen'}, dimensions={0} | all-to-all | bytes 2359296 | tf_op jit(solution)/shard_map/all_to_all | solution.py:317
  151.0 0.0 copy-done.2
  151.0 3.3 %shard_map.91 = (f32[32,16,512]{2,1,0:T(8,128)}, f32[32,16,512]{2,1,0:T(8,128)}) custom-call(f32[32,9,8,128]{3,2,1,0:T(8,128)S(1)} %all_to_all.23.recv_ref, f32[32,16,512]{2,1,0:T(8,128)S(1)} %copy-done.4, f32[32,16,512]{2,1,0:T(8,128)S(1)} %copy-done.2, f32[32,16,512]{2,1,0:T(8,128)S(1)} %get-tuple-element.23.q_ref, ...), custom_call_target="tpu_custom_call" | custom-call | tf_op jit(solution)/shard_map/pallas_call | solution.py:365
  (2 shorter events, 0.0 us)
Async XLA Ops:
  0.6 19.2 %copy-start = (f32[512,512]{1,0:T(8,128)S(1)}, f32[512,512]{1,0:T(8,128)}, u32[]{:S(2)}) copy-start(f32[512,512]{1,0:T(8,128)} %constant.8.clone.c_ref) | copy-start | bytes 3145732
  0.6 1.3 copy-start.1
  2.0 1.2 copy-start.3
  3.2 16.6 %copy-start.4 = (f32[32,16,512]{2,1,0:T(8,128)S(1)}, f32[32,16,512]{2,1,0:T(8,128)}, u32[]{:S(2)}) copy-start(f32[32,16,512]{2,1,0:T(8,128)} %r_ref.3) | copy-start | bytes 3145732
  3.3 16.5 %collective-permute-start.2 = (f32[32,512]{1,0:T(8,128)S(1)}, f32[32,512]{1,0:T(8,128)S(1)}, u32[]{:S(2)}, u32[]{:S(2)}) collective-permute-start(f32[32,512]{1,0:T(8,128)S(1)} %get-tuple-element.15), channel_id=1, source_target_pairs={{0,1},{1,2},{2,3},{3,4},{4,5},{5,6},{6,7},{7,8},{8,9},{9,10},{10,1... | collective-permute-start | bytes 196616 | tf_op jit(solution)/shard_map/ppermute | solution.py:333
  8.0 11.8 %collective-permute-start.3 = (f32[32,512]{1,0:T(8,128)S(1)}, f32[32,512]{1,0:T(8,128)S(1)}, u32[]{:S(2)}, u32[]{:S(2)}) collective-permute-start(f32[32,512]{1,0:T(8,128)S(1)} %get-tuple-element.16), channel_id=1, source_target_pairs={{1,0},{2,1},{3,2},{4,3},{5,4},{6,5},{7,6},{8,7},{9,8},{10,9},{11,1... | collective-permute-start | bytes 196616 | tf_op jit(solution)/shard_map/ppermute | solution.py:336
  13.5 2.6 %collective-permute-start = (f32[1,16,512]{2,1,0:T(8,128)S(1)}, f32[1,16,512]{2,1,0:T(8,128)S(1)}, u32[]{:S(2)}, u32[]{:S(2)}) collective-permute-start(f32[1,16,512]{2,1,0:T(8,128)S(1)} %get-tuple-element.13), channel_id=1, source_target_pairs={{0,32},{32,64},{64,96},{96,128},{128,160},{160,192},{192,224},{224... | collective-permute-start | bytes 98312 | tf_op jit(solution)/shard_map/ppermute | solution.py:333
  14.8 5.0 %collective-permute-start.1 = (f32[1,16,512]{2,1,0:T(8,128)S(1)}, f32[1,16,512]{2,1,0:T(8,128)S(1)}, u32[]{:S(2)}, u32[]{:S(2)}) collective-permute-start(f32[1,16,512]{2,1,0:T(8,128)S(1)} %get-tuple-element.14), channel_id=1, source_target_pairs={{32,0},{64,32},{96,64},{128,96},{160,128},{192,160},{224,192},{256... | collective-permute-start | bytes 98312 | tf_op jit(solution)/shard_map/ppermute | solution.py:336
  28.2 37.7 %copy-start.5 = (f32[512]{0:T(512)S(1)}, f32[512]{0:T(512)}, u32[]{:S(2)}) copy-start(f32[512]{0:T(512)} %constant.9.clone.ez_ref) | copy-start | bytes 6148
  28.2 37.7 %copy-start.6 = (f32[1,512]{1,0:T(1,128)S(1)}, f32[1,512]{1,0:T(1,128)}, u32[]{:S(2)}) copy-start(f32[1,512]{1,0:T(1,128)} %constant.10.clone.ey_ref) | copy-start | bytes 6148
  65.9 33.1 %copy-start.7 = (f32[8,128]{1,0:T(8,128)S(1)}, f32[8,128]{1,0:T(8,128)}, u32[]{:S(2)}) copy-start(f32[8,128]{1,0:T(8,128)} %constant.11.clone.ey_ref) | copy-start | bytes 12292
  125.2 25.8 %copy-start.2 = (f32[32,16,512]{2,1,0:T(8,128)S(1)}, f32[32,16,512]{2,1,0:T(8,128)}, u32[]{:S(2)}) copy-start(f32[32,16,512]{2,1,0:T(8,128)} %d_ref.5) | copy-start | bytes 3145732

commit v2 on v1

--- a/solution.py
+++ b/solution.py
@@ -14,6 +14,7 @@
 PEN = 32
 BX = N // GRP
 BY = N // PEN
+PARTS = 8
 BK = N // PEN
 ABSORPTION = 0.02
 CONDUCT = 5.0
@@ -72,14 +73,39 @@
     return jnp.where(material == 1, jnp.float32(SOLID), jnp.float32(1.0))
 
 
-def faces_kernel(d_ref, m_ref, xlo_ref, xhi_ref, ylo_ref, yhi_ref):
+def faces_kernel(d_hbm, m_hbm, xlo_ref, xhi_ref, ylo_ref, yhi_ref, d_ref, m_ref, sems):
+    copies = []
+    for i in range(PARTS):
+        part = pl.ds(i * (BX // PARTS), BX // PARTS)
+        for j, (source, target) in enumerate(((d_hbm, d_ref), (m_hbm, m_ref))):
+            copies.append(pltpu.make_async_copy(source.at[part], target.at[part], sems.at[i, j]))
+            copies[-1].start()
+    for copy in copies:
+        copy.wait()
     xlo_ref[0] = stiffness_of(m_ref[0]) * d_ref[0]
     xhi_ref[0] = stiffness_of(m_ref[BX - 1]) * d_ref[BX - 1]
     ylo_ref[...] = stiffness_of(m_ref[:, 0, :]) * d_ref[:, 0, :]
     yhi_ref[...] = stiffness_of(m_ref[:, BY - 1, :]) * d_ref[:, BY - 1, :]
 
 
-def forward_kernel(r_ref, d_ref, m_ref, xl_ref, xh_ref, yl_ref, yh_ref, c_ref, q_ref, send_ref, u_ref):
+def third_modes(field_ref, c_ref):
+    return matmul(c_ref[...], field_ref[...].reshape(BX * BY, N), ((1,), (1,)))
+
+
+def put_modes(modes, first, send_ref):
+    for b in range(4):
+        part = modes[:, 128 * b : 128 * b + 128].reshape(PEN, 2, 8, 128)
+        for a in range(2):
+            send_ref[:, first + 4 * a + b] = part[:, a]
+
+
+def residual_kernel(r_ref, c_ref, modes_ref):
+    modes_ref[...] = third_modes(r_ref, c_ref)
+
+
+def operated_kernel(
+    r_ref, d_ref, m_ref, modes_ref, xl_ref, xh_ref, yl_ref, yh_ref, c_ref, q_ref, send_ref, u_ref
+):
     u_ref[0] = xl_ref[0]
     u_ref[BX + 1] = xh_ref[0]
 
@@ -107,12 +133,8 @@
     curvature, projection = lax.fori_loop(0, BX, stencil, (zero, zero))
     half = lax.broadcasted_iota(jnp.int32, (8, 128), 0) < 4
     sums = jnp.where(half, fold(curvature, 4), fold(projection, 4))
-    for field, ref in enumerate((r_ref, q_ref)):
-        modes = matmul(c_ref[...], ref[...].reshape(BX * BY, N), ((1,), (1,)))
-        for b in range(4):
-            part = modes[:, 128 * b : 128 * b + 128].reshape(PEN, 2, 8, 128)
-            for a in range(2):
-                send_ref[:, 8 * field + 4 * a + b] = part[:, a]
+    put_modes(modes_ref[...], 0, send_ref)
+    put_modes(third_modes(q_ref, c_ref), 8, send_ref)
     for j in range(PEN):
         send_ref[j, 16] = sums
 
@@ -127,7 +149,6 @@
                     for i in range(8):
                         y_ref[8 * b + i, 8 * a : 8 * a + 8, 128 * s : 128 * s + 128] = rows[i]
         out_ref[...] = matmul(y_ref[...].reshape(BX * BK, N), c_ref[...], ((1,), (1,))).reshape(BX, BK, N)
-
     dots = [jnp.zeros((8, 128), F32), jnp.zeros((8, 128), F32)]
     k0 = lax.axis_index("pen") * BK
     for h in range(2):
@@ -156,7 +177,7 @@
             for side, x in enumerate(parts):
                 for b in range(4):
                     for i in range(8):
-                        send_ref[8 * h + i, t, 4 * side + b : 4 * side + b + 1, :] = x[
+                        send_ref[8 * h + i, 8 * t + 4 * side + b] = x[
                             i : i + 1, 128 * b : 128 * b + 128
                         ]
         for i, x in enumerate((rq, qq)):
@@ -167,33 +188,36 @@
     for j in range(1, PEN):
         sums = sums + recv_ref[j, 16]
     row = lax.broadcasted_iota(jnp.int32, (8, 128), 0)
-    sums = fold(sums, 6)
-    rq = fold(fold(dots[0], 4), 2)
-    qq = fold(fold(dots[1], 4), 2)
-    sums = jnp.where(
-        row < 2, sums, jnp.where(row < 4, pltpu.roll(sums, 6, 0), jnp.where(row < 6, rq, qq))
-    )
+    four = (jnp.where(row < 4, sums, 0.0), jnp.where(row < 4, 0.0, sums), dots[0], dots[1])
+    group = lax.broadcasted_iota(jnp.int32, (1, 128), 1) // 32
+    packed = jnp.zeros((1, 128), F32)
+    for i, x in enumerate(four):
+        x = jnp.sum(x, axis=0, keepdims=True)
+        x = x + pltpu.roll(x, 64, 1)
+        packed = jnp.where(group == i, x + pltpu.roll(x, 32, 1), packed)
     for j in range(GRP):
-        send_ref[j, 2] = sums
+        send_ref[j, 16] = packed
 
 
 def interface_kernel(recv_ref, ez_ref, ey_ref, send_ref, control_ref):
     row = lax.broadcasted_iota(jnp.int32, (8, 128), 0)
-    sums = recv_ref[0, 2]
+    group = lax.broadcasted_iota(jnp.int32, (1, 128), 1) // 32
+    sums = recv_ref[0, 16]
     for p in range(1, GRP):
-        sums = sums + recv_ref[p, 2]
-
-    def total(low):
-        return jnp.full((8, 128), jnp.sum(jnp.where((row >= low) & (row < low + 2), sums, 0.0)), F32)
-
-    curvature, projection, rq, qq = total(0), total(2), total(4), total(6)
+        sums = sums + recv_ref[p, 16]
+
+    def total(i):
+        return jnp.full((8, 128), jnp.sum(jnp.where(group == i, sums, 0.0)), F32)
+
+    curvature, projection, rq, qq = total(0), total(1), total(2), total(3)
     step = projection / curvature
     ez = ez_ref[lax.axis_index("pen") * BK + lax.axis_index("grp")]
     rho, factor = decay(ABSORPTION / CONDUCT + ez + ey_ref[...])
     across = rho
     for _ in range(5):
         across = across * across
-    tiles = [recv_ref[p, 0] - step * recv_ref[p, 1] for p in range(GRP)]
+    others = [recv_ref[p, 8:16].reshape(8, 128) for p in range(GRP)]
+    tiles = [recv_ref[p, 0:8].reshape(8, 128) - step * others[p] for p in range(GRP)]
     zero = jnp.zeros((8, 128), F32)
     rising = [zero]
     for p in range(GRP):
@@ -215,11 +239,11 @@
             rising[p] + powers[p] * images,
             falling[GRP - 1 - p] + powers[GRP - 1 - p] * images,
         )
-        send_ref[p, 0] = state
-        dots = dots + state * pltpu.roll(recv_ref[p, 1], 4, 0)
-    dots = rho * factor * dots
+        send_ref[p, 0:8] = state.reshape(8, 1, 128)
+        dots = dots + state * pltpu.roll(others[p], 4, 0)
+    dots = jnp.sum(rho * factor * dots, axis=0, keepdims=True)
     for p in range(GRP):
-        send_ref[p, 1] = dots
+        send_ref[p, 8] = dots
     control_ref[0] = step
     control_ref[1] = curvature
     control_ref[2] = rq - step * qq
@@ -239,7 +263,7 @@
             return jnp.concatenate(
                 [
                     jnp.concatenate(
-                        [recv_ref[8 * h + i, 0, 4 * side + b : 4 * side + b + 1, :] for i in range(8)],
+                        [recv_ref[8 * h + i, 4 * side + b] for i in range(8)],
                         axis=0,
                     )
                     for b in range(4)
@@ -272,13 +296,12 @@
                 )
                 for i in range(8):
                     send_ref[8 * s + i, 4 * a + b] = rows[i]
-    sums = recv_ref[0, 1]
+    sums = recv_ref[0, 8]
     for p in range(1, GRP):
-        sums = sums + recv_ref[p, 1]
-    first = (lax.broadcasted_iota(jnp.int32, (8, 128), 0) == 0) & (
-        lax.broadcasted_iota(jnp.int32, (8, 128), 1) == 0
-    )
-    sums = sums + jnp.where(first, control_ref[2], 0.0)
+        sums = sums + recv_ref[p, 8]
+    row = lax.broadcasted_iota(jnp.int32, (8, 128), 0)
+    first = (row == 0) & (lax.broadcasted_iota(jnp.int32, (8, 128), 1) == 0)
+    sums = jnp.where(row == 0, sums, 0.0) + jnp.where(first, control_ref[2], 0.0)
     for j in range(PEN):
         send_ref[j, 8] = sums
 
@@ -308,7 +331,7 @@
         in_specs=ins,
         out_specs=[VMEM] * len(outs),
         out_shape=outs,
-        scratch_shapes=[pltpu.VMEM(s, F32) for s in scratch],
+        scratch_shapes=[pltpu.VMEM(s, F32) if isinstance(s, tuple) else s for s in scratch],
         compiler_params=PARAMS,
     )
 
@@ -326,7 +349,14 @@
     block = shape(BX, BY, N)
 
     xlo, xhi, ylo, yhi = call(
-        faces_kernel, [VMEM] * 2, [shape(1, BY, N), shape(1, BY, N), shape(BX, N), shape(BX, N)]
+        faces_kernel,
+        [pl.BlockSpec(memory_space=pl.ANY)] * 2,
+        [shape(1, BY, N), shape(1, BY, N), shape(BX, N), shape(BX, N)],
+        [
+            pltpu.VMEM((BX, BY, N), F32),
+            pltpu.VMEM((BX, BY, N), jnp.int32),
+            pltpu.SemaphoreType.DMA((PARTS, 2)),
+        ],
     )(direction, material)
 
     def up(x, axis, count):
@@ -338,18 +368,19 @@
     xl, xh = up(xhi, "grp", GRP), down(xlo, "grp", GRP)
     yl, yh = up(yhi, "pen", PEN), down(ylo, "pen", PEN)
 
+    (modes_r,) = call(residual_kernel, [VMEM] * 2, [shape(N, BX * BY)])(residual, matrix)
     operated, send = call(
-        forward_kernel, [VMEM] * 8, [block, shape(PEN, 17, 8, 128)], [(BX + 2, BY, N)]
-    )(residual, direction, material, xl, xh, yl, yh, matrix)
+        operated_kernel, [VMEM] * 9, [block, shape(PEN, 17, 8, 128)], [(BX + 2, BY, N)]
+    )(residual, direction, material, modes_r, xl, xh, yl, yh, matrix)
 
     recv = exchange(send, "pen")
     field_r, field_q, send = call(
-        blocks_kernel, [VMEM, VMEM, SMEM, VMEM], [block, block, shape(GRP, 3, 8, 128)], [(BX, BK, N)]
+        blocks_kernel, [VMEM, VMEM, SMEM, VMEM], [block, block, shape(GRP, 17, 1, 128)], [(BX, BK, N)]
     )(recv, matrix, ez, ey_row)
 
     recv = exchange(send, "grp")
     send, control = call(
-        interface_kernel, [VMEM, SMEM, VMEM], [shape(GRP, 2, 8, 128), shape(3, 8, 128)]
+        interface_kernel, [VMEM, SMEM, VMEM], [shape(GRP, 9, 1, 128), shape(3, 8, 128)]
     )(recv, ez, ey_tile)
 
     recv = exchange(send, "grp")

time: 155 us -> 153 us (0.987)
  Pallas kernels: 23.3 us -> 27.7 us
  blocking collectives: 111 us -> 107 us
  waiting for transfers between devices: 3.69 us -> 1.82 us
    pallas_call x4 -> x5, Pallas kernels: 14.9 us -> 19.3 us  [the longest x1 7.85 us: on_device(): call(operated_kernel, [VMEM] * 9, [block, shape(PEN, 17, 8, 128)], [(BX +...]
    all_to_all x4, blocking collectives: 111 us -> 107 us  [exchange(): return lax.all_to_all(x, axis, 0, 0)]
    ppermute x2, waiting for transfers between devices: 3.68 us -> 1.81 us  [down(): return lax.ppermute(x, axis, [(i + 1, i) for i in range(count - 1)])]
  transfers between devices with their start and end apart: 4 -> 4, of which waited for: 1 -> 1; matrix products, arithmetic and copies ran while one was open for 0% -> 0% of each run, Pallas kernels for 0% -> 1%
where the time goes in v2:
time: 153 us
  blocking collectives  107 us (70%)
  Pallas kernels  27.7 us (18%)
  starting transfers between devices  12.7 us (8%)
  local copies, waits for them, and re-layouts  2.57 us (2%)
  waiting for transfers between devices  1.82 us (1%)
    all_to_all x4, blocking collectives, exchange(): return lax.all_to_all(x, axis, 0, 0)  107 us
    pallas_call x1, Pallas kernels, on_device(): call(operated_kernel, [VMEM] * 9, [block, shape(PEN, 17, 8, 128)], [(BX +...  7.85 us
    ppermute x2, starting transfers between devices, down(): return lax.ppermute(x, axis, [(i + 1, i) for i in range(count - 1)])  6.78 us
    ppermute x2, starting transfers between devices, up(): return lax.ppermute(x, axis, [(i, i + 1) for i in range(count - 1)])  5.89 us
    pallas_call x1, Pallas kernels, on_device(): call(blocks_kernel, [VMEM, VMEM, SMEM, VMEM], [block, block, shape(GRP, 1...  5.75 us
    pallas_call x1, Pallas kernels, on_device(): call(solve_kernel, [VMEM] * 5 + [SMEM, VMEM], [shape(PEN, 9, 8, 128)], [(...  5.13 us
    pallas_call x1, Pallas kernels, on_device(): call(finish_kernel, [VMEM] * 6, [block, block], [(PEN, 2, 8, BX * BY)])  3.26 us
  transfers between devices with their start and end apart: 4, of which 1 were waited for; matrix products, arithmetic and copies ran while one was open for 0% of the time, Pallas kernels for 1%

profile of v2, /device:TPU:1, one launch (start us, length us, event | category | flops | bytes accessed | tf_op | source)
XLA Modules:
  0.0 152.6 jit_solution(16714709755345700506)
XLA Ops:
  0.6 0.0 copy-start
  0.6 0.0 copy-start.3
  0.7 1.3 copy-done.3
  2.0 1.2 copy-done.5
  3.2 2.9 %shard_map.87 = (f32[1,16,512]{2,1,0:T(8,128)S(1)}, f32[1,16,512]{2,1,0:T(8,128)S(1)}, f32[32,512]{1,0:T(8,128)S(1)}, f32[32,512]{1,0:T(8,128)S(1)}) custom-call(f32[32,16,512]{2,1,0:T(8,128)S(1)} %copy-done.3, s32[32,16,512]{2,1,0:T(8,128)S(1)} %copy-done.5), custom_call_target="tpu_custom_call" | custom-call | tf_op jit(solution)/shard_map/pallas_call | solution.py:351
  6.1 4.6 %collective-permute-start.2 = (f32[32,512]{1,0:T(8,128)S(1)}, f32[32,512]{1,0:T(8,128)S(1)}, u32[]{:S(2)}, u32[]{:S(2)}) collective-permute-start(f32[32,512]{1,0:T(8,128)S(1)} %get-tuple-element.15), channel_id=1, source_target_pairs={{0,1},{1,2},{2,3},{3,4},{4,5},{5,6},{6,7},{7,8},{8,9},{9,10},{10,1... | collective-permute-start | bytes 196616 | tf_op jit(solution)/shard_map/ppermute | solution.py:363
  10.7 5.5 %collective-permute-start.3 = (f32[32,512]{1,0:T(8,128)S(1)}, f32[32,512]{1,0:T(8,128)S(1)}, u32[]{:S(2)}, u32[]{:S(2)}) collective-permute-start(f32[32,512]{1,0:T(8,128)S(1)} %get-tuple-element.16), channel_id=1, source_target_pairs={{1,0},{2,1},{3,2},{4,3},{5,4},{6,5},{7,6},{8,7},{9,8},{10,9},{11,1... | collective-permute-start | bytes 196616 | tf_op jit(solution)/shard_map/ppermute | solution.py:366
  16.2 1.3 collective-permute-start
  17.5 1.3 collective-permute-start.1
  18.8 0.0 copy-done
  18.8 0.0 copy-done.2
  18.8 1.8 %shard_map.86.modes_ref = f32[512,512]{1,0:T(8,128)S(1)} custom-call(f32[32,16,512]{2,1,0:T(8,128)S(1)} %copy-done.2, f32[512,512]{1,0:T(8,128)S(1)} %copy-done), custom_call_target="tpu_custom_call" | custom-call | tf_op jit(solution)/shard_map/pallas_call | solution.py:371
  20.7 0.0 collective-permute-done.xl_ref
  20.7 1.8 %collective-permute-done.1.xh_ref = f32[1,16,512]{2,1,0:T(8,128)S(1)} collective-permute-done((f32[1,16,512]{2,1,0:T(8,128)S(1)}, f32[1,16,512]{2,1,0:T(8,128)S(1)}, u32[]{:S(2)}, u32[]{:S(2)}) %collective-permute-start.1) | collective-permute-done | bytes 32800 | tf_op jit(solution)/shard_map/ppermute | solution.py:366
  22.5 0.0 collective-permute-done.2.yl_ref
  22.5 0.0 collective-permute-done.3.yh_ref
  22.5 0.0 copy-done.6
  22.5 7.9 %shard_map.88 = (f32[32,16,512]{2,1,0:T(8,128)S(1)}, f32[32,17,8,128]{3,2,1,0:T(8,128)}) custom-call(f32[32,16,512]{2,1,0:T(8,128)S(1)} %copy-done.2, f32[32,16,512]{2,1,0:T(8,128)S(1)} %copy-done.3, s32[32,16,512]{2,1,0:T(8,128)S(1)} %copy-done.6, f32[512,512]{1,0:T(8,128)S(1)} %shard_map.86.modes_ref, f32[1,16,512]{2,1,0:T(8,128)S(1)} %collective-permute-done.xl_ref, ...), custom_call_target="tpu_custom_call" | custom-call | tf_op jit(solution)/shard_map/pallas_call | solution.py:372
  30.4 37.7 %all_to_all.20.recv_ref = f32[32,17,8,128]{3,2,1,0:T(8,128)S(1)} all-to-all(f32[32,17,8,128]{3,2,1,0:T(8,128)} %get-tuple-element.17), channel_id=1, replica_groups=mesh['grp'=16,'pen'=32] {'pen'}, dimensions={0} | all-to-all | bytes 4456448 | tf_op jit(solution)/shard_map/all_to_all | solution.py:340
  68.1 0.0 copy-done.1
  68.1 0.0 copy-done.7
  68.1 0.0 copy-done.8
  68.1 0.0 copy-start.9
  68.1 5.7 %shard_map.89 = (f32[32,16,512]{2,1,0:T(8,128)S(1)}, f32[32,16,512]{2,1,0:T(8,128)S(1)}, f32[16,17,1,128]{3,2,1,0:T(1,128)S(1)}) custom-call(f32[32,17,8,128]{3,2,1,0:T(8,128)S(1)} %all_to_all.20.recv_ref, f32[512,512]{1,0:T(8,128)S(1)} %copy-done.1, f32[512]{0:T(512)S(1)} %copy-done.7, f32[1,512]{1,0:T(1,128)S(1)} %copy-done.8), custom_call_target="tpu_custom_call" | custom-call | tf_op jit(solution)/shard_map/pallas_call | solution.py:377
  73.9 26.8 %all_to_all.21.recv_ref = f32[16,17,1,128]{3,2,1,0:T(1,128)S(1)} all-to-all(f32[16,17,1,128]{3,2,1,0:T(1,128)S(1)} %get-tuple-element.20), channel_id=1, replica_groups=mesh['grp'=16,'pen'=32] {'grp'}, dimensions={0} | all-to-all | bytes 278528 | tf_op jit(solution)/shard_map/all_to_all | solution.py:340
  100.6 0.0 copy-done.9
  100.6 0.9 shard_map.90
  101.6 18.3 %all_to_all.22.recv_ref = f32[16,9,1,128]{3,2,1,0:T(1,128)S(1)} all-to-all(f32[16,9,1,128]{3,2,1,0:T(1,128)S(1)} %get-tuple-element.21), channel_id=1, replica_groups=mesh['grp'=16,'pen'=32] {'grp'}, dimensions={0} | all-to-all | bytes 147456 | tf_op jit(solution)/shard_map/all_to_all | solution.py:340
  119.8 5.1 %shard_map.91 = f32[32,9,8,128]{3,2,1,0:T(8,128)S(1)} custom-call(f32[32,16,512]{2,1,0:T(8,128)S(1)} %get-tuple-element.18.fr_ref, f32[32,16,512]{2,1,0:T(8,128)S(1)} %get-tuple-element.19.fq_ref, f32[16,9,1,128]{3,2,1,0:T(1,128)S(1)} %all_to_all.22.recv_ref, f32[3,8,128]{2,1,0:T(8,128)S(1)} %get-tuple-element.22.control_ref, f32[512,512]{1,0:T(8,128)S(1)} %copy-done.1, ...), custom_call_target="tpu_custom_call" | custom-call | tf_op jit(solution)/shard_map/pallas_call | solution.py:387
  125.0 0.0 copy-start.4
  125.0 24.3 %all_to_all.23.recv_ref = f32[32,9,8,128]{3,2,1,0:T(8,128)S(1)} all-to-all(f32[32,9,8,128]{3,2,1,0:T(8,128)S(1)} %shard_map.91), channel_id=1, replica_groups=mesh['grp'=16,'pen'=32] {'pen'}, dimensions={0} | all-to-all | bytes 2359296 | tf_op jit(solution)/shard_map/all_to_all | solution.py:340
  149.3 3.3 %shard_map.92 = (f32[32,16,512]{2,1,0:T(8,128)}, f32[32,16,512]{2,1,0:T(8,128)}) custom-call(f32[32,9,8,128]{3,2,1,0:T(8,128)S(1)} %all_to_all.23.recv_ref, f32[32,16,512]{2,1,0:T(8,128)S(1)} %copy-done.2, f32[32,16,512]{2,1,0:T(8,128)S(1)} %copy-done.4, f32[32,16,512]{2,1,0:T(8,128)S(1)} %get-tuple-element.23.q_ref, ...), custom_call_target="tpu_custom_call" | custom-call | tf_op jit(solution)/shard_map/pallas_call | solution.py:396
  (7 shorter events, 0.0 us)
Async XLA Ops:
  0.6 18.2 %copy-start = (f32[512,512]{1,0:T(8,128)S(1)}, f32[512,512]{1,0:T(8,128)}, u32[]{:S(2)}) copy-start(f32[512,512]{1,0:T(8,128)} %constant.8.clone.c_ref) | copy-start | bytes 3145732
  0.6 1.3 copy-start.3
  2.0 1.2 copy-start.5
  3.2 15.7 %copy-start.2 = (f32[32,16,512]{2,1,0:T(8,128)S(1)}, f32[32,16,512]{2,1,0:T(8,128)}, u32[]{:S(2)}) copy-start(f32[32,16,512]{2,1,0:T(8,128)} %r_ref.5) | copy-start | bytes 3145732
  3.2 19.3 %copy-start.6 = (s32[32,16,512]{2,1,0:T(8,128)S(1)}, s32[32,16,512]{2,1,0:T(8,128)}, u32[]{:S(2)}) copy-start(s32[32,16,512]{2,1,0:T(8,128)} %m_ref.1) | copy-start | bytes 3145732
  6.1 16.4 %collective-permute-start.2 = (f32[32,512]{1,0:T(8,128)S(1)}, f32[32,512]{1,0:T(8,128)S(1)}, u32[]{:S(2)}, u32[]{:S(2)}) collective-permute-start(f32[32,512]{1,0:T(8,128)S(1)} %get-tuple-element.15), channel_id=1, source_target_pairs={{0,1},{1,2},{2,3},{3,4},{4,5},{5,6},{6,7},{7,8},{8,9},{9,10},{10,1... | collective-permute-start | bytes 196616 | tf_op jit(solution)/shard_map/ppermute | solution.py:363
  10.7 11.8 %collective-permute-start.3 = (f32[32,512]{1,0:T(8,128)S(1)}, f32[32,512]{1,0:T(8,128)S(1)}, u32[]{:S(2)}, u32[]{:S(2)}) collective-permute-start(f32[32,512]{1,0:T(8,128)S(1)} %get-tuple-element.16), channel_id=1, source_target_pairs={{1,0},{2,1},{3,2},{4,3},{5,4},{6,5},{7,6},{8,7},{9,8},{10,9},{11,1... | collective-permute-start | bytes 196616 | tf_op jit(solution)/shard_map/ppermute | solution.py:366
  16.2 4.5 %collective-permute-start = (f32[1,16,512]{2,1,0:T(8,128)S(1)}, f32[1,16,512]{2,1,0:T(8,128)S(1)}, u32[]{:S(2)}, u32[]{:S(2)}) collective-permute-start(f32[1,16,512]{2,1,0:T(8,128)S(1)} %get-tuple-element.13), channel_id=1, source_target_pairs={{0,32},{32,64},{64,96},{96,128},{128,160},{160,192},{192,224},{224... | collective-permute-start | bytes 98312 | tf_op jit(solution)/shard_map/ppermute | solution.py:363
  17.5 5.0 %collective-permute-start.1 = (f32[1,16,512]{2,1,0:T(8,128)S(1)}, f32[1,16,512]{2,1,0:T(8,128)S(1)}, u32[]{:S(2)}, u32[]{:S(2)}) collective-permute-start(f32[1,16,512]{2,1,0:T(8,128)S(1)} %get-tuple-element.14), channel_id=1, source_target_pairs={{32,0},{64,32},{96,64},{128,96},{160,128},{192,160},{224,192},{256... | collective-permute-start | bytes 98312 | tf_op jit(solution)/shard_map/ppermute | solution.py:366
  30.4 37.7 %copy-start.1 = (f32[512,512]{1,0:T(8,128)S(1)}, f32[512,512]{1,0:T(8,128)}, u32[]{:S(2)}) copy-start(f32[512,512]{1,0:T(8,128)} %constant.8.clone.c_ref) | copy-start | bytes 3145732
  30.4 37.7 %copy-start.7 = (f32[512]{0:T(512)S(1)}, f32[512]{0:T(512)}, u32[]{:S(2)}) copy-start(f32[512]{0:T(512)} %constant.9.clone.ez_ref) | copy-start | bytes 6148
  30.4 37.7 %copy-start.8 = (f32[1,512]{1,0:T(1,128)S(1)}, f32[1,512]{1,0:T(1,128)}, u32[]{:S(2)}) copy-start(f32[1,512]{1,0:T(1,128)} %constant.10.clone.ey_ref) | copy-start | bytes 6148
  68.1 32.5 %copy-start.9 = (f32[8,128]{1,0:T(8,128)S(1)}, f32[8,128]{1,0:T(8,128)}, u32[]{:S(2)}) copy-start(f32[8,128]{1,0:T(8,128)} %constant.11.clone.ey_ref) | copy-start | bytes 12292
  125.0 24.4 %copy-start.4 = (f32[32,16,512]{2,1,0:T(8,128)S(1)}, f32[32,16,512]{2,1,0:T(8,128)}, u32[]{:S(2)}) copy-start(f32[32,16,512]{2,1,0:T(8,128)} %d_ref.3) | copy-start | bytes 3145732

commit v3 on v2

--- a/solution.py
+++ b/solution.py
@@ -21,6 +21,7 @@
 SOLID = math.sqrt(30.0)
 F32 = jnp.float32
 VMEM = pl.BlockSpec(memory_space=pltpu.VMEM)
+HBM = pl.BlockSpec(memory_space=pltpu.HBM)
 SMEM = pl.BlockSpec(memory_space=pltpu.SMEM)
 PARAMS = pltpu.CompilerParams(vmem_limit_bytes=48 * 1024 * 1024)
 
@@ -99,21 +100,19 @@
             send_ref[:, first + 4 * a + b] = part[:, a]
 
 
-def residual_kernel(r_ref, c_ref, modes_ref):
-    modes_ref[...] = third_modes(r_ref, c_ref)
-
-
-def operated_kernel(
-    r_ref, d_ref, m_ref, modes_ref, xl_ref, xh_ref, yl_ref, yh_ref, c_ref, q_ref, send_ref, u_ref
-):
-    u_ref[0] = xl_ref[0]
-    u_ref[BX + 1] = xh_ref[0]
+def residual_kernel(r_ref, c_ref, send_ref):
+    put_modes(third_modes(r_ref, c_ref), 0, send_ref)
+
+
+def inner_kernel(r_ref, d_ref, m_ref, q_ref, sums_ref, u_ref):
+    u_ref[0] = jnp.zeros((BY, N), F32)
+    u_ref[BX + 1] = jnp.zeros((BY, N), F32)
 
     def scale(x, _):
         u_ref[x + 1] = stiffness_of(m_ref[x]) * d_ref[x]
         return 0
 
-    lax.fori_loop(0, BX, scale, 0)
+    lax.fori_loop(0, BX, scale, 0, unroll=4)
     row = lax.broadcasted_iota(jnp.int32, (BY, N), 0)
     lane = lax.broadcasted_iota(jnp.int32, (BY, N), 1)
 
@@ -121,8 +120,8 @@
         u = u_ref[x + 1]
         d = d_ref[x]
         beside = u_ref[x] + u_ref[x + 2]
-        beside += jnp.where(row == 0, yl_ref[pl.ds(x, 1), :], pltpu.roll(u, 1, 0))
-        beside += jnp.where(row == BY - 1, yh_ref[pl.ds(x, 1), :], pltpu.roll(u, BY - 1, 0))
+        beside += jnp.where(row == 0, 0.0, pltpu.roll(u, 1, 0))
+        beside += jnp.where(row == BY - 1, 0.0, pltpu.roll(u, BY - 1, 0))
         beside += jnp.where(lane == 0, 0.0, pltpu.roll(u, 1, 1))
         beside += jnp.where(lane == N - 1, 0.0, pltpu.roll(u, N - 1, 1))
         q = ABSORPTION * d + stiffness_of(m_ref[x]) * (6.0 * u - beside)
@@ -130,63 +129,108 @@
         return sums[0] + to_tile(d * q), sums[1] + to_tile(r_ref[x] * d)
 
     zero = jnp.zeros((8, 128), F32)
-    curvature, projection = lax.fori_loop(0, BX, stencil, (zero, zero))
+    sums = lax.fori_loop(0, BX, stencil, (zero, zero), unroll=4)
+    sums_ref[0], sums_ref[1] = sums
+
+
+def operated_kernel(
+    q_ref, sums_ref, d_ref, m_ref, xl_ref, xh_ref, yl_ref, yh_ref, c_ref, out_ref, send_ref
+):
+    row = lax.broadcasted_iota(jnp.int32, (8, N), 0)
+
+    def low_high(x, total):
+        for first, edge, side_ref in ((0, 0, yl_ref), (8, 7, yh_ref)):
+            rows = pl.ds(first, 8)
+            add = stiffness_of(m_ref[x, rows]) * jnp.where(row == edge, side_ref[pl.ds(x, 1), :], 0.0)
+            out_ref[x, rows] = q_ref[x, rows] - add
+            total = total + d_ref[x, rows] * add
+        return total
+
+    total = lax.fori_loop(0, BX, low_high, jnp.zeros((8, N), F32), unroll=4)
+    total = jnp.concatenate([total, jnp.zeros((8, N), F32)], axis=0)
+    for x, side_ref in ((0, xl_ref), (BX - 1, xh_ref)):
+        add = stiffness_of(m_ref[x]) * side_ref[0]
+        out_ref[x] = out_ref[x] - add
+        total = total + d_ref[x] * add
+    curvature = sums_ref[0] - to_tile(total)
     half = lax.broadcasted_iota(jnp.int32, (8, 128), 0) < 4
-    sums = jnp.where(half, fold(curvature, 4), fold(projection, 4))
-    put_modes(modes_ref[...], 0, send_ref)
-    put_modes(third_modes(q_ref, c_ref), 8, send_ref)
+    sums = jnp.where(half, fold(curvature, 4), fold(sums_ref[1], 4))
+    put_modes(third_modes(out_ref, c_ref), 0, send_ref)
     for j in range(PEN):
-        send_ref[j, 16] = sums
-
-
-def blocks_kernel(recv_ref, c_ref, ez_ref, ey_ref, fr_ref, fq_ref, send_ref, y_ref):
-    for field, out_ref in enumerate((fr_ref, fq_ref)):
+        send_ref[j, 8] = sums
+
+
+def second_modes(recv_ref, c_ref, out_ref, y_ref):
+    def part(b, _):
+        for s in range(4):
+            for a in range(2):
+                rows = swap_units([recv_ref[8 * s + i, 4 * a + b] for i in range(8)])
+                for i in range(8):
+                    y_ref[8 * b + i, 8 * a : 8 * a + 8, 128 * s : 128 * s + 128] = rows[i]
+        return 0
+
+    lax.fori_loop(0, 4, part, 0)
+    out_ref[...] = matmul(y_ref[...].reshape(BX * BK, N), c_ref[...], ((1,), (1,))).reshape(BX, BK, N)
+
+
+def third_eigen(ez_ref, h):
+    k0 = lax.axis_index("pen") * BK + 8 * h
+    return jnp.concatenate([jnp.full((1, N), ez_ref[k0 + i], F32) for i in range(8)], axis=0)
+
+
+def put_states(v, w, h, send_ref, first):
+    for side, x in enumerate((v, w)):
         for b in range(4):
-            for s in range(4):
-                for a in range(2):
-                    t = 8 * field + 4 * a + b
-                    rows = swap_units([recv_ref[8 * s + i, t] for i in range(8)])
-                    for i in range(8):
-                        y_ref[8 * b + i, 8 * a : 8 * a + 8, 128 * s : 128 * s + 128] = rows[i]
-        out_ref[...] = matmul(y_ref[...].reshape(BX * BK, N), c_ref[...], ((1,), (1,))).reshape(BX, BK, N)
-    dots = [jnp.zeros((8, 128), F32), jnp.zeros((8, 128), F32)]
-    k0 = lax.axis_index("pen") * BK
+            for i in range(8):
+                send_ref[8 * h + i, first + 4 * side + b] = x[i : i + 1, 128 * b : 128 * b + 128]
+
+
+def residual_blocks_kernel(recv_ref, c_ref, ez_ref, ey_ref, fr_ref, states_ref, y_ref):
+    second_modes(recv_ref, c_ref, fr_ref, y_ref)
     for h in range(2):
         rows = pl.ds(8 * h, 8)
-        ez = jnp.concatenate(
-            [jnp.full((1, N), ez_ref[k0 + 8 * h + i], F32) for i in range(8)], axis=0
-        )
-        rho, factor = decay(ABSORPTION / CONDUCT + ez + ey_ref[...])
+        rho, _ = decay(ABSORPTION / CONDUCT + third_eigen(ez_ref, h) + ey_ref[...])
 
         def sweep(x, carry):
-            power, vr, vq, wr, wq, rq, qq = carry
+            power, v, w = carry
+            f = fr_ref[x, rows]
+            return power * rho, f + rho * v, w + power * f
+
+        zero = jnp.zeros((8, N), F32)
+        _, v, w = lax.fori_loop(0, BX, sweep, (jnp.ones((8, N), F32), zero, zero), unroll=4)
+        put_states(v, w, h, states_ref, 0)
+
+
+def operated_blocks_kernel(
+    recv_ref, fr_ref, states_ref, c_ref, ez_ref, ey_ref, fq_ref, send_ref, y_ref
+):
+    second_modes(recv_ref, c_ref, fq_ref, y_ref)
+    dots = [jnp.zeros((8, 128), F32), jnp.zeros((8, 128), F32)]
+    for h in range(2):
+        rows = pl.ds(8 * h, 8)
+        rho, factor = decay(ABSORPTION / CONDUCT + third_eigen(ez_ref, h) + ey_ref[...])
+
+        def sweep(x, carry):
+            power, vr, vq, wq, rq, qq = carry
             r = fr_ref[x, rows]
             q = fq_ref[x, rows]
-            vr = r + rho * vr
-            vq = q + rho * vq
-            wr = wr + power * r
-            wq = wq + power * q
-            rq = rq + (vr * q + vq * r - r * q)
-            qq = qq + (2.0 * vq - q) * q
-            return power * rho, vr, vq, wr, wq, rq, qq
+            before_r, before_q = rho * vr, rho * vq
+            vq = q + before_q
+            rq = rq + (before_r * q + vq * r)
+            qq = qq + (vq + before_q) * q
+            return power * rho, r + before_r, vq, wq + power * q, rq, qq
 
         zero = jnp.zeros((8, N), F32)
-        carry = lax.fori_loop(0, BX, sweep, (jnp.ones((8, N), F32),) + (zero,) * 6)
-        _, vr, vq, wr, wq, rq, qq = carry
-        for t, parts in enumerate(((vr, wr), (vq, wq))):
-            for side, x in enumerate(parts):
-                for b in range(4):
-                    for i in range(8):
-                        send_ref[8 * h + i, 8 * t + 4 * side + b] = x[
-                            i : i + 1, 128 * b : 128 * b + 128
-                        ]
+        carry = (jnp.ones((8, N), F32),) + (zero,) * 5
+        _, _, vq, wq, rq, qq = lax.fori_loop(0, BX, sweep, carry, unroll=4)
+        put_states(vq, wq, h, send_ref, 8)
         for i, x in enumerate((rq, qq)):
             x = factor * x
             dots[i] += x[:, 0:128] + x[:, 128:256] + x[:, 256:384] + x[:, 384:512]
 
-    sums = recv_ref[0, 16]
+    sums = recv_ref[0, 8]
     for j in range(1, PEN):
-        sums = sums + recv_ref[j, 16]
+        sums = sums + recv_ref[j, 8]
     row = lax.broadcasted_iota(jnp.int32, (8, 128), 0)
     four = (jnp.where(row < 4, sums, 0.0), jnp.where(row < 4, 0.0, sums), dots[0], dots[1])
     group = lax.broadcasted_iota(jnp.int32, (1, 128), 1) // 32
@@ -196,6 +240,7 @@
         x = x + pltpu.roll(x, 64, 1)
         packed = jnp.where(group == i, x + pltpu.roll(x, 32, 1), packed)
     for j in range(GRP):
+        send_ref[j, 0:8] = states_ref[j]
         send_ref[j, 16] = packed
 
 
@@ -251,44 +296,36 @@
 
 def solve_kernel(fr_ref, fq_ref, recv_ref, control_ref, c_ref, ez_ref, ey_ref, send_ref, f_ref, u_ref, y_ref):
     step = control_ref[0, 0:1, 0:1]
-    k0 = lax.axis_index("pen") * BK
-    for h in range(2):
-        rows = pl.ds(8 * h, 8)
-        ez = jnp.concatenate(
-            [jnp.full((1, N), ez_ref[k0 + 8 * h + i], F32) for i in range(8)], axis=0
+    ez = jnp.concatenate([third_eigen(ez_ref, h) for h in range(2)], axis=0)
+    rho, factor = decay(ABSORPTION / CONDUCT + ez + ey_ref[...])
+
+    def state(side):
+        return jnp.concatenate(
+            [
+                jnp.concatenate([recv_ref[i, 4 * side + b] for i in range(BK)], axis=0)
+                for b in range(4)
+            ],
+            axis=1,
         )
-        rho, factor = decay(ABSORPTION / CONDUCT + ez + ey_ref[...])
-
-        def state(side):
-            return jnp.concatenate(
-                [
-                    jnp.concatenate(
-                        [recv_ref[8 * h + i, 4 * side + b] for i in range(8)],
-                        axis=0,
-                    )
-                    for b in range(4)
-                ],
-                axis=1,
-            )
-
-        def rise(x, carry):
-            f = fr_ref[x, rows] - step * fq_ref[x, rows]
-            carry = f + rho * carry
-            f_ref[x] = f
-            u_ref[x, rows] = carry
-            return carry
-
-        def fall(i, carry):
-            x = BX - 1 - i
-            f = f_ref[x]
-            u_ref[x, rows] = factor * (u_ref[x, rows] + rho * carry)
-            return f + rho * carry
-
-        lax.fori_loop(0, BX, rise, state(0))
-        lax.fori_loop(0, BX, fall, state(1))
-
+
+    def rise(x, carry):
+        f = fr_ref[x] - step * fq_ref[x]
+        carry = f + rho * carry
+        f_ref[x] = f
+        u_ref[x] = carry
+        return carry
+
+    def fall(i, carry):
+        x = BX - 1 - i
+        carry = rho * carry
+        u_ref[x] = factor * (u_ref[x] + carry)
+        return f_ref[x] + carry
+
+    lax.fori_loop(0, BX, rise, state(0), unroll=4)
+    lax.fori_loop(0, BX, fall, state(1), unroll=4)
     y_ref[...] = matmul(u_ref[...].reshape(BX * BK, N), c_ref[...], ((1,), (0,))).reshape(BX, BK, N)
-    for b in range(4):
+
+    def part(b, _):
         for s in range(4):
             for a in range(2):
                 rows = swap_units(
@@ -296,6 +333,9 @@
                 )
                 for i in range(8):
                     send_ref[8 * s + i, 4 * a + b] = rows[i]
+        return 0
+
+    lax.fori_loop(0, 4, part, 0)
     sums = recv_ref[0, 8]
     for p in range(1, GRP):
         sums = sums + recv_ref[p, 8]
@@ -306,19 +346,21 @@
         send_ref[j, 8] = sums
 
 
-def finish_kernel(recv_ref, r_ref, d_ref, q_ref, control_ref, c_ref, nr_ref, nd_ref, g_ref):
+def new_residual_kernel(r_ref, q_ref, control_ref, out_ref):
+    out_ref[...] = r_ref[...] - control_ref[0, 0:1, 0:1] * q_ref[...]
+
+
+def finish_kernel(recv_ref, d_ref, control_ref, c_ref, out_ref, g_ref):
     for b in range(4):
         for a in range(2):
             g_ref[:, a, :, 128 * b : 128 * b + 128] = recv_ref[:, 4 * a + b]
     sums = recv_ref[0, 8]
     for j in range(1, PEN):
         sums = sums + recv_ref[j, 8]
-    step = control_ref[0, 0:1, 0:1]
     conjugacy = jnp.full((8, 128), jnp.sum(sums), F32)
     ratio = (conjugacy / control_ref[1])[0:1, 0:1]
     smoothed = matmul(g_ref[...].reshape(N, BX * BY), c_ref[...], ((0,), (0,)))
-    nd_ref[...] = smoothed.reshape(BX, BY, N) - ratio * d_ref[...]
-    nr_ref[...] = r_ref[...] - step * q_ref[...]
+    out_ref[...] = smoothed.reshape(BX, BY, N) - ratio * d_ref[...]
 
 
 def shape(*dims):
@@ -348,9 +390,12 @@
     ey_tile = jnp.asarray(np.concatenate([eigen.reshape(4, 128)] * 2, 0))
     block = shape(BX, BY, N)
 
+    (send,) = call(residual_kernel, [VMEM] * 2, [shape(PEN, 8, 8, 128)])(residual, matrix)
+    recv_r = exchange(send, "pen")
+
     xlo, xhi, ylo, yhi = call(
         faces_kernel,
-        [pl.BlockSpec(memory_space=pl.ANY)] * 2,
+        [HBM] * 2,
         [shape(1, BY, N), shape(1, BY, N), shape(BX, N), shape(BX, N)],
         [
             pltpu.VMEM((BX, BY, N), F32),
@@ -368,15 +413,26 @@
     xl, xh = up(xhi, "grp", GRP), down(xlo, "grp", GRP)
     yl, yh = up(yhi, "pen", PEN), down(ylo, "pen", PEN)
 
-    (modes_r,) = call(residual_kernel, [VMEM] * 2, [shape(N, BX * BY)])(residual, matrix)
-    operated, send = call(
-        operated_kernel, [VMEM] * 9, [block, shape(PEN, 17, 8, 128)], [(BX + 2, BY, N)]
-    )(residual, direction, material, modes_r, xl, xh, yl, yh, matrix)
-
-    recv = exchange(send, "pen")
-    field_r, field_q, send = call(
-        blocks_kernel, [VMEM, VMEM, SMEM, VMEM], [block, block, shape(GRP, 17, 1, 128)], [(BX, BK, N)]
-    )(recv, matrix, ez, ey_row)
+    inner, sums = call(
+        inner_kernel, [VMEM] * 3, [block, shape(2, 8, 128)], [(BX + 2, BY, N)]
+    )(residual, direction, material)
+    operated, send = call(operated_kernel, [VMEM] * 9, [block, shape(PEN, 9, 8, 128)])(
+        inner, sums, direction, material, xl, xh, yl, yh, matrix
+    )
+    recv_q = exchange(send, "pen")
+
+    field_r, states = call(
+        residual_blocks_kernel,
+        [VMEM, VMEM, SMEM, VMEM],
+        [block, shape(GRP, 8, 1, 128)],
+        [(BX, BK, N)],
+    )(recv_r, matrix, ez, ey_row)
+    field_q, send = call(
+        operated_blocks_kernel,
+        [VMEM] * 4 + [SMEM, VMEM],
+        [block, shape(GRP, 17, 1, 128)],
+        [(BX, BK, N)],
+    )(recv_q, field_r, states, matrix, ez, ey_row)
 
     recv = exchange(send, "grp")
     send, control = call(
@@ -388,15 +444,15 @@
         solve_kernel,
         [VMEM] * 5 + [SMEM, VMEM],
         [shape(PEN, 9, 8, 128)],
-        [(BX, 8, N), (BX, BK, N), (BX, BK, N)],
+        [(BX, BK, N)] * 3,
     )(field_r, field_q, recv, control, matrix, ez, ey_row)
 
     recv = exchange(send, "pen")
-    return tuple(
-        call(finish_kernel, [VMEM] * 6, [block, block], [(PEN, 2, 8, BX * BY)])(
-            recv, residual, direction, operated, control, matrix
-        )
+    (new_residual,) = call(new_residual_kernel, [VMEM] * 3, [block])(residual, operated, control)
+    (new_direction,) = call(finish_kernel, [VMEM] * 4, [block], [(PEN, 2, 8, BX * BY)])(
+        recv, direction, control, matrix
     )
+    return new_residual, new_direction
 
 
 def solution(mesh):

time: 153 us -> 152 us (level)
  blocking collectives: 107 us -> 45 us
  waiting for transfers between devices: 1.82 us -> 31 us
  starting transfers between devices: 12.7 us -> 34.4 us
  local copies, waits for them, and re-layouts: 2.57 us -> 8.85 us
  Pallas kernels: 27.7 us -> 30.5 us
    all_to_all x4 -> x2, blocking collectives: 107 us -> 45 us  [exchange(): return lax.all_to_all(x, axis, 0, 0)]
    all_to_all x0 -> x3, waiting for transfers between devices: none -> 28.7 us  [exchange(): return lax.all_to_all(x, axis, 0, 0)]
    all_to_all x0 -> x3, starting transfers between devices: none -> 26.3 us  [exchange(): return lax.all_to_all(x, axis, 0, 0)]
    unnamed x20 -> x32, local copies, waits for them, and re-layouts: 2.57 us -> 8.85 us
    ppermute x2, starting transfers between devices: 6.78 us -> 3.34 us  [down(): return lax.ppermute(x, axis, [(i + 1, i) for i in range(count - 1)])]
    pallas_call x5 -> x8, Pallas kernels: 21.6 us -> 25 us  [the longest x1 5.52 us: on_device(): call(operated_blocks_kernel, [VMEM] * 4 + [SMEM, VMEM], [block, shape(GRP...]
  transfers between devices with their start and end apart: 4 -> 7, of which waited for: 1 -> 3; matrix products, arithmetic and copies ran while one was open for 0% -> 0% of each run, Pallas kernels for 1% -> 9%
where the time goes in v3:
time: 152 us; the launch traced here: 151 us
  blocking collectives  45 us (30%)
  starting transfers between devices  34.4 us (23%)
  waiting for transfers between devices  31 us (20%)
  Pallas kernels  30.5 us (20%)
  local copies, waits for them, and re-layouts  8.85 us (6%)
    all_to_all x2, blocking collectives, exchange(): return lax.all_to_all(x, axis, 0, 0)  45 us
    all_to_all x3, waiting for transfers between devices, exchange(): return lax.all_to_all(x, axis, 0, 0)  28.7 us
    all_to_all x3, starting transfers between devices, exchange(): return lax.all_to_all(x, axis, 0, 0)  26.3 us
    unnamed x32, local copies, waits for them, and re-layouts  8.85 us
    pallas_call x1, Pallas kernels, on_device(): call(operated_blocks_kernel, [VMEM] * 4 + [SMEM, VMEM], [block, shape(GRP...  5.52 us
    ppermute x2, starting transfers between devices, up(): return lax.ppermute(x, axis, [(i, i + 1) for i in range(count - 1)])  4.84 us
    pallas_call x1, Pallas kernels, on_device(): call(residual_blocks_kernel, [VMEM, VMEM, SMEM, VMEM], [block, shape(GRP,...  4.81 us
    pallas_call x1, Pallas kernels, on_device(): call(solve_kernel, [VMEM] * 5 + [SMEM, VMEM], [shape(PEN, 9, 8, 128)], [(...  4.62 us
  transfers between devices with their start and end apart: 7, of which 3 were waited for; matrix products, arithmetic and copies ran while one was open for 0% of the time, Pallas kernels for 9%

profile of v3, /device:TPU:1, one launch (start us, length us, event | category | flops | bytes accessed | tf_op | source)
XLA Modules:
  0.0 150.7 jit_solution(15995413122849085778)
XLA Ops:
  0.6 0.0 copy-start
  0.6 1.2 copy-done
  1.9 1.2 copy-done.3
  3.1 1.8 %shard_map.89 = f32[32,8,8,128]{3,2,1,0:T(8,128)S(1)} custom-call(f32[32,16,512]{2,1,0:T(8,128)S(1)} %copy-done.3, f32[512,512]{1,0:T(8,128)S(1)} %copy-done), custom_call_target="tpu_custom_call" | custom-call | tf_op jit(solution)/shard_map/pallas_call | solution.py:393
  4.9 1.0 copy-done.8
  5.9 11.2 %all-to-all-start.1 = ((f32[32,8,8,128]{3,2,1,0:T(8,128)}), f32[32,8,8,128]{3,2,1,0:T(8,128)}, u32[]{:S(2)}, u32[]{:S(2)}) async-start(f32[32,8,8,128]{3,2,1,0:T(8,128)} %copy-done.8), calls=%async_computation.1 | async-start | bytes 2097152 | tf_op jit(solution)/shard_map/all_to_all | solution.py:382
  17.2 3.0 %shard_map.87 = (f32[1,16,512]{2,1,0:T(8,128)S(1)}, f32[1,16,512]{2,1,0:T(8,128)S(1)}, f32[32,512]{1,0:T(8,128)S(1)}, f32[32,512]{1,0:T(8,128)S(1)}) custom-call(f32[32,16,512]{2,1,0:T(8,128)S(1)} %copy-done.2, s32[32,16,512]{2,1,0:T(8,128)S(1)} %copy-done.5), custom_call_target="tpu_custom_call" | custom-call | tf_op jit(solution)/shard_map/pallas_call | solution.py:396
  20.2 3.5 %collective-permute-start.2 = (f32[32,512]{1,0:T(8,128)S(1)}, f32[32,512]{1,0:T(8,128)S(1)}, u32[]{:S(2)}, u32[]{:S(2)}) collective-permute-start(f32[32,512]{1,0:T(8,128)S(1)} %get-tuple-element.20), channel_id=1, source_target_pairs={{0,1},{1,2},{2,3},{3,4},{4,5},{5,6},{6,7},{7,8},{8,9},{9,10},{10,1... | collective-permute-start | bytes 196616 | tf_op jit(solution)/shard_map/ppermute | solution.py:408
  23.7 1.9 %collective-permute-start.3 = (f32[32,512]{1,0:T(8,128)S(1)}, f32[32,512]{1,0:T(8,128)S(1)}, u32[]{:S(2)}, u32[]{:S(2)}) collective-permute-start(f32[32,512]{1,0:T(8,128)S(1)} %get-tuple-element.21), channel_id=1, source_target_pairs={{1,0},{2,1},{3,2},{4,3},{5,4},{6,5},{7,6},{8,7},{9,8},{10,9},{11,1... | collective-permute-start | bytes 196616 | tf_op jit(solution)/shard_map/ppermute | solution.py:411
  25.7 1.3 collective-permute-start
  27.0 0.0 copy-start.1
  27.0 1.4 collective-permute-start.1
  28.4 1.4 shard_map.86
  29.8 2.3 %collective-permute-done.1.xh_ref = f32[1,16,512]{2,1,0:T(8,128)S(1)} collective-permute-done((f32[1,16,512]{2,1,0:T(8,128)S(1)}, f32[1,16,512]{2,1,0:T(8,128)S(1)}, u32[]{:S(2)}, u32[]{:S(2)}) %collective-permute-start.1) | collective-permute-done | bytes 32800 | tf_op jit(solution)/shard_map/ppermute | solution.py:411
  32.2 3.2 %shard_map.88 = (f32[32,16,512]{2,1,0:T(8,128)S(1)}, f32[32,9,8,128]{3,2,1,0:T(8,128)}) custom-call(f32[32,16,512]{2,1,0:T(8,128)S(1)} %get-tuple-element.16.q_ref, f32[2,8,128]{2,1,0:T(8,128)S(1)} %get-tuple-element.17.sums_ref, f32[32,16,512]{2,1,0:T(8,128)S(1)} %copy-done.2, s32[32,16,512]{2,1,0:T(8,128)S(1)} %copy-done.6, ...), custom_call_target="tpu_custom_call" | custom-call | tf_op jit(solution)/shard_map/pallas_call | solution.py:419
  35.4 1.0 copy-done.11
  36.3 8.5 %all-to-all-start = ((f32[32,9,8,128]{3,2,1,0:T(8,128)}), f32[32,9,8,128]{3,2,1,0:T(8,128)}, u32[]{:S(2)}, u32[]{:S(2)}) async-start(f32[32,9,8,128]{3,2,1,0:T(8,128)} %get-tuple-element.23), calls=%async_computation | async-start | bytes 2359296 | tf_op jit(solution)/shard_map/all_to_all | solution.py:382
  44.9 4.8 %shard_map.90 = (f32[32,16,512]{2,1,0:T(8,128)S(1)}, f32[16,8,1,128]{3,2,1,0:T(1,128)S(1)}) custom-call(f32[32,8,8,128]{3,2,1,0:T(8,128)} %all-to-all-done.1.recv_ref, f32[512,512]{1,0:T(8,128)S(1)} %copy-done.1, f32[512]{0:T(512)S(1)} %copy-done.13, f32[1,512]{1,0:T(1,128)S(1)} %copy-done.14), custom_call_target="tpu_custom_call" | custom-call | tf_op jit(solution)/shard_map/pallas_call | solution.py:424
  49.7 1.0 copy-done.9
  50.7 12.6 %all-to-all-done.recv_ref = f32[32,9,8,128]{3,2,1,0:T(8,128)} async-done(((f32[32,9,8,128]{3,2,1,0:T(8,128)}), f32[32,9,8,128]{3,2,1,0:T(8,128)}, u32[]{:S(2)}, u32[]{:S(2)}) %all-to-all-start) | async-done | bytes 1179680 | tf_op jit(solution)/shard_map/all_to_all | solution.py:382
  63.3 1.2 copy-done.10
  64.5 5.5 %shard_map.91 = (f32[32,16,512]{2,1,0:T(8,128)S(1)}, f32[16,17,1,128]{3,2,1,0:T(1,128)S(1)}) custom-call(f32[32,9,8,128]{3,2,1,0:T(8,128)} %all-to-all-done.recv_ref, f32[32,16,512]{2,1,0:T(8,128)S(1)} %copy-done.10, f32[16,8,1,128]{3,2,1,0:T(1,128)S(1)} %get-tuple-element.25.states_ref, f32[512,512]{1,0:T(8,128)S(1)} %copy-done.1, f32[512]{0:T(512)S(1)} %copy-done.13, ...), custom_call_target="tpu_custom_call" | custom-call | tf_op jit(solution)/shard_map/pallas_call | solution.py:430
  70.0 26.7 %all_to_all.25.recv_ref = f32[16,17,1,128]{3,2,1,0:T(1,128)S(1)} all-to-all(f32[16,17,1,128]{3,2,1,0:T(1,128)S(1)} %get-tuple-element.26), channel_id=1, replica_groups=mesh['grp'=16,'pen'=32] {'grp'}, dimensions={0} | all-to-all | bytes 278528 | tf_op jit(solution)/shard_map/all_to_all | solution.py:382
  96.7 0.9 shard_map.92
  97.6 18.3 %all_to_all.26.recv_ref = f32[16,9,1,128]{3,2,1,0:T(1,128)S(1)} all-to-all(f32[16,9,1,128]{3,2,1,0:T(1,128)S(1)} %get-tuple-element.29), channel_id=1, replica_groups=mesh['grp'=16,'pen'=32] {'grp'}, dimensions={0} | all-to-all | bytes 147456 | tf_op jit(solution)/shard_map/all_to_all | solution.py:382
  115.9 4.6 %shard_map.94 = f32[32,9,8,128]{3,2,1,0:T(8,128)S(1)} custom-call(f32[32,16,512]{2,1,0:T(8,128)S(1)} %copy-done.10, f32[32,16,512]{2,1,0:T(8,128)S(1)} %get-tuple-element.28.fq_ref, f32[16,9,1,128]{3,2,1,0:T(1,128)S(1)} %all_to_all.26.recv_ref, f32[3,8,128]{2,1,0:T(8,128)S(1)} %get-tuple-element.27.control_ref, f32[512,512]{1,0:T(8,128)S(1)} %copy-done.1, ...), custom_call_target="tpu_custom_call" | custom-call | tf_op jit(solution)/shard_map/pallas_call | solution.py:443
  120.6 1.0 copy-done.7
  121.6 6.5 %all-to-all-start.4 = ((f32[32,9,8,128]{3,2,1,0:T(8,128)}), f32[32,9,8,128]{3,2,1,0:T(8,128)}, u32[]{:S(2)}, u32[]{:S(2)}) async-start(f32[32,9,8,128]{3,2,1,0:T(8,128)} %copy-done.7), calls=%async_computation.4 | async-start | bytes 2359296 | tf_op jit(solution)/shard_map/all_to_all | solution.py:382
  128.1 1.2 copy-done.12
  129.3 1.2 shard_map.93
  130.5 16.1 %all-to-all-done.4.recv_ref = f32[32,9,8,128]{3,2,1,0:T(8,128)} async-done(((f32[32,9,8,128]{3,2,1,0:T(8,128)}), f32[32,9,8,128]{3,2,1,0:T(8,128)}, u32[]{:S(2)}, u32[]{:S(2)}) %all-to-all-start.4) | async-done | bytes 1179680 | tf_op jit(solution)/shard_map/all_to_all | solution.py:382
  146.6 4.1 %shard_map.95 = f32[32,16,512]{2,1,0:T(8,128)} custom-call(f32[32,9,8,128]{3,2,1,0:T(8,128)} %all-to-all-done.4.recv_ref, f32[32,16,512]{2,1,0:T(8,128)S(1)} %copy-done.2, f32[3,8,128]{2,1,0:T(8,128)S(1)} %get-tuple-element.27.control_ref, f32[512,512]{1,0:T(8,128)S(1)} %copy-done.1), custom_call_target="tpu_custom_call" | custom-call | tf_op jit(solution)/shard_map/pallas_call | solution.py:452
  (26 shorter events, 0.1 us)
Async XLA Ops:
  0.6 1.2 copy-start
  1.9 1.2 copy-start.3
  4.9 1.0 copy-start.8
  5.9 11.3 %copy-start.2 = (f32[32,16,512]{2,1,0:T(8,128)S(1)}, f32[32,16,512]{2,1,0:T(8,128)}, u32[]{:S(2)}) copy-start(f32[32,16,512]{2,1,0:T(8,128)} %d_ref.5) | copy-start | bytes 3145732
  5.9 11.3 %copy-start.5 = (s32[32,16,512]{2,1,0:T(8,128)S(1)}, s32[32,16,512]{2,1,0:T(8,128)}, u32[]{:S(2)}) copy-start(s32[32,16,512]{2,1,0:T(8,128)} %m_ref.3) | copy-start | bytes 3145732
  5.9 30.4 %all-to-all-start.1 = ((f32[32,8,8,128]{3,2,1,0:T(8,128)}), f32[32,8,8,128]{3,2,1,0:T(8,128)}, u32[]{:S(2)}, u32[]{:S(2)}) async-start(f32[32,8,8,128]{3,2,1,0:T(8,128)} %copy-done.8), calls=%async_computation.1 | async-start | bytes 2097152 | tf_op jit(solution)/shard_map/all_to_all | solution.py:382
  17.2 11.2 %copy-start.4 = (f32[32,16,512]{2,1,0:T(8,128)S(1)}, f32[32,16,512]{2,1,0:T(8,128)}, u32[]{:S(2)}) copy-start(f32[32,16,512]{2,1,0:T(8,128)} %r_ref.5) | copy-start | bytes 3145732
  17.2 11.2 %copy-start.6 = (s32[32,16,512]{2,1,0:T(8,128)S(1)}, s32[32,16,512]{2,1,0:T(8,128)}, u32[]{:S(2)}) copy-start(s32[32,16,512]{2,1,0:T(8,128)} %m_ref.3) | copy-start | bytes 3145732
  20.2 12.0 %collective-permute-start.2 = (f32[32,512]{1,0:T(8,128)S(1)}, f32[32,512]{1,0:T(8,128)S(1)}, u32[]{:S(2)}, u32[]{:S(2)}) collective-permute-start(f32[32,512]{1,0:T(8,128)S(1)} %get-tuple-element.20), channel_id=1, source_target_pairs={{0,1},{1,2},{2,3},{3,4},{4,5},{5,6},{6,7},{7,8},{8,9},{9,10},{10,1... | collective-permute-start | bytes 196616 | tf_op jit(solution)/shard_map/ppermute | solution.py:408
  23.7 8.4 %collective-permute-start.3 = (f32[32,512]{1,0:T(8,128)S(1)}, f32[32,512]{1,0:T(8,128)S(1)}, u32[]{:S(2)}, u32[]{:S(2)}) collective-permute-start(f32[32,512]{1,0:T(8,128)S(1)} %get-tuple-element.21), channel_id=1, source_target_pairs={{1,0},{2,1},{3,2},{4,3},{5,4},{6,5},{7,6},{8,7},{9,8},{10,9},{11,1... | collective-permute-start | bytes 196616 | tf_op jit(solution)/shard_map/ppermute | solution.py:411
  25.7 4.2 %collective-permute-start = (f32[1,16,512]{2,1,0:T(8,128)S(1)}, f32[1,16,512]{2,1,0:T(8,128)S(1)}, u32[]{:S(2)}, u32[]{:S(2)}) collective-permute-start(f32[1,16,512]{2,1,0:T(8,128)S(1)} %get-tuple-element.18), channel_id=1, source_target_pairs={{0,32},{32,64},{64,96},{96,128},{128,160},{160,192},{192,224},{224... | collective-permute-start | bytes 98312 | tf_op jit(solution)/shard_map/ppermute | solution.py:408
  27.0 5.2 %copy-start.1 = (f32[512,512]{1,0:T(8,128)S(1)}, f32[512,512]{1,0:T(8,128)}, u32[]{:S(2)}) copy-start(f32[512,512]{1,0:T(8,128)} %constant.8.clone.c_ref) | copy-start | bytes 3145732
  27.0 5.2 %collective-permute-start.1 = (f32[1,16,512]{2,1,0:T(8,128)S(1)}, f32[1,16,512]{2,1,0:T(8,128)S(1)}, u32[]{:S(2)}, u32[]{:S(2)}) collective-permute-start(f32[1,16,512]{2,1,0:T(8,128)S(1)} %get-tuple-element.19), channel_id=1, source_target_pairs={{32,0},{64,32},{96,64},{128,96},{160,128},{192,160},{224,192},{256... | collective-permute-start | bytes 98312 | tf_op jit(solution)/shard_map/ppermute | solution.py:411
  35.4 1.0 copy-start.11
  36.3 8.5 %copy-start.13 = (f32[512]{0:T(512)S(1)}, f32[512]{0:T(512)}, u32[]{:S(2)}) copy-start(f32[512]{0:T(512)} %constant.9.clone.ez_ref) | copy-start | bytes 6148
  36.3 8.5 %copy-start.14 = (f32[1,512]{1,0:T(1,128)S(1)}, f32[1,512]{1,0:T(1,128)}, u32[]{:S(2)}) copy-start(f32[1,512]{1,0:T(1,128)} %constant.10.clone.ey_ref) | copy-start | bytes 6148
  36.3 26.9 %all-to-all-start = ((f32[32,9,8,128]{3,2,1,0:T(8,128)}), f32[32,9,8,128]{3,2,1,0:T(8,128)}, u32[]{:S(2)}, u32[]{:S(2)}) async-start(f32[32,9,8,128]{3,2,1,0:T(8,128)} %get-tuple-element.23), calls=%async_computation | async-start | bytes 2359296 | tf_op jit(solution)/shard_map/all_to_all | solution.py:382
  49.7 1.0 copy-start.9
  63.3 1.2 copy-start.10
  64.5 32.2 %copy-start.15 = (f32[8,128]{1,0:T(8,128)S(1)}, f32[8,128]{1,0:T(8,128)}, u32[]{:S(2)}) copy-start(f32[8,128]{1,0:T(8,128)} %constant.11.clone.ey_ref) | copy-start | bytes 12292
  120.5 1.0 copy-start.7
  121.6 25.0 %all-to-all-start.4 = ((f32[32,9,8,128]{3,2,1,0:T(8,128)}), f32[32,9,8,128]{3,2,1,0:T(8,128)}, u32[]{:S(2)}, u32[]{:S(2)}) async-start(f32[32,9,8,128]{3,2,1,0:T(8,128)} %copy-done.7), calls=%async_computation.4 | async-start | bytes 2359296 | tf_op jit(solution)/shard_map/all_to_all | solution.py:382
  128.1 1.2 copy-start.12

commit v4 on v3

--- a/solution.py
+++ b/solution.py
@@ -14,7 +14,6 @@
 PEN = 32
 BX = N // GRP
 BY = N // PEN
-PARTS = 8
 BK = N // PEN
 ABSORPTION = 0.02
 CONDUCT = 5.0
@@ -74,34 +73,61 @@
     return jnp.where(material == 1, jnp.float32(SOLID), jnp.float32(1.0))
 
 
-def faces_kernel(d_hbm, m_hbm, xlo_ref, xhi_ref, ylo_ref, yhi_ref, d_ref, m_ref, sems):
-    copies = []
-    for i in range(PARTS):
-        part = pl.ds(i * (BX // PARTS), BX // PARTS)
-        for j, (source, target) in enumerate(((d_hbm, d_ref), (m_hbm, m_ref))):
-            copies.append(pltpu.make_async_copy(source.at[part], target.at[part], sems.at[i, j]))
-            copies[-1].start()
-    for copy in copies:
-        copy.wait()
+def faces_kernel(d_ref, m_ref, xlo_ref, xhi_ref, ylo_ref, yhi_ref):
     xlo_ref[0] = stiffness_of(m_ref[0]) * d_ref[0]
     xhi_ref[0] = stiffness_of(m_ref[BX - 1]) * d_ref[BX - 1]
     ylo_ref[...] = stiffness_of(m_ref[:, 0, :]) * d_ref[:, 0, :]
     yhi_ref[...] = stiffness_of(m_ref[:, BY - 1, :]) * d_ref[:, BY - 1, :]
 
 
-def third_modes(field_ref, c_ref):
-    return matmul(c_ref[...], field_ref[...].reshape(BX * BY, N), ((1,), (1,)))
-
-
-def put_modes(modes, first, send_ref):
-    for b in range(4):
-        part = modes[:, 128 * b : 128 * b + 128].reshape(PEN, 2, 8, 128)
+def start(copies):
+    for copy in copies:
+        copy.start()
+    return copies
+
+
+def wait(copies):
+    for copy in copies:
+        copy.wait()
+
+
+def send_third_modes(field_ref, c_ref, ready, send_ref, send_hbm, sems):
+    copies = []
+    for h in range(2):
+        ready(h)
+        field = field_ref[16 * h : 16 * h + 16].reshape(16 * BY, N)
+        modes = matmul(c_ref[...], field, ((1,), (1,)))
+        for b in range(2):
+            part = modes[:, 128 * b : 128 * b + 128].reshape(PEN, 2, 8, 128)
+            for a in range(2):
+                tile = 4 * a + 2 * h + b
+                send_ref[:, tile] = part[:, a]
         for a in range(2):
-            send_ref[:, first + 4 * a + b] = part[:, a]
-
-
-def residual_kernel(r_ref, c_ref, send_ref):
-    put_modes(third_modes(r_ref, c_ref), 0, send_ref)
+            tiles = pl.ds(4 * a + 2 * h, 2)
+            copies += start(
+                [pltpu.make_async_copy(send_ref.at[:, tiles], send_hbm.at[:, tiles], sems.at[2 * h + a])]
+            )
+    return copies
+
+
+def residual_kernel(r_hbm, c_hbm, send_hbm, r_ref, c_ref, send_ref, sems):
+    into_c = [
+        pltpu.make_async_copy(c_hbm.at[rows], c_ref.at[rows], sems.at[4 + i])
+        for i, rows in enumerate(pl.ds(128 * i, 128) for i in range(4))
+    ]
+    into_r = [
+        pltpu.make_async_copy(r_hbm.at[part], r_ref.at[part], sems.at[8 + i])
+        for i, part in enumerate(pl.ds(8 * i, 8) for i in range(4))
+    ]
+    for i in (0, 1):
+        start(into_c[2 * i : 2 * i + 2] + into_r[2 * i : 2 * i + 2])
+
+    def ready(h):
+        if h == 0:
+            wait(into_c)
+        wait(into_r[2 * h : 2 * h + 2])
+
+    wait(send_third_modes(r_ref, c_ref, ready, send_ref, send_hbm, sems))
 
 
 def inner_kernel(r_ref, d_ref, m_ref, q_ref, sums_ref, u_ref):
@@ -134,7 +160,7 @@
 
 
 def operated_kernel(
-    q_ref, sums_ref, d_ref, m_ref, xl_ref, xh_ref, yl_ref, yh_ref, c_ref, out_ref, send_ref
+    q_ref, sums_ref, d_ref, m_ref, xl_ref, xh_ref, yl_ref, yh_ref, c_ref, out_hbm, send_hbm, out_ref, send_ref, sems
 ):
     row = lax.broadcasted_iota(jnp.int32, (8, N), 0)
 
@@ -155,13 +181,21 @@
     curvature = sums_ref[0] - to_tile(total)
     half = lax.broadcasted_iota(jnp.int32, (8, 128), 0) < 4
     sums = jnp.where(half, fold(curvature, 4), fold(sums_ref[1], 4))
-    put_modes(third_modes(out_ref, c_ref), 0, send_ref)
     for j in range(PEN):
         send_ref[j, 8] = sums
-
-
-def second_modes(recv_ref, c_ref, out_ref, y_ref):
+    copies = start(
+        [
+            pltpu.make_async_copy(out_ref, out_hbm, sems.at[4]),
+            pltpu.make_async_copy(send_ref.at[:, pl.ds(8, 1)], send_hbm.at[:, pl.ds(8, 1)], sems.at[5]),
+        ]
+    )
+    copies += send_third_modes(out_ref, c_ref, lambda h: None, send_ref, send_hbm, sems)
+    wait(copies)
+
+
+def second_modes(recv_ref, c_ref, out_ref, y_ref, ready=lambda b: None):
     def part(b, _):
+        ready(b)
         for s in range(4):
             for a in range(2):
                 rows = swap_units([recv_ref[8 * s + i, 4 * a + b] for i in range(8)])
@@ -185,8 +219,9 @@
                 send_ref[8 * h + i, first + 4 * side + b] = x[i : i + 1, 128 * b : 128 * b + 128]
 
 
-def residual_blocks_kernel(recv_ref, c_ref, ez_ref, ey_ref, fr_ref, states_ref, y_ref):
+def residual_blocks_kernel(recv_ref, c_ref, ez_ref, ey_ref, fr_hbm, states_ref, y_ref, fr_ref, sem):
     second_modes(recv_ref, c_ref, fr_ref, y_ref)
+    copies = start([pltpu.make_async_copy(fr_ref, fr_hbm, sem)])
     for h in range(2):
         rows = pl.ds(8 * h, 8)
         rho, _ = decay(ABSORPTION / CONDUCT + third_eigen(ez_ref, h) + ey_ref[...])
@@ -199,12 +234,29 @@
         zero = jnp.zeros((8, N), F32)
         _, v, w = lax.fori_loop(0, BX, sweep, (jnp.ones((8, N), F32), zero, zero), unroll=4)
         put_states(v, w, h, states_ref, 0)
+    wait(copies)
 
 
 def operated_blocks_kernel(
-    recv_ref, fr_ref, states_ref, c_ref, ez_ref, ey_ref, fq_ref, send_ref, y_ref
+    recv_hbm, fr_hbm, states_ref, c_ref, ez_ref, ey_ref, fq_ref, send_ref, y_ref, recv_ref, fr_ref, sems
 ):
-    second_modes(recv_ref, c_ref, fq_ref, y_ref)
+    def into(b):
+        tiles = [b, b + 4]
+        return [
+            pltpu.make_async_copy(recv_hbm.at[:, t], recv_ref.at[:, t], sems.at[i, b])
+            for i, t in enumerate(tiles)
+        ]
+
+    for b in range(4):
+        start(into(b))
+    late = start(
+        [
+            pltpu.make_async_copy(recv_hbm.at[:, 8], recv_ref.at[:, 8], sems.at[2, 0]),
+            pltpu.make_async_copy(fr_hbm, fr_ref, sems.at[2, 1]),
+        ]
+    )
+    second_modes(recv_ref, c_ref, fq_ref, y_ref, lambda b: wait(into(b)))
+    wait(late)
     dots = [jnp.zeros((8, 128), F32), jnp.zeros((8, 128), F32)]
     for h in range(2):
         rows = pl.ds(8 * h, 8)
@@ -346,11 +398,11 @@
         send_ref[j, 8] = sums
 
 
-def new_residual_kernel(r_ref, q_ref, control_ref, out_ref):
-    out_ref[...] = r_ref[...] - control_ref[0, 0:1, 0:1] * q_ref[...]
-
-
-def finish_kernel(recv_ref, d_ref, control_ref, c_ref, out_ref, g_ref):
+def finish_kernel(
+    recv_ref, r_ref, d_ref, q_ref, control_ref, c_ref, nr_hbm, nd_hbm, g_ref, nr_ref, nd_ref, sems
+):
+    nr_ref[...] = r_ref[...] - control_ref[0, 0:1, 0:1] * q_ref[...]
+    copies = start([pltpu.make_async_copy(nr_ref, nr_hbm, sems.at[0])])
     for b in range(4):
         for a in range(2):
             g_ref[:, a, :, 128 * b : 128 * b + 128] = recv_ref[:, 4 * a + b]
@@ -359,19 +411,28 @@
         sums = sums + recv_ref[j, 8]
     conjugacy = jnp.full((8, 128), jnp.sum(sums), F32)
     ratio = (conjugacy / control_ref[1])[0:1, 0:1]
-    smoothed = matmul(g_ref[...].reshape(N, BX * BY), c_ref[...], ((0,), (0,)))
-    out_ref[...] = smoothed.reshape(BX, BY, N) - ratio * d_ref[...]
+    for h in range(2):
+        part = pl.ds(16 * h, 16)
+        half = g_ref[:, :, :, 256 * h : 256 * h + 256].reshape(N, 256)
+        smoothed = matmul(half, c_ref[...], ((0,), (0,)))
+        nd_ref[part] = smoothed.reshape(16, BY, N) - ratio * d_ref[part]
+        copies += start([pltpu.make_async_copy(nd_ref.at[part], nd_hbm.at[part], sems.at[1 + h])])
+    wait(copies)
 
 
 def shape(*dims):
     return jax.ShapeDtypeStruct(dims, F32)
+
+
+def in_hbm(x):
+    return pltpu.with_memory_space_constraint(x, pltpu.HBM)
 
 
 def call(kernel, ins, outs, scratch=()):
     return pl.pallas_call(
         kernel,
         in_specs=ins,
-        out_specs=[VMEM] * len(outs),
+        out_specs=[VMEM if isinstance(out, jax.ShapeDtypeStruct) else HBM for out in outs],
         out_shape=outs,
         scratch_shapes=[pltpu.VMEM(s, F32) if isinstance(s, tuple) else s for s in scratch],
         compiler_params=PARAMS,
@@ -390,18 +451,16 @@
     ey_tile = jnp.asarray(np.concatenate([eigen.reshape(4, 128)] * 2, 0))
     block = shape(BX, BY, N)
 
-    (send,) = call(residual_kernel, [VMEM] * 2, [shape(PEN, 8, 8, 128)])(residual, matrix)
+    (send,) = call(
+        residual_kernel,
+        [HBM] * 2,
+        [pltpu.HBM((PEN, 8, 8, 128), F32)],
+        [(BX, BY, N), (N, N), (PEN, 8, 8, 128), pltpu.SemaphoreType.DMA((12,))],
+    )(in_hbm(residual), in_hbm(matrix))
     recv_r = exchange(send, "pen")
 
     xlo, xhi, ylo, yhi = call(
-        faces_kernel,
-        [HBM] * 2,
-        [shape(1, BY, N), shape(1, BY, N), shape(BX, N), shape(BX, N)],
-        [
-            pltpu.VMEM((BX, BY, N), F32),
-            pltpu.VMEM((BX, BY, N), jnp.int32),
-            pltpu.SemaphoreType.DMA((PARTS, 2)),
-        ],
+        faces_kernel, [VMEM] * 2, [shape(1, BY, N), shape(1, BY, N), shape(BX, N), shape(BX, N)]
     )(direction, material)
 
     def up(x, axis, count):
@@ -416,23 +475,26 @@
     inner, sums = call(
         inner_kernel, [VMEM] * 3, [block, shape(2, 8, 128)], [(BX + 2, BY, N)]
     )(residual, direction, material)
-    operated, send = call(operated_kernel, [VMEM] * 9, [block, shape(PEN, 9, 8, 128)])(
-        inner, sums, direction, material, xl, xh, yl, yh, matrix
-    )
+    operated, send = call(
+        operated_kernel,
+        [VMEM] * 9,
+        [pltpu.HBM((BX, BY, N), F32), pltpu.HBM((PEN, 9, 8, 128), F32)],
+        [(BX, BY, N), (PEN, 9, 8, 128), pltpu.SemaphoreType.DMA((6,))],
+    )(inner, sums, direction, material, xl, xh, yl, yh, matrix)
     recv_q = exchange(send, "pen")
 
     field_r, states = call(
         residual_blocks_kernel,
         [VMEM, VMEM, SMEM, VMEM],
-        [block, shape(GRP, 8, 1, 128)],
-        [(BX, BK, N)],
+        [pltpu.HBM((BX, BK, N), F32), shape(GRP, 8, 1, 128)],
+        [(BX, BK, N), (BX, BK, N), pltpu.SemaphoreType.DMA],
     )(recv_r, matrix, ez, ey_row)
     field_q, send = call(
         operated_blocks_kernel,
-        [VMEM] * 4 + [SMEM, VMEM],
+        [HBM, HBM, VMEM, VMEM, SMEM, VMEM],
         [block, shape(GRP, 17, 1, 128)],
-        [(BX, BK, N)],
-    )(recv_q, field_r, states, matrix, ez, ey_row)
+        [(BX, BK, N), (PEN, 9, 8, 128), (BX, BK, N), pltpu.SemaphoreType.DMA((3, 4))],
+    )(in_hbm(recv_q), in_hbm(field_r), states, matrix, ez, ey_row)
 
     recv = exchange(send, "grp")
     send, control = call(
@@ -448,11 +510,14 @@
     )(field_r, field_q, recv, control, matrix, ez, ey_row)
 
     recv = exchange(send, "pen")
-    (new_residual,) = call(new_residual_kernel, [VMEM] * 3, [block])(residual, operated, control)
-    (new_direction,) = call(finish_kernel, [VMEM] * 4, [block], [(PEN, 2, 8, BX * BY)])(
-        recv, direction, control, matrix
+    return tuple(
+        call(
+            finish_kernel,
+            [VMEM] * 6,
+            [pltpu.HBM((BX, BY, N), F32), pltpu.HBM((BX, BY, N), F32)],
+            [(PEN, 2, 8, BX * BY), (BX, BY, N), (BX, BY, N), pltpu.SemaphoreType.DMA((3,))],
+        )(recv, residual, direction, operated, control, matrix)
     )
-    return new_residual, new_direction
 
 
 def solution(mesh):

time: 152 us -> 145 us (0.954)
  blocking collectives: 45 us -> 69.2 us
  waiting for transfers between devices: 31 us -> 16.8 us
  local copies, waits for them, and re-layouts: 8.85 us -> 0.05 us
  starting transfers between devices: 34.4 us -> 26.8 us
    all_to_all x2 -> x3, blocking collectives: 45 us -> 69.2 us  [exchange(): return lax.all_to_all(x, axis, 0, 0)]
    all_to_all x3 -> x2, waiting for transfers between devices: 28.7 us -> 13.1 us  [exchange(): return lax.all_to_all(x, axis, 0, 0)]
    unnamed x32 -> x20, local copies, waits for them, and re-layouts: 8.85 us -> 0.05 us
    all_to_all x3 -> x2, starting transfers between devices: 26.3 us -> 18.5 us  [exchange(): return lax.all_to_all(x, axis, 0, 0)]
    pallas_call x7 -> x6, Pallas kernels: 23.6 us -> 23.9 us  [the longest x1 5.91 us: on_device(): call(operated_blocks_kernel, [HBM, HBM, VMEM, VMEM, SMEM, VMEM], [block,...]
  transfers between devices with their start and end apart: 7 -> 6, of which waited for: 3 -> 4; matrix products, arithmetic and copies ran while one was open for 0% -> 0% of each run, Pallas kernels for 9% -> 7%
where the time goes in v4:
time: 145 us
  blocking collectives  69.2 us (48%)
  Pallas kernels  30.8 us (21%)
  starting transfers between devices  26.8 us (18%)
  waiting for transfers between devices  16.8 us (12%)
    all_to_all x3, blocking collectives, exchange(): return lax.all_to_all(x, axis, 0, 0)  69.2 us
    all_to_all x2, starting transfers between devices, exchange(): return lax.all_to_all(x, axis, 0, 0)  18.5 us
    all_to_all x2, waiting for transfers between devices, exchange(): return lax.all_to_all(x, axis, 0, 0)  13.1 us
    pallas_call x1, Pallas kernels, on_device(): call(operated_blocks_kernel, [HBM, HBM, VMEM, VMEM, SMEM, VMEM], [block,...  5.91 us
    pallas_call x1, Pallas kernels, on_device(): call(residual_kernel, [HBM] * 2, [pltpu.HBM((PEN, 8, 8, 128), F32)], [(BX...  5.85 us
    pallas_call x1, Pallas kernels, on_device(): call(residual_blocks_kernel, [VMEM, VMEM, SMEM, VMEM], [pltpu.HBM((BX, BK...  5.54 us
    ppermute x2, starting transfers between devices, up(): return lax.ppermute(x, axis, [(i, i + 1) for i in range(count - 1)])  4.97 us
    pallas_call x1, Pallas kernels, on_device(): call(solve_kernel, [VMEM] * 5 + [SMEM, VMEM], [shape(PEN, 9, 8, 128)], [(...  4.62 us
  transfers between devices with their start and end apart: 6, of which 4 were waited for; matrix products, arithmetic and copies ran while one was open for 0% of the time, Pallas kernels for 7%

profile of v4, /device:TPU:1, one launch (start us, length us, event | category | flops | bytes accessed | tf_op | source)
XLA Modules:
  0.0 144.6 jit_solution(15842811240358577983)
XLA Ops:
  0.6 5.9 %shard_map.86 = f32[32,8,8,128]{3,2,1,0:T(8,128)} custom-call(f32[32,16,512]{2,1,0:T(8,128)} %r_ref.3, f32[512,512]{1,0:T(8,128)} %constant.8.clone.c_hbm.c_ref), custom_call_target="tpu_custom_call" | custom-call | tf_op jit(solution)/shard_map/pallas_call | solution.py:454
  6.5 0.0 copy-start.1
  6.5 0.0 copy-start.3
  6.5 11.3 %all-to-all-start = ((f32[32,8,8,128]{3,2,1,0:T(8,128)}), f32[32,8,8,128]{3,2,1,0:T(8,128)}, u32[]{:S(2)}, u32[]{:S(2)}) async-start(f32[32,8,8,128]{3,2,1,0:T(8,128)} %shard_map.86), calls=%async_computation | async-start | bytes 2097152 | tf_op jit(solution)/shard_map/all_to_all | solution.py:443
  17.8 0.0 copy-done.1
  17.8 0.0 copy-done.3
  17.8 0.0 copy-start.2
  17.8 0.0 copy-start.4
  17.8 0.1 shard_map.89
  17.9 3.7 %collective-permute-start.2 = (f32[32,512]{1,0:T(8,128)S(1)}, f32[32,512]{1,0:T(8,128)S(1)}, u32[]{:S(2)}, u32[]{:S(2)}) collective-permute-start(f32[32,512]{1,0:T(8,128)S(1)} %get-tuple-element.21), channel_id=1, source_target_pairs={{0,1},{1,2},{2,3},{3,4},{4,5},{5,6},{6,7},{7,8},{8,9},{9,10},{10,1... | collective-permute-start | bytes 196616 | tf_op jit(solution)/shard_map/ppermute | solution.py:467
  21.6 1.9 %collective-permute-start.3 = (f32[32,512]{1,0:T(8,128)S(1)}, f32[32,512]{1,0:T(8,128)S(1)}, u32[]{:S(2)}, u32[]{:S(2)}) collective-permute-start(f32[32,512]{1,0:T(8,128)S(1)} %get-tuple-element.22), channel_id=1, source_target_pairs={{1,0},{2,1},{3,2},{4,3},{5,4},{6,5},{7,6},{8,7},{9,8},{10,9},{11,1... | collective-permute-start | bytes 196616 | tf_op jit(solution)/shard_map/ppermute | solution.py:470
  23.5 1.3 collective-permute-start
  24.8 0.0 copy-start
  24.8 1.4 collective-permute-start.1
  26.3 1.4 shard_map.88
  27.7 0.0 collective-permute-done.xl_ref
  27.7 2.3 %collective-permute-done.1.xh_ref = f32[1,16,512]{2,1,0:T(8,128)S(1)} collective-permute-done((f32[1,16,512]{2,1,0:T(8,128)S(1)}, f32[1,16,512]{2,1,0:T(8,128)S(1)}, u32[]{:S(2)}, u32[]{:S(2)}) %collective-permute-start.1) | collective-permute-done | bytes 32800 | tf_op jit(solution)/shard_map/ppermute | solution.py:470
  30.0 0.0 collective-permute-done.2.yl_ref
  30.0 1.4 collective-permute-done.3.yh_ref
  31.4 3.2 %shard_map.90 = (f32[32,16,512]{2,1,0:T(8,128)}, f32[32,9,8,128]{3,2,1,0:T(8,128)}) custom-call(f32[32,16,512]{2,1,0:T(8,128)S(1)} %get-tuple-element.17.q_ref, f32[2,8,128]{2,1,0:T(8,128)S(1)} %get-tuple-element.18.sums_ref, f32[32,16,512]{2,1,0:T(8,128)S(1)} %copy-done.1, s32[32,16,512]{2,1,0:T(8,128)S(1)} %copy-done.4, ...), custom_call_target="tpu_custom_call" | custom-call | tf_op jit(solution)/shard_map/pallas_call | solution.py:478
  34.6 0.2 all-to-all-done.recv_ref
  34.8 7.2 %all-to-all-start.1 = ((f32[32,9,8,128]{3,2,1,0:T(8,128)}), f32[32,9,8,128]{3,2,1,0:T(8,128)}, u32[]{:S(2)}, u32[]{:S(2)}) async-start(f32[32,9,8,128]{3,2,1,0:T(8,128)} %get-tuple-element.23), calls=%async_computation.1 | async-start | bytes 2359296 | tf_op jit(solution)/shard_map/all_to_all | solution.py:443
  42.1 5.5 %shard_map.87 = (f32[32,16,512]{2,1,0:T(8,128)}, f32[16,8,1,128]{3,2,1,0:T(1,128)S(1)}) custom-call(f32[32,8,8,128]{3,2,1,0:T(8,128)} %all-to-all-done.recv_ref, f32[512,512]{1,0:T(8,128)S(1)} %copy-done, f32[512]{0:T(512)S(1)} %copy-done.7, f32[1,512]{1,0:T(1,128)S(1)} %copy-done.8), custom_call_target="tpu_custom_call" | custom-call | tf_op jit(solution)/shard_map/pallas_call | solution.py:486
  47.6 12.8 %all-to-all-done.1.recv_hbm = f32[32,9,8,128]{3,2,1,0:T(8,128)} async-done(((f32[32,9,8,128]{3,2,1,0:T(8,128)}), f32[32,9,8,128]{3,2,1,0:T(8,128)}, u32[]{:S(2)}, u32[]{:S(2)}) %all-to-all-start.1) | async-done | bytes 1179680 | tf_op jit(solution)/shard_map/all_to_all | solution.py:443
  60.5 5.9 %shard_map.91 = (f32[32,16,512]{2,1,0:T(8,128)S(1)}, f32[16,17,1,128]{3,2,1,0:T(1,128)S(1)}) custom-call(f32[32,9,8,128]{3,2,1,0:T(8,128)} %all-to-all-done.1.recv_hbm, f32[32,16,512]{2,1,0:T(8,128)} %get-tuple-element.16.fr_hbm.fr_ref, f32[16,8,1,128]{3,2,1,0:T(1,128)S(1)} %get-tuple-element.24.states_ref, f32[512,512]{1,0:T(8,128)S(1)} %copy-done, ...), custom_call_target="tpu_custom_call" | custom-call | tf_op jit(solution)/shard_map/pallas_call | solution.py:492
  66.4 26.3 %all_to_all.25.recv_ref = f32[16,17,1,128]{3,2,1,0:T(1,128)S(1)} all-to-all(f32[16,17,1,128]{3,2,1,0:T(1,128)S(1)} %get-tuple-element.26), channel_id=1, replica_groups=mesh['grp'=16,'pen'=32] {'grp'}, dimensions={0} | all-to-all | bytes 278528 | tf_op jit(solution)/shard_map/all_to_all | solution.py:443
  92.7 0.9 shard_map.92
  93.6 18.3 %all_to_all.26.recv_ref = f32[16,9,1,128]{3,2,1,0:T(1,128)S(1)} all-to-all(f32[16,9,1,128]{3,2,1,0:T(1,128)S(1)} %get-tuple-element.27), channel_id=1, replica_groups=mesh['grp'=16,'pen'=32] {'grp'}, dimensions={0} | all-to-all | bytes 147456 | tf_op jit(solution)/shard_map/all_to_all | solution.py:443
  111.9 4.6 %shard_map.93 = f32[32,9,8,128]{3,2,1,0:T(8,128)S(1)} custom-call(f32[32,16,512]{2,1,0:T(8,128)S(1)} %copy-done.5, f32[32,16,512]{2,1,0:T(8,128)S(1)} %get-tuple-element.25.fq_ref, f32[16,9,1,128]{3,2,1,0:T(1,128)S(1)} %all_to_all.26.recv_ref, f32[3,8,128]{2,1,0:T(8,128)S(1)} %get-tuple-element.28.control_ref, f32[512,512]{1,0:T(8,128)S(1)} %copy-done, ...), custom_call_target="tpu_custom_call" | custom-call | tf_op jit(solution)/shard_map/pallas_call | solution.py:505
  116.5 0.0 copy-start.6
  116.5 24.5 %all_to_all.27.recv_ref = f32[32,9,8,128]{3,2,1,0:T(8,128)S(1)} all-to-all(f32[32,9,8,128]{3,2,1,0:T(8,128)S(1)} %shard_map.93), channel_id=1, replica_groups=mesh['grp'=16,'pen'=32] {'pen'}, dimensions={0} | all-to-all | bytes 2359296 | tf_op jit(solution)/shard_map/all_to_all | solution.py:443
  141.1 3.4 %shard_map.94 = (f32[32,16,512]{2,1,0:T(8,128)}, f32[32,16,512]{2,1,0:T(8,128)}) custom-call(f32[32,9,8,128]{3,2,1,0:T(8,128)S(1)} %all_to_all.27.recv_ref, f32[32,16,512]{2,1,0:T(8,128)S(1)} %copy-done.2, f32[32,16,512]{2,1,0:T(8,128)S(1)} %copy-done.1, f32[32,16,512]{2,1,0:T(8,128)S(1)} %copy-done.6, f32[3,8,128]{2,1,0:T(8,128)S(1)} %get-tuple-element.28.control_ref, ...), custom_call_target="tpu_custom_call" | custom-call | tf_op jit(solution)/shard_map/pallas_call | solution.py:514
  (12 shorter events, 0.0 us)
Async XLA Ops:
  6.5 11.3 %copy-start.1 = (f32[32,16,512]{2,1,0:T(8,128)S(1)}, f32[32,16,512]{2,1,0:T(8,128)}, u32[]{:S(2)}) copy-start(f32[32,16,512]{2,1,0:T(8,128)} %d_ref.7) | copy-start | bytes 3145732
  6.5 11.3 %copy-start.3 = (s32[32,16,512]{2,1,0:T(8,128)S(1)}, s32[32,16,512]{2,1,0:T(8,128)}, u32[]{:S(2)}) copy-start(s32[32,16,512]{2,1,0:T(8,128)} %m_ref.5) | copy-start | bytes 3145732
  6.5 28.3 %all-to-all-start = ((f32[32,8,8,128]{3,2,1,0:T(8,128)}), f32[32,8,8,128]{3,2,1,0:T(8,128)}, u32[]{:S(2)}, u32[]{:S(2)}) async-start(f32[32,8,8,128]{3,2,1,0:T(8,128)} %shard_map.86), calls=%async_computation | async-start | bytes 2097152 | tf_op jit(solution)/shard_map/all_to_all | solution.py:443
  17.8 8.5 %copy-start.2 = (f32[32,16,512]{2,1,0:T(8,128)S(1)}, f32[32,16,512]{2,1,0:T(8,128)}, u32[]{:S(2)}) copy-start(f32[32,16,512]{2,1,0:T(8,128)} %r_ref.3) | copy-start | bytes 3145732
  17.8 8.5 %copy-start.4 = (s32[32,16,512]{2,1,0:T(8,128)S(1)}, s32[32,16,512]{2,1,0:T(8,128)}, u32[]{:S(2)}) copy-start(s32[32,16,512]{2,1,0:T(8,128)} %m_ref.5) | copy-start | bytes 3145732
  17.9 12.1 %collective-permute-start.2 = (f32[32,512]{1,0:T(8,128)S(1)}, f32[32,512]{1,0:T(8,128)S(1)}, u32[]{:S(2)}, u32[]{:S(2)}) collective-permute-start(f32[32,512]{1,0:T(8,128)S(1)} %get-tuple-element.21), channel_id=1, source_target_pairs={{0,1},{1,2},{2,3},{3,4},{4,5},{5,6},{6,7},{7,8},{8,9},{9,10},{10,1... | collective-permute-start | bytes 196616 | tf_op jit(solution)/shard_map/ppermute | solution.py:467
  21.6 9.8 %collective-permute-start.3 = (f32[32,512]{1,0:T(8,128)S(1)}, f32[32,512]{1,0:T(8,128)S(1)}, u32[]{:S(2)}, u32[]{:S(2)}) collective-permute-start(f32[32,512]{1,0:T(8,128)S(1)} %get-tuple-element.22), channel_id=1, source_target_pairs={{1,0},{2,1},{3,2},{4,3},{5,4},{6,5},{7,6},{8,7},{9,8},{10,9},{11,1... | collective-permute-start | bytes 196616 | tf_op jit(solution)/shard_map/ppermute | solution.py:470
  23.5 4.2 %collective-permute-start = (f32[1,16,512]{2,1,0:T(8,128)S(1)}, f32[1,16,512]{2,1,0:T(8,128)S(1)}, u32[]{:S(2)}, u32[]{:S(2)}) collective-permute-start(f32[1,16,512]{2,1,0:T(8,128)S(1)} %get-tuple-element.19), channel_id=1, source_target_pairs={{0,32},{32,64},{64,96},{96,128},{128,160},{160,192},{192,224},{224... | collective-permute-start | bytes 98312 | tf_op jit(solution)/shard_map/ppermute | solution.py:467
  24.8 6.6 %copy-start = (f32[512,512]{1,0:T(8,128)S(1)}, f32[512,512]{1,0:T(8,128)}, u32[]{:S(2)}) copy-start(f32[512,512]{1,0:T(8,128)} %constant.8.clone.c_hbm.c_ref) | copy-start | bytes 3145732
  24.8 5.2 %collective-permute-start.1 = (f32[1,16,512]{2,1,0:T(8,128)S(1)}, f32[1,16,512]{2,1,0:T(8,128)S(1)}, u32[]{:S(2)}, u32[]{:S(2)}) collective-permute-start(f32[1,16,512]{2,1,0:T(8,128)S(1)} %get-tuple-element.20), channel_id=1, source_target_pairs={{32,0},{64,32},{96,64},{128,96},{160,128},{192,160},{224,192},{256... | collective-permute-start | bytes 98312 | tf_op jit(solution)/shard_map/ppermute | solution.py:470
  34.8 7.2 %copy-start.7 = (f32[512]{0:T(512)S(1)}, f32[512]{0:T(512)}, u32[]{:S(2)}) copy-start(f32[512]{0:T(512)} %constant.9.clone.ez_ref) | copy-start | bytes 6148
  34.8 7.2 %copy-start.8 = (f32[1,512]{1,0:T(1,128)S(1)}, f32[1,512]{1,0:T(1,128)}, u32[]{:S(2)}) copy-start(f32[1,512]{1,0:T(1,128)} %constant.10.clone.ey_ref) | copy-start | bytes 6148
  34.8 25.6 %all-to-all-start.1 = ((f32[32,9,8,128]{3,2,1,0:T(8,128)}), f32[32,9,8,128]{3,2,1,0:T(8,128)}, u32[]{:S(2)}, u32[]{:S(2)}) async-start(f32[32,9,8,128]{3,2,1,0:T(8,128)} %get-tuple-element.23), calls=%async_computation.1 | async-start | bytes 2359296 | tf_op jit(solution)/shard_map/all_to_all | solution.py:443
  60.5 32.2 %copy-start.9 = (f32[8,128]{1,0:T(8,128)S(1)}, f32[8,128]{1,0:T(8,128)}, u32[]{:S(2)}) copy-start(f32[8,128]{1,0:T(8,128)} %constant.11.clone.ey_ref) | copy-start | bytes 12292
  60.5 51.4 %copy-start.5 = (f32[32,16,512]{2,1,0:T(8,128)S(1)}, f32[32,16,512]{2,1,0:T(8,128)}, u32[]{:S(2)}) copy-start(f32[32,16,512]{2,1,0:T(8,128)} %get-tuple-element.16.fr_hbm.fr_ref) | copy-start | bytes 3145732
  116.5 24.6 %copy-start.6 = (f32[32,16,512]{2,1,0:T(8,128)S(1)}, f32[32,16,512]{2,1,0:T(8,128)}, u32[]{:S(2)}) copy-start(f32[32,16,512]{2,1,0:T(8,128)} %get-tuple-element.29.q_ref) | copy-start | bytes 3145732

commit v5 on v4

--- a/solution.py
+++ b/solution.py
@@ -29,17 +29,27 @@
     k = np.arange(N)[:, None]
     n = np.arange(N)[None, :]
     weight = np.where(k == 0, math.sqrt(1.0 / N), math.sqrt(2.0 / N))
-    return (weight * np.cos(math.pi * (k * (2 * n + 1) % (4 * N)) / (2.0 * N))).astype(np.float32)
+    return weight * np.cos(math.pi * (k * (2 * n + 1) % (4 * N)) / (2.0 * N))
 
 
 def eigen_values():
     return (4.0 * np.sin(math.pi * np.arange(N) / (2.0 * N)) ** 2).astype(np.float32)
 
 
-def matmul(a, b, dims):
-    return lax.dot_general(
-        a, b, (dims, ((), ())), precision=lax.Precision.HIGHEST, preferred_element_type=F32
-    )
+def halves(x):
+    high = x.astype(jnp.bfloat16)
+    return high, (x - high.astype(F32)).astype(jnp.bfloat16)
+
+
+def product(a, b, dims):
+    def one(x, y):
+        return lax.dot_general(x, y, (dims, ((), ())), preferred_element_type=F32)
+
+    return one(a[0], b[0]) + (one(a[0], b[1]) + one(a[1], b[0]))
+
+
+def whole(refs):
+    return tuple(ref[...] for ref in refs)
 
 
 def decay(shift):
@@ -91,43 +101,26 @@
         copy.wait()
 
 
-def send_third_modes(field_ref, c_ref, ready, send_ref, send_hbm, sems):
-    copies = []
-    for h in range(2):
-        ready(h)
-        field = field_ref[16 * h : 16 * h + 16].reshape(16 * BY, N)
-        modes = matmul(c_ref[...], field, ((1,), (1,)))
-        for b in range(2):
-            part = modes[:, 128 * b : 128 * b + 128].reshape(PEN, 2, 8, 128)
-            for a in range(2):
-                tile = 4 * a + 2 * h + b
-                send_ref[:, tile] = part[:, a]
+def third_modes(field_ref, c_refs, send_ref):
+    modes = product(whole(c_refs), halves(field_ref[...].reshape(BX * BY, N)), ((1,), (1,)))
+    for b in range(4):
+        part = modes[:, 128 * b : 128 * b + 128].reshape(PEN, 2, 8, 128)
         for a in range(2):
-            tiles = pl.ds(4 * a + 2 * h, 2)
-            copies += start(
-                [pltpu.make_async_copy(send_ref.at[:, tiles], send_hbm.at[:, tiles], sems.at[2 * h + a])]
-            )
-    return copies
-
-
-def residual_kernel(r_hbm, c_hbm, send_hbm, r_ref, c_ref, send_ref, sems):
-    into_c = [
-        pltpu.make_async_copy(c_hbm.at[rows], c_ref.at[rows], sems.at[4 + i])
-        for i, rows in enumerate(pl.ds(128 * i, 128) for i in range(4))
-    ]
-    into_r = [
-        pltpu.make_async_copy(r_hbm.at[part], r_ref.at[part], sems.at[8 + i])
-        for i, part in enumerate(pl.ds(8 * i, 8) for i in range(4))
-    ]
-    for i in (0, 1):
-        start(into_c[2 * i : 2 * i + 2] + into_r[2 * i : 2 * i + 2])
-
-    def ready(h):
-        if h == 0:
-            wait(into_c)
-        wait(into_r[2 * h : 2 * h + 2])
-
-    wait(send_third_modes(r_ref, c_ref, ready, send_ref, send_hbm, sems))
+            send_ref[:, 4 * a + b] = part[:, a]
+
+
+def residual_kernel(r_hbm, ch_hbm, cl_hbm, send_hbm, r_ref, ch_ref, cl_ref, send_ref, sems):
+    wait(
+        start(
+            [
+                pltpu.make_async_copy(r_hbm, r_ref, sems.at[0]),
+                pltpu.make_async_copy(ch_hbm, ch_ref, sems.at[1]),
+                pltpu.make_async_copy(cl_hbm, cl_ref, sems.at[2]),
+            ]
+        )
+    )
+    third_modes(r_ref, (ch_ref, cl_ref), send_ref)
+    wait(start([pltpu.make_async_copy(send_ref, send_hbm, sems.at[3])]))
 
 
 def inner_kernel(r_ref, d_ref, m_ref, q_ref, sums_ref, u_ref):
@@ -160,7 +153,7 @@
 
 
 def operated_kernel(
-    q_ref, sums_ref, d_ref, m_ref, xl_ref, xh_ref, yl_ref, yh_ref, c_ref, out_hbm, send_hbm, out_ref, send_ref, sems
+    q_ref, sums_ref, d_ref, m_ref, xl_ref, xh_ref, yl_ref, yh_ref, ch_ref, cl_ref, out_hbm, send_hbm, out_ref, send_ref, sems
 ):
     row = lax.broadcasted_iota(jnp.int32, (8, N), 0)
 
@@ -183,17 +176,12 @@
     sums = jnp.where(half, fold(curvature, 4), fold(sums_ref[1], 4))
     for j in range(PEN):
         send_ref[j, 8] = sums
-    copies = start(
-        [
-            pltpu.make_async_copy(out_ref, out_hbm, sems.at[4]),
-            pltpu.make_async_copy(send_ref.at[:, pl.ds(8, 1)], send_hbm.at[:, pl.ds(8, 1)], sems.at[5]),
-        ]
-    )
-    copies += send_third_modes(out_ref, c_ref, lambda h: None, send_ref, send_hbm, sems)
-    wait(copies)
-
-
-def second_modes(recv_ref, c_ref, out_ref, y_ref, ready=lambda b: None):
+    copies = start([pltpu.make_async_copy(out_ref, out_hbm, sems.at[0])])
+    third_modes(out_ref, (ch_ref, cl_ref), send_ref)
+    wait(copies + start([pltpu.make_async_copy(send_ref, send_hbm, sems.at[1])]))
+
+
+def second_modes(recv_ref, c_refs, out_ref, y_ref, ready=lambda b: None):
     def part(b, _):
         ready(b)
         for s in range(4):
@@ -204,7 +192,8 @@
         return 0
 
     lax.fori_loop(0, 4, part, 0)
-    out_ref[...] = matmul(y_ref[...].reshape(BX * BK, N), c_ref[...], ((1,), (1,))).reshape(BX, BK, N)
+    field = halves(y_ref[...].reshape(BX * BK, N))
+    out_ref[...] = product(field, whole(c_refs), ((1,), (1,))).reshape(BX, BK, N)
 
 
 def third_eigen(ez_ref, h):
@@ -219,8 +208,10 @@
                 send_ref[8 * h + i, first + 4 * side + b] = x[i : i + 1, 128 * b : 128 * b + 128]
 
 
-def residual_blocks_kernel(recv_ref, c_ref, ez_ref, ey_ref, fr_hbm, states_ref, y_ref, fr_ref, sem):
-    second_modes(recv_ref, c_ref, fr_ref, y_ref)
+def residual_blocks_kernel(
+    recv_ref, ch_ref, cl_ref, ez_ref, ey_ref, fr_hbm, states_ref, y_ref, fr_ref, sem
+):
+    second_modes(recv_ref, (ch_ref, cl_ref), fr_ref, y_ref)
     copies = start([pltpu.make_async_copy(fr_ref, fr_hbm, sem)])
     for h in range(2):
         rows = pl.ds(8 * h, 8)
@@ -238,7 +229,7 @@
 
 
 def operated_blocks_kernel(
-    recv_hbm, fr_hbm, states_ref, c_ref, ez_ref, ey_ref, fq_ref, send_ref, y_ref, recv_ref, fr_ref, sems
+    recv_hbm, fr_hbm, states_ref, ch_ref, cl_ref, ez_ref, ey_ref, fq_ref, send_ref, y_ref, recv_ref, fr_ref, sems
 ):
     def into(b):
         tiles = [b, b + 4]
@@ -255,7 +246,7 @@
             pltpu.make_async_copy(fr_hbm, fr_ref, sems.at[2, 1]),
         ]
     )
-    second_modes(recv_ref, c_ref, fq_ref, y_ref, lambda b: wait(into(b)))
+    second_modes(recv_ref, (ch_ref, cl_ref), fq_ref, y_ref, lambda b: wait(into(b)))
     wait(late)
     dots = [jnp.zeros((8, 128), F32), jnp.zeros((8, 128), F32)]
     for h in range(2):
@@ -346,7 +337,9 @@
     control_ref[2] = rq - step * qq
 
 
-def solve_kernel(fr_ref, fq_ref, recv_ref, control_ref, c_ref, ez_ref, ey_ref, send_ref, f_ref, u_ref, y_ref):
+def solve_kernel(
+    fr_ref, fq_ref, recv_ref, control_ref, ch_ref, cl_ref, ez_ref, ey_ref, send_ref, f_ref, u_ref, y_ref
+):
     step = control_ref[0, 0:1, 0:1]
     ez = jnp.concatenate([third_eigen(ez_ref, h) for h in range(2)], axis=0)
     rho, factor = decay(ABSORPTION / CONDUCT + ez + ey_ref[...])
@@ -375,7 +368,8 @@
 
     lax.fori_loop(0, BX, rise, state(0), unroll=4)
     lax.fori_loop(0, BX, fall, state(1), unroll=4)
-    y_ref[...] = matmul(u_ref[...].reshape(BX * BK, N), c_ref[...], ((1,), (0,))).reshape(BX, BK, N)
+    solved = halves(u_ref[...].reshape(BX * BK, N))
+    y_ref[...] = product(solved, (ch_ref[...], cl_ref[...]), ((1,), (0,))).reshape(BX, BK, N)
 
     def part(b, _):
         for s in range(4):
@@ -399,7 +393,7 @@
 
 
 def finish_kernel(
-    recv_ref, r_ref, d_ref, q_ref, control_ref, c_ref, nr_hbm, nd_hbm, g_ref, nr_ref, nd_ref, sems
+    recv_ref, r_ref, d_ref, q_ref, control_ref, ch_ref, cl_ref, nr_hbm, nd_hbm, g_ref, nr_ref, nd_ref, sems
 ):
     nr_ref[...] = r_ref[...] - control_ref[0, 0:1, 0:1] * q_ref[...]
     copies = start([pltpu.make_async_copy(nr_ref, nr_hbm, sems.at[0])])
@@ -411,13 +405,10 @@
         sums = sums + recv_ref[j, 8]
     conjugacy = jnp.full((8, 128), jnp.sum(sums), F32)
     ratio = (conjugacy / control_ref[1])[0:1, 0:1]
-    for h in range(2):
-        part = pl.ds(16 * h, 16)
-        half = g_ref[:, :, :, 256 * h : 256 * h + 256].reshape(N, 256)
-        smoothed = matmul(half, c_ref[...], ((0,), (0,)))
-        nd_ref[part] = smoothed.reshape(16, BY, N) - ratio * d_ref[part]
-        copies += start([pltpu.make_async_copy(nd_ref.at[part], nd_hbm.at[part], sems.at[1 + h])])
-    wait(copies)
+    modes = halves(g_ref[...].reshape(N, BX * BY))
+    smoothed = product(modes, (ch_ref[...], cl_ref[...]), ((0,), (0,)))
+    nd_ref[...] = smoothed.reshape(BX, BY, N) - ratio * d_ref[...]
+    wait(copies + start([pltpu.make_async_copy(nd_ref, nd_hbm, sems.at[1])]))
 
 
 def shape(*dims):
@@ -444,19 +435,23 @@
 
 
 def on_device(residual, direction, material):
-    matrix = jnp.asarray(dct_matrix())
+    matrix = dct_matrix()
+    high = matrix.astype(jnp.bfloat16)
+    low = (matrix - high.astype(np.float64)).astype(jnp.bfloat16)
+    high, low = jnp.asarray(high), jnp.asarray(low)
     eigen = eigen_values()
     ez = jnp.asarray(eigen)
     ey_row = jnp.asarray(eigen[None, :])
     ey_tile = jnp.asarray(np.concatenate([eigen.reshape(4, 128)] * 2, 0))
     block = shape(BX, BY, N)
+    half = pltpu.VMEM((N, N), jnp.bfloat16)
 
     (send,) = call(
         residual_kernel,
-        [HBM] * 2,
+        [HBM] * 3,
         [pltpu.HBM((PEN, 8, 8, 128), F32)],
-        [(BX, BY, N), (N, N), (PEN, 8, 8, 128), pltpu.SemaphoreType.DMA((12,))],
-    )(in_hbm(residual), in_hbm(matrix))
+        [(BX, BY, N), half, half, (PEN, 8, 8, 128), pltpu.SemaphoreType.DMA((4,))],
+    )(in_hbm(residual), in_hbm(high), in_hbm(low))
     recv_r = exchange(send, "pen")
 
     xlo, xhi, ylo, yhi = call(
@@ -477,24 +472,24 @@
     )(residual, direction, material)
     operated, send = call(
         operated_kernel,
-        [VMEM] * 9,
+        [VMEM] * 10,
         [pltpu.HBM((BX, BY, N), F32), pltpu.HBM((PEN, 9, 8, 128), F32)],
-        [(BX, BY, N), (PEN, 9, 8, 128), pltpu.SemaphoreType.DMA((6,))],
-    )(inner, sums, direction, material, xl, xh, yl, yh, matrix)
+        [(BX, BY, N), (PEN, 9, 8, 128), pltpu.SemaphoreType.DMA((2,))],
+    )(inner, sums, direction, material, xl, xh, yl, yh, high, low)
     recv_q = exchange(send, "pen")
 
     field_r, states = call(
         residual_blocks_kernel,
-        [VMEM, VMEM, SMEM, VMEM],
+        [VMEM, VMEM, VMEM, SMEM, VMEM],
         [pltpu.HBM((BX, BK, N), F32), shape(GRP, 8, 1, 128)],
         [(BX, BK, N), (BX, BK, N), pltpu.SemaphoreType.DMA],
-    )(recv_r, matrix, ez, ey_row)
+    )(recv_r, high, low, ez, ey_row)
     field_q, send = call(
         operated_blocks_kernel,
-        [HBM, HBM, VMEM, VMEM, SMEM, VMEM],
+        [HBM, HBM, VMEM, VMEM, VMEM, SMEM, VMEM],
         [block, shape(GRP, 17, 1, 128)],
         [(BX, BK, N), (PEN, 9, 8, 128), (BX, BK, N), pltpu.SemaphoreType.DMA((3, 4))],
-    )(in_hbm(recv_q), in_hbm(field_r), states, matrix, ez, ey_row)
+    )(in_hbm(recv_q), in_hbm(field_r), states, high, low, ez, ey_row)
 
     recv = exchange(send, "grp")
     send, control = call(
@@ -504,19 +499,19 @@
     recv = exchange(send, "grp")
     (send,) = call(
         solve_kernel,
-        [VMEM] * 5 + [SMEM, VMEM],
+        [VMEM] * 6 + [SMEM, VMEM],
         [shape(PEN, 9, 8, 128)],
         [(BX, BK, N)] * 3,
-    )(field_r, field_q, recv, control, matrix, ez, ey_row)
+    )(field_r, field_q, recv, control, high, low, ez, ey_row)
 
     recv = exchange(send, "pen")
     return tuple(
         call(
             finish_kernel,
-            [VMEM] * 6,
+            [VMEM] * 7,
             [pltpu.HBM((BX, BY, N), F32), pltpu.HBM((BX, BY, N), F32)],
-            [(PEN, 2, 8, BX * BY), (BX, BY, N), (BX, BY, N), pltpu.SemaphoreType.DMA((3,))],
-        )(recv, residual, direction, operated, control, matrix)
+            [(PEN, 2, 8, BX * BY), (BX, BY, N), (BX, BY, N), pltpu.SemaphoreType.DMA((2,))],
+        )(recv, residual, direction, operated, control, high, low)
     )
 
 

time: 145 us -> 139 us (0.959)
  Pallas kernels: 30.8 us -> 24.4 us
  waiting for transfers between devices: 16.8 us -> 18.4 us
    pallas_call x6, Pallas kernels: 28.4 us -> 22 us  [the longest x1 5.08 us: on_device(): call(operated_blocks_kernel, [HBM, HBM, VMEM, VMEM, VMEM, SMEM, VMEM], [b...]
    all_to_all x2, waiting for transfers between devices: 13.1 us -> 14.7 us  [exchange(): return lax.all_to_all(x, axis, 0, 0)]
  transfers between devices with their start and end apart: 6 -> 6, of which waited for: 4 -> 4; matrix products, arithmetic and copies ran while one was open for 0% -> 0% of each run, Pallas kernels for 7% -> 6%
where the time goes in v5:
time: 139 us
  blocking collectives  69.1 us (50%)
  starting transfers between devices  26 us (19%)
  Pallas kernels  24.4 us (18%)
  waiting for transfers between devices  18.4 us (13%)
    all_to_all x3, blocking collectives, exchange(): return lax.all_to_all(x, axis, 0, 0)  69.1 us
    all_to_all x2, starting transfers between devices, exchange(): return lax.all_to_all(x, axis, 0, 0)  17.7 us
    all_to_all x2, waiting for transfers between devices, exchange(): return lax.all_to_all(x, axis, 0, 0)  14.7 us
    pallas_call x1, Pallas kernels, on_device(): call(operated_blocks_kernel, [HBM, HBM, VMEM, VMEM, VMEM, SMEM, VMEM], [b...  5.08 us
    ppermute x2, starting transfers between devices, up(): return lax.ppermute(x, axis, [(i, i + 1) for i in range(count - 1)])  4.97 us
    pallas_call x1, Pallas kernels, on_device(): call(residual_blocks_kernel, [VMEM, VMEM, VMEM, SMEM, VMEM], [pltpu.HBM((...  4.72 us
    pallas_call x1, Pallas kernels, on_device(): call(solve_kernel, [VMEM] * 6 + [SMEM, VMEM], [shape(PEN, 9, 8, 128)], [(...  3.78 us
    ppermute x2, waiting for transfers between devices, down(): return lax.ppermute(x, axis, [(i + 1, i) for i in range(count - 1)])  3.69 us
  transfers between devices with their start and end apart: 6, of which 4 were waited for; matrix products, arithmetic and copies ran while one was open for 0% of the time, Pallas kernels for 6%

profile of v5, /device:TPU:1, one launch (start us, length us, event | category | flops | bytes accessed | tf_op | source)
XLA Modules:
  0.0 138.8 jit_solution(9551985223029792189)
XLA Ops:
  0.6 3.5 %shard_map.95 = f32[32,8,8,128]{3,2,1,0:T(8,128)} custom-call(f32[32,16,512]{2,1,0:T(8,128)} %r_ref.3, bf16[512,512]{1,0:T(8,128)(2,1)} %constant.10.clone.ch_hbm.ch_ref, bf16[512,512]{1,0:T(8,128)(2,1)} %constant.11.clone.cl_hbm.cl_ref), custom_call_target="tpu_custom_call" | custom-call | tf_op jit(solution)/shard_map/pallas_call | solution.py:449
  4.2 0.0 copy-start.2
  4.2 0.0 copy-start.4
  4.2 11.3 %all-to-all-start = ((f32[32,8,8,128]{3,2,1,0:T(8,128)}), f32[32,8,8,128]{3,2,1,0:T(8,128)}, u32[]{:S(2)}, u32[]{:S(2)}) async-start(f32[32,8,8,128]{3,2,1,0:T(8,128)} %shard_map.95), calls=%async_computation | async-start | bytes 2097152 | tf_op jit(solution)/shard_map/all_to_all | solution.py:434
  15.5 0.0 copy-done.2
  15.5 0.0 copy-start.3
  15.5 0.0 copy-start.5
  15.5 0.1 shard_map.98
  15.6 3.7 %collective-permute-start.2 = (f32[32,512]{1,0:T(8,128)S(1)}, f32[32,512]{1,0:T(8,128)S(1)}, u32[]{:S(2)}, u32[]{:S(2)}) collective-permute-start(f32[32,512]{1,0:T(8,128)S(1)} %get-tuple-element.21), channel_id=1, source_target_pairs={{0,1},{1,2},{2,3},{3,4},{4,5},{5,6},{6,7},{7,8},{8,9},{9,10},{10,1... | collective-permute-start | bytes 196616 | tf_op jit(solution)/shard_map/ppermute | solution.py:462
  19.3 1.9 %collective-permute-start.3 = (f32[32,512]{1,0:T(8,128)S(1)}, f32[32,512]{1,0:T(8,128)S(1)}, u32[]{:S(2)}, u32[]{:S(2)}) collective-permute-start(f32[32,512]{1,0:T(8,128)S(1)} %get-tuple-element.22), channel_id=1, source_target_pairs={{1,0},{2,1},{3,2},{4,3},{5,4},{6,5},{7,6},{8,7},{9,8},{10,9},{11,1... | collective-permute-start | bytes 196616 | tf_op jit(solution)/shard_map/ppermute | solution.py:465
  21.2 1.3 collective-permute-start
  22.5 0.0 copy-start
  22.5 0.0 copy-start.1
  22.6 1.4 %collective-permute-start.1 = (f32[1,16,512]{2,1,0:T(8,128)S(1)}, f32[1,16,512]{2,1,0:T(8,128)S(1)}, u32[]{:S(2)}, u32[]{:S(2)}) collective-permute-start(f32[1,16,512]{2,1,0:T(8,128)S(1)} %get-tuple-element.20), channel_id=1, source_target_pairs={{32,0},{64,32},{96,64},{128,96},{160,128},{192,160},{224,192},{256... | collective-permute-start | bytes 98312 | tf_op jit(solution)/shard_map/ppermute | solution.py:465
  24.0 1.4 %shard_map.97 = (f32[32,16,512]{2,1,0:T(8,128)S(1)}, f32[2,8,128]{2,1,0:T(8,128)S(1)}) custom-call(f32[32,16,512]{2,1,0:T(8,128)S(1)} %copy-done.3, f32[32,16,512]{2,1,0:T(8,128)S(1)} %copy-done.2, s32[32,16,512]{2,1,0:T(8,128)S(1)} %copy-done.5), custom_call_target="tpu_custom_call" | custom-call | tf_op jit(solution)/shard_map/pallas_call | solution.py:470
  25.4 0.0 collective-permute-done.xl_ref
  25.4 2.3 %collective-permute-done.1.xh_ref = f32[1,16,512]{2,1,0:T(8,128)S(1)} collective-permute-done((f32[1,16,512]{2,1,0:T(8,128)S(1)}, f32[1,16,512]{2,1,0:T(8,128)S(1)}, u32[]{:S(2)}, u32[]{:S(2)}) %collective-permute-start.1) | collective-permute-done | bytes 32800 | tf_op jit(solution)/shard_map/ppermute | solution.py:465
  27.7 0.0 collective-permute-done.2.yl_ref
  27.7 1.4 collective-permute-done.3.yh_ref
  29.1 2.4 %shard_map.99 = (f32[32,16,512]{2,1,0:T(8,128)}, f32[32,9,8,128]{3,2,1,0:T(8,128)}) custom-call(f32[32,16,512]{2,1,0:T(8,128)S(1)} %get-tuple-element.17.q_ref, f32[2,8,128]{2,1,0:T(8,128)S(1)} %get-tuple-element.18.sums_ref, f32[32,16,512]{2,1,0:T(8,128)S(1)} %copy-done.2, s32[32,16,512]{2,1,0:T(8,128)S(1)} %copy-done.5, ...), custom_call_target="tpu_custom_call" | custom-call | tf_op jit(solution)/shard_map/pallas_call | solution.py:473
  31.5 1.0 all-to-all-done.recv_ref
  32.5 6.4 %all-to-all-start.1 = ((f32[32,9,8,128]{3,2,1,0:T(8,128)}), f32[32,9,8,128]{3,2,1,0:T(8,128)}, u32[]{:S(2)}, u32[]{:S(2)}) async-start(f32[32,9,8,128]{3,2,1,0:T(8,128)} %get-tuple-element.23), calls=%async_computation.1 | async-start | bytes 2359296 | tf_op jit(solution)/shard_map/all_to_all | solution.py:434
  39.0 4.7 %shard_map.96 = (f32[32,16,512]{2,1,0:T(8,128)}, f32[16,8,1,128]{3,2,1,0:T(1,128)S(1)}) custom-call(f32[32,8,8,128]{3,2,1,0:T(8,128)} %all-to-all-done.recv_ref, bf16[512,512]{1,0:T(8,128)(2,1)S(1)} %copy-done, bf16[512,512]{1,0:T(8,128)(2,1)S(1)} %copy-done.1, f32[512]{0:T(512)S(1)} %copy-done.8, f32[1,512]{1,0:T(1,128)S(1)} %copy-done.9), custom_call_target="tpu_custom_call" | custom-call | tf_op jit(solution)/shard_map/pallas_call | solution.py:481
  43.7 13.7 %all-to-all-done.1.recv_hbm = f32[32,9,8,128]{3,2,1,0:T(8,128)} async-done(((f32[32,9,8,128]{3,2,1,0:T(8,128)}), f32[32,9,8,128]{3,2,1,0:T(8,128)}, u32[]{:S(2)}, u32[]{:S(2)}) %all-to-all-start.1) | async-done | bytes 1179680 | tf_op jit(solution)/shard_map/all_to_all | solution.py:434
  57.4 5.1 %shard_map.100 = (f32[32,16,512]{2,1,0:T(8,128)S(1)}, f32[16,17,1,128]{3,2,1,0:T(1,128)S(1)}) custom-call(f32[32,9,8,128]{3,2,1,0:T(8,128)} %all-to-all-done.1.recv_hbm, f32[32,16,512]{2,1,0:T(8,128)} %get-tuple-element.16.fr_hbm.fr_ref, f32[16,8,1,128]{3,2,1,0:T(1,128)S(1)} %get-tuple-element.24.states_ref, bf16[512,512]{1,0:T(8,128)(2,1)S(1)} %copy-done, ...), custom_call_target="tpu_custom_call" | custom-call | tf_op jit(solution)/shard_map/pallas_call | solution.py:487
  62.5 26.3 %all_to_all.25.recv_ref = f32[16,17,1,128]{3,2,1,0:T(1,128)S(1)} all-to-all(f32[16,17,1,128]{3,2,1,0:T(1,128)S(1)} %get-tuple-element.26), channel_id=1, replica_groups=mesh['grp'=16,'pen'=32] {'grp'}, dimensions={0} | all-to-all | bytes 278528 | tf_op jit(solution)/shard_map/all_to_all | solution.py:434
  88.7 0.9 shard_map.101
  89.6 18.3 %all_to_all.26.recv_ref = f32[16,9,1,128]{3,2,1,0:T(1,128)S(1)} all-to-all(f32[16,9,1,128]{3,2,1,0:T(1,128)S(1)} %get-tuple-element.27), channel_id=1, replica_groups=mesh['grp'=16,'pen'=32] {'grp'}, dimensions={0} | all-to-all | bytes 147456 | tf_op jit(solution)/shard_map/all_to_all | solution.py:434
  108.0 3.8 %shard_map.102 = f32[32,9,8,128]{3,2,1,0:T(8,128)S(1)} custom-call(f32[32,16,512]{2,1,0:T(8,128)S(1)} %copy-done.6, f32[32,16,512]{2,1,0:T(8,128)S(1)} %get-tuple-element.25.fq_ref, f32[16,9,1,128]{3,2,1,0:T(1,128)S(1)} %all_to_all.26.recv_ref, f32[3,8,128]{2,1,0:T(8,128)S(1)} %get-tuple-element.28.control_ref, bf16[512,512]{1,0:T(8,128)(2,1)S(1)} %copy-done, ...), custom_call_target="tpu_custom_call" | custom-call | tf_op jit(solution)/shard_map/pallas_call | solution.py:500
  111.8 0.0 copy-start.7
  111.8 24.5 %all_to_all.27.recv_ref = f32[32,9,8,128]{3,2,1,0:T(8,128)S(1)} all-to-all(f32[32,9,8,128]{3,2,1,0:T(8,128)S(1)} %shard_map.102), channel_id=1, replica_groups=mesh['grp'=16,'pen'=32] {'pen'}, dimensions={0} | all-to-all | bytes 2359296 | tf_op jit(solution)/shard_map/all_to_all | solution.py:434
  136.3 2.5 %shard_map.103 = (f32[32,16,512]{2,1,0:T(8,128)}, f32[32,16,512]{2,1,0:T(8,128)}) custom-call(f32[32,9,8,128]{3,2,1,0:T(8,128)S(1)} %all_to_all.27.recv_ref, f32[32,16,512]{2,1,0:T(8,128)S(1)} %copy-done.3, f32[32,16,512]{2,1,0:T(8,128)S(1)} %copy-done.2, f32[32,16,512]{2,1,0:T(8,128)S(1)} %copy-done.7, f32[3,8,128]{2,1,0:T(8,128)S(1)} %get-tuple-element.28.control_ref, ...), custom_call_target="tpu_custom_call" | custom-call | tf_op jit(solution)/shard_map/pallas_call | solution.py:509
  (14 shorter events, 0.0 us)
Async XLA Ops:
  4.2 11.3 %copy-start.2 = (f32[32,16,512]{2,1,0:T(8,128)S(1)}, f32[32,16,512]{2,1,0:T(8,128)}, u32[]{:S(2)}) copy-start(f32[32,16,512]{2,1,0:T(8,128)} %d_ref.7) | copy-start | bytes 3145732
  4.2 11.3 %copy-start.4 = (s32[32,16,512]{2,1,0:T(8,128)S(1)}, s32[32,16,512]{2,1,0:T(8,128)}, u32[]{:S(2)}) copy-start(s32[32,16,512]{2,1,0:T(8,128)} %m_ref.5) | copy-start | bytes 3145732
  4.2 28.3 %all-to-all-start = ((f32[32,8,8,128]{3,2,1,0:T(8,128)}), f32[32,8,8,128]{3,2,1,0:T(8,128)}, u32[]{:S(2)}, u32[]{:S(2)}) async-start(f32[32,8,8,128]{3,2,1,0:T(8,128)} %shard_map.95), calls=%async_computation | async-start | bytes 2097152 | tf_op jit(solution)/shard_map/all_to_all | solution.py:434
  15.5 8.5 %copy-start.3 = (f32[32,16,512]{2,1,0:T(8,128)S(1)}, f32[32,16,512]{2,1,0:T(8,128)}, u32[]{:S(2)}) copy-start(f32[32,16,512]{2,1,0:T(8,128)} %r_ref.3) | copy-start | bytes 3145732
  15.5 8.5 %copy-start.5 = (s32[32,16,512]{2,1,0:T(8,128)S(1)}, s32[32,16,512]{2,1,0:T(8,128)}, u32[]{:S(2)}) copy-start(s32[32,16,512]{2,1,0:T(8,128)} %m_ref.5) | copy-start | bytes 3145732
  15.6 12.1 %collective-permute-start.2 = (f32[32,512]{1,0:T(8,128)S(1)}, f32[32,512]{1,0:T(8,128)S(1)}, u32[]{:S(2)}, u32[]{:S(2)}) collective-permute-start(f32[32,512]{1,0:T(8,128)S(1)} %get-tuple-element.21), channel_id=1, source_target_pairs={{0,1},{1,2},{2,3},{3,4},{4,5},{5,6},{6,7},{7,8},{8,9},{9,10},{10,1... | collective-permute-start | bytes 196616 | tf_op jit(solution)/shard_map/ppermute | solution.py:462
  19.3 9.8 %collective-permute-start.3 = (f32[32,512]{1,0:T(8,128)S(1)}, f32[32,512]{1,0:T(8,128)S(1)}, u32[]{:S(2)}, u32[]{:S(2)}) collective-permute-start(f32[32,512]{1,0:T(8,128)S(1)} %get-tuple-element.22), channel_id=1, source_target_pairs={{1,0},{2,1},{3,2},{4,3},{5,4},{6,5},{7,6},{8,7},{9,8},{10,9},{11,1... | collective-permute-start | bytes 196616 | tf_op jit(solution)/shard_map/ppermute | solution.py:465
  21.2 4.2 %collective-permute-start = (f32[1,16,512]{2,1,0:T(8,128)S(1)}, f32[1,16,512]{2,1,0:T(8,128)S(1)}, u32[]{:S(2)}, u32[]{:S(2)}) collective-permute-start(f32[1,16,512]{2,1,0:T(8,128)S(1)} %get-tuple-element.19), channel_id=1, source_target_pairs={{0,32},{32,64},{64,96},{96,128},{128,160},{160,192},{192,224},{224... | collective-permute-start | bytes 98312 | tf_op jit(solution)/shard_map/ppermute | solution.py:462
  22.5 6.6 %copy-start = (bf16[512,512]{1,0:T(8,128)(2,1)S(1)}, bf16[512,512]{1,0:T(8,128)(2,1)}, u32[]{:S(2)}) copy-start(bf16[512,512]{1,0:T(8,128)(2,1)} %constant.10.clone.ch_hbm.ch_ref) | copy-start | bytes 1572868
  22.5 6.6 %copy-start.1 = (bf16[512,512]{1,0:T(8,128)(2,1)S(1)}, bf16[512,512]{1,0:T(8,128)(2,1)}, u32[]{:S(2)}) copy-start(bf16[512,512]{1,0:T(8,128)(2,1)} %constant.11.clone.cl_hbm.cl_ref) | copy-start | bytes 1572868
  22.6 5.2 %collective-permute-start.1 = (f32[1,16,512]{2,1,0:T(8,128)S(1)}, f32[1,16,512]{2,1,0:T(8,128)S(1)}, u32[]{:S(2)}, u32[]{:S(2)}) collective-permute-start(f32[1,16,512]{2,1,0:T(8,128)S(1)} %get-tuple-element.20), channel_id=1, source_target_pairs={{32,0},{64,32},{96,64},{128,96},{160,128},{192,160},{224,192},{256... | collective-permute-start | bytes 98312 | tf_op jit(solution)/shard_map/ppermute | solution.py:465
  32.5 6.4 %copy-start.8 = (f32[512]{0:T(512)S(1)}, f32[512]{0:T(512)}, u32[]{:S(2)}) copy-start(f32[512]{0:T(512)} %constant.12.clone.ez_ref) | copy-start | bytes 6148
  32.5 6.4 %copy-start.9 = (f32[1,512]{1,0:T(1,128)S(1)}, f32[1,512]{1,0:T(1,128)}, u32[]{:S(2)}) copy-start(f32[1,512]{1,0:T(1,128)} %constant.13.clone.ey_ref) | copy-start | bytes 6148
  32.5 24.8 %all-to-all-start.1 = ((f32[32,9,8,128]{3,2,1,0:T(8,128)}), f32[32,9,8,128]{3,2,1,0:T(8,128)}, u32[]{:S(2)}, u32[]{:S(2)}) async-start(f32[32,9,8,128]{3,2,1,0:T(8,128)} %get-tuple-element.23), calls=%async_computation.1 | async-start | bytes 2359296 | tf_op jit(solution)/shard_map/all_to_all | solution.py:434
  57.4 31.4 %copy-start.10 = (f32[8,128]{1,0:T(8,128)S(1)}, f32[8,128]{1,0:T(8,128)}, u32[]{:S(2)}) copy-start(f32[8,128]{1,0:T(8,128)} %constant.14.clone.ey_ref) | copy-start | bytes 12292
  57.4 50.6 %copy-start.6 = (f32[32,16,512]{2,1,0:T(8,128)S(1)}, f32[32,16,512]{2,1,0:T(8,128)}, u32[]{:S(2)}) copy-start(f32[32,16,512]{2,1,0:T(8,128)} %get-tuple-element.16.fr_hbm.fr_ref) | copy-start | bytes 3145732
  111.8 24.6 %copy-start.7 = (f32[32,16,512]{2,1,0:T(8,128)S(1)}, f32[32,16,512]{2,1,0:T(8,128)}, u32[]{:S(2)}) copy-start(f32[32,16,512]{2,1,0:T(8,128)} %get-tuple-element.29.q_ref) | copy-start | bytes 3145732

commit v6 on v5

--- a/solution.py
+++ b/solution.py
@@ -57,17 +57,17 @@
     return rho, rho / (CONDUCT * (1.0 - rho * rho))
 
 
+def turn(x, units):
+    return pltpu.roll(x, 16 * units % 128, 1) if units % 8 else x
+
+
 def swap_units(rows):
-    rows = list(rows)
     unit = lax.broadcasted_iota(jnp.int32, rows[0].shape, 1) // 16
-    for d in (4, 2, 1):
-        keep = (unit & d) == 0
-        for i in range(8):
-            if i & d == 0:
-                a, b = rows[i], rows[i + d]
-                rows[i] = jnp.where(keep, a, pltpu.roll(b, 16 * d, 1))
-                rows[i + d] = jnp.where(keep, pltpu.roll(a, 128 - 16 * d, 1), b)
-    return rows
+    rows = [turn(row, i) for i, row in enumerate(rows)]
+    for d in (1, 2, 4):
+        late = (unit & d) != 0
+        rows = [jnp.where(late, rows[(i + d) % 8], rows[i]) for i in range(8)]
+    return [turn(rows[-k % 8], -k) for k in range(8)]
 
 
 def to_tile(x):
@@ -101,12 +101,12 @@
         copy.wait()
 
 
-def third_modes(field_ref, c_refs, send_ref):
+def third_modes(field_ref, c_refs, put):
     modes = product(whole(c_refs), halves(field_ref[...].reshape(BX * BY, N)), ((1,), (1,)))
     for b in range(4):
         part = modes[:, 128 * b : 128 * b + 128].reshape(PEN, 2, 8, 128)
         for a in range(2):
-            send_ref[:, 4 * a + b] = part[:, a]
+            put(4 * a + b, part[:, a])
 
 
 def residual_kernel(r_hbm, ch_hbm, cl_hbm, send_hbm, r_ref, ch_ref, cl_ref, send_ref, sems):
@@ -119,7 +119,11 @@
             ]
         )
     )
-    third_modes(r_ref, (ch_ref, cl_ref), send_ref)
+
+    def put(tile, x):
+        send_ref[:, tile] = x
+
+    third_modes(r_ref, (ch_ref, cl_ref), put)
     wait(start([pltpu.make_async_copy(send_ref, send_hbm, sems.at[3])]))
 
 
@@ -172,21 +176,26 @@
         out_ref[x] = out_ref[x] - add
         total = total + d_ref[x] * add
     curvature = sums_ref[0] - to_tile(total)
-    half = lax.broadcasted_iota(jnp.int32, (8, 128), 0) < 4
-    sums = jnp.where(half, fold(curvature, 4), fold(sums_ref[1], 4))
+    first = lax.broadcasted_iota(jnp.int32, (8, 128), 0) < 2
+    sums = jnp.where(first, fold(fold(curvature, 4), 2), fold(fold(sums_ref[1], 4), 2))
     for j in range(PEN):
-        send_ref[j, 8] = sums
+        send_ref[j, 16] = sums[:4]
     copies = start([pltpu.make_async_copy(out_ref, out_hbm, sems.at[0])])
-    third_modes(out_ref, (ch_ref, cl_ref), send_ref)
+
+    def put(tile, x):
+        send_ref[:, 2 * tile] = x[:, :4]
+        send_ref[:, 2 * tile + 1] = x[:, 4:]
+
+    third_modes(out_ref, (ch_ref, cl_ref), put)
     wait(copies + start([pltpu.make_async_copy(send_ref, send_hbm, sems.at[1])]))
 
 
-def second_modes(recv_ref, c_refs, out_ref, y_ref, ready=lambda b: None):
+def second_modes(get, c_refs, out_ref, y_ref, ready=lambda b: None):
     def part(b, _):
         ready(b)
         for s in range(4):
             for a in range(2):
-                rows = swap_units([recv_ref[8 * s + i, 4 * a + b] for i in range(8)])
+                rows = swap_units([get(8 * s + i, 4 * a + b) for i in range(8)])
                 for i in range(8):
                     y_ref[8 * b + i, 8 * a : 8 * a + 8, 128 * s : 128 * s + 128] = rows[i]
         return 0
@@ -209,30 +218,39 @@
 
 
 def residual_blocks_kernel(
-    recv_ref, ch_ref, cl_ref, ez_ref, ey_ref, fr_hbm, states_ref, y_ref, fr_ref, sem
+    recv_ref, ch_ref, cl_ref, ez_ref, ey_ref, fr_hbm, zr_hbm, states_ref, table_ref, y_ref, fr_ref, zr_ref, sems
 ):
-    second_modes(recv_ref, (ch_ref, cl_ref), fr_ref, y_ref)
-    copies = start([pltpu.make_async_copy(fr_ref, fr_hbm, sem)])
+    second_modes(lambda j, tile: recv_ref[j, tile], (ch_ref, cl_ref), fr_ref, y_ref)
+    copies = start([pltpu.make_async_copy(fr_ref, fr_hbm, sems.at[0])])
     for h in range(2):
         rows = pl.ds(8 * h, 8)
-        rho, _ = decay(ABSORPTION / CONDUCT + third_eigen(ez_ref, h) + ey_ref[...])
-
-        def sweep(x, carry):
-            power, v, w = carry
-            f = fr_ref[x, rows]
-            return power * rho, f + rho * v, w + power * f
+        rho, factor = decay(ABSORPTION / CONDUCT + third_eigen(ez_ref, h) + ey_ref[...])
+        table_ref[0, rows] = rho
+        table_ref[1, rows] = factor
+
+        def rise(x, v):
+            v = fr_ref[x, rows] + rho * v
+            zr_ref[x, rows] = v
+            return v
+
+        def fall(i, w):
+            x = BX - 1 - i
+            before = rho * w
+            zr_ref[x, rows] = factor * (zr_ref[x, rows] + before)
+            return fr_ref[x, rows] + before
 
         zero = jnp.zeros((8, N), F32)
-        _, v, w = lax.fori_loop(0, BX, sweep, (jnp.ones((8, N), F32), zero, zero), unroll=4)
+        v = lax.fori_loop(0, BX, rise, zero, unroll=4)
+        w = lax.fori_loop(0, BX, fall, zero, unroll=4)
         put_states(v, w, h, states_ref, 0)
-    wait(copies)
+    wait(copies + start([pltpu.make_async_copy(zr_ref, zr_hbm, sems.at[1])]))
 
 
 def operated_blocks_kernel(
-    recv_hbm, fr_hbm, states_ref, ch_ref, cl_ref, ez_ref, ey_ref, fq_ref, send_ref, y_ref, recv_ref, fr_ref, sems
+    recv_hbm, zr_hbm, states_ref, table_ref, ch_ref, cl_ref, fq_ref, send_ref, y_ref, recv_ref, zr_ref, sems
 ):
     def into(b):
-        tiles = [b, b + 4]
+        tiles = [pl.ds(2 * b, 2), pl.ds(2 * b + 8, 2)]
         return [
             pltpu.make_async_copy(recv_hbm.at[:, t], recv_ref.at[:, t], sems.at[i, b])
             for i, t in enumerate(tiles)
@@ -242,43 +260,41 @@
         start(into(b))
     late = start(
         [
-            pltpu.make_async_copy(recv_hbm.at[:, 8], recv_ref.at[:, 8], sems.at[2, 0]),
-            pltpu.make_async_copy(fr_hbm, fr_ref, sems.at[2, 1]),
+            pltpu.make_async_copy(recv_hbm.at[:, 16], recv_ref.at[:, 16], sems.at[2, 0]),
+            pltpu.make_async_copy(zr_hbm, zr_ref, sems.at[2, 1]),
         ]
     )
-    second_modes(recv_ref, (ch_ref, cl_ref), fq_ref, y_ref, lambda b: wait(into(b)))
+
+    def get(j, tile):
+        return jnp.concatenate([recv_ref[j, 2 * tile], recv_ref[j, 2 * tile + 1]], axis=0)
+
+    second_modes(get, (ch_ref, cl_ref), fq_ref, y_ref, lambda b: wait(into(b)))
     wait(late)
     dots = [jnp.zeros((8, 128), F32), jnp.zeros((8, 128), F32)]
     for h in range(2):
         rows = pl.ds(8 * h, 8)
-        rho, factor = decay(ABSORPTION / CONDUCT + third_eigen(ez_ref, h) + ey_ref[...])
+        rho = table_ref[0, rows]
 
         def sweep(x, carry):
-            power, vr, vq, wq, rq, qq = carry
-            r = fr_ref[x, rows]
+            power, vq, wq, rq, qq = carry
             q = fq_ref[x, rows]
-            before_r, before_q = rho * vr, rho * vq
-            vq = q + before_q
-            rq = rq + (before_r * q + vq * r)
-            qq = qq + (vq + before_q) * q
-            return power * rho, r + before_r, vq, wq + power * q, rq, qq
+            before = rho * vq
+            vq = q + before
+            return power * rho, vq, wq + power * q, rq + zr_ref[x, rows] * q, qq + (vq + before) * q
 
         zero = jnp.zeros((8, N), F32)
-        carry = (jnp.ones((8, N), F32),) + (zero,) * 5
-        _, _, vq, wq, rq, qq = lax.fori_loop(0, BX, sweep, carry, unroll=4)
+        carry = (jnp.ones((8, N), F32),) + (zero,) * 4
+        _, vq, wq, rq, qq = lax.fori_loop(0, BX, sweep, carry, unroll=4)
         put_states(vq, wq, h, send_ref, 8)
-        for i, x in enumerate((rq, qq)):
-            x = factor * x
+        for i, x in enumerate((rq, table_ref[1, rows] * qq)):
             dots[i] += x[:, 0:128] + x[:, 128:256] + x[:, 256:384] + x[:, 384:512]
 
-    sums = recv_ref[0, 8]
+    sums = recv_ref[0, 16]
     for j in range(1, PEN):
-        sums = sums + recv_ref[j, 8]
-    row = lax.broadcasted_iota(jnp.int32, (8, 128), 0)
-    four = (jnp.where(row < 4, sums, 0.0), jnp.where(row < 4, 0.0, sums), dots[0], dots[1])
+        sums = sums + recv_ref[j, 16]
     group = lax.broadcasted_iota(jnp.int32, (1, 128), 1) // 32
     packed = jnp.zeros((1, 128), F32)
-    for i, x in enumerate(four):
+    for i, x in enumerate((sums[0:2], sums[2:4], dots[0], dots[1])):
         x = jnp.sum(x, axis=0, keepdims=True)
         x = x + pltpu.roll(x, 64, 1)
         packed = jnp.where(group == i, x + pltpu.roll(x, 32, 1), packed)
@@ -338,11 +354,10 @@
 
 
 def solve_kernel(
-    fr_ref, fq_ref, recv_ref, control_ref, ch_ref, cl_ref, ez_ref, ey_ref, send_ref, f_ref, u_ref, y_ref
+    fr_ref, fq_ref, recv_ref, control_ref, table_ref, ch_ref, cl_ref, send_ref, f_ref, u_ref, y_ref
 ):
     step = control_ref[0, 0:1, 0:1]
-    ez = jnp.concatenate([third_eigen(ez_ref, h) for h in range(2)], axis=0)
-    rho, factor = decay(ABSORPTION / CONDUCT + ez + ey_ref[...])
+    rho, factor = table_ref[0], table_ref[1]
 
     def state(side):
         return jnp.concatenate(
@@ -378,7 +393,9 @@
                     [y_ref[8 * b + i, 8 * a : 8 * a + 8, 128 * s : 128 * s + 128] for i in range(8)]
                 )
                 for i in range(8):
-                    send_ref[8 * s + i, 4 * a + b] = rows[i]
+                    tile = 8 * a + 2 * b
+                    send_ref[8 * s + i, tile] = rows[i][:4]
+                    send_ref[8 * s + i, tile + 1] = rows[i][4:]
         return 0
 
     lax.fori_loop(0, 4, part, 0)
@@ -389,7 +406,7 @@
     first = (row == 0) & (lax.broadcasted_iota(jnp.int32, (8, 128), 1) == 0)
     sums = jnp.where(row == 0, sums, 0.0) + jnp.where(first, control_ref[2], 0.0)
     for j in range(PEN):
-        send_ref[j, 8] = sums
+        send_ref[j, 16] = sums[:4]
 
 
 def finish_kernel(
@@ -399,10 +416,12 @@
     copies = start([pltpu.make_async_copy(nr_ref, nr_hbm, sems.at[0])])
     for b in range(4):
         for a in range(2):
-            g_ref[:, a, :, 128 * b : 128 * b + 128] = recv_ref[:, 4 * a + b]
-    sums = recv_ref[0, 8]
+            for c in range(2):
+                rows = slice(4 * c, 4 * c + 4)
+                g_ref[:, a, rows, 128 * b : 128 * b + 128] = recv_ref[:, 8 * a + 2 * b + c]
+    sums = recv_ref[0, 16]
     for j in range(1, PEN):
-        sums = sums + recv_ref[j, 8]
+        sums = sums + recv_ref[j, 16]
     conjugacy = jnp.full((8, 128), jnp.sum(sums), F32)
     ratio = (conjugacy / control_ref[1])[0:1, 0:1]
     modes = halves(g_ref[...].reshape(N, BX * BY))
@@ -473,23 +492,28 @@
     operated, send = call(
         operated_kernel,
         [VMEM] * 10,
-        [pltpu.HBM((BX, BY, N), F32), pltpu.HBM((PEN, 9, 8, 128), F32)],
-        [(BX, BY, N), (PEN, 9, 8, 128), pltpu.SemaphoreType.DMA((2,))],
+        [pltpu.HBM((BX, BY, N), F32), pltpu.HBM((PEN, 17, 4, 128), F32)],
+        [(BX, BY, N), (PEN, 17, 4, 128), pltpu.SemaphoreType.DMA((2,))],
     )(inner, sums, direction, material, xl, xh, yl, yh, high, low)
     recv_q = exchange(send, "pen")
 
-    field_r, states = call(
+    field_r, inside_r, states, table = call(
         residual_blocks_kernel,
         [VMEM, VMEM, VMEM, SMEM, VMEM],
-        [pltpu.HBM((BX, BK, N), F32), shape(GRP, 8, 1, 128)],
-        [(BX, BK, N), (BX, BK, N), pltpu.SemaphoreType.DMA],
+        [
+            pltpu.HBM((BX, BK, N), F32),
+            pltpu.HBM((BX, BK, N), F32),
+            shape(GRP, 8, 1, 128),
+            shape(2, BK, N),
+        ],
+        [(BX, BK, N)] * 3 + [pltpu.SemaphoreType.DMA((2,))],
     )(recv_r, high, low, ez, ey_row)
     field_q, send = call(
         operated_blocks_kernel,
-        [HBM, HBM, VMEM, VMEM, VMEM, SMEM, VMEM],
+        [HBM, HBM] + [VMEM] * 4,
         [block, shape(GRP, 17, 1, 128)],
-        [(BX, BK, N), (PEN, 9, 8, 128), (BX, BK, N), pltpu.SemaphoreType.DMA((3, 4))],
-    )(in_hbm(recv_q), in_hbm(field_r), states, high, low, ez, ey_row)
+        [(BX, BK, N), (PEN, 17, 4, 128), (BX, BK, N), pltpu.SemaphoreType.DMA((3, 4))],
+    )(in_hbm(recv_q), in_hbm(inside_r), states, table, high, low)
 
     recv = exchange(send, "grp")
     send, control = call(
@@ -499,10 +523,10 @@
     recv = exchange(send, "grp")
     (send,) = call(
         solve_kernel,
-        [VMEM] * 6 + [SMEM, VMEM],
-        [shape(PEN, 9, 8, 128)],
+        [VMEM] * 7,
+        [shape(PEN, 17, 4, 128)],
         [(BX, BK, N)] * 3,
-    )(field_r, field_q, recv, control, high, low, ez, ey_row)
+    )(field_r, field_q, recv, control, table, high, low)
 
     recv = exchange(send, "pen")
     return tuple(

time: 139 us -> 136 us (0.978)
  Pallas kernels: 24.4 us -> 22.1 us
    pallas_call x2, Pallas kernels: 8.86 us -> 6.4 us  [the longest x1 3.74 us: on_device(): call(operated_blocks_kernel, [HBM, HBM] + [VMEM] * 4, [block, shape(GRP,...]
where the time goes in v6:
time: 136 us; the launch traced here: 135 us
  blocking collectives  68.6 us (50%)
  starting transfers between devices  26 us (19%)
  Pallas kernels  22.1 us (16%)
  waiting for transfers between devices  17.6 us (13%)
    all_to_all x3, blocking collectives, exchange(): return lax.all_to_all(x, axis, 0, 0)  68.6 us
    all_to_all x2, starting transfers between devices, exchange(): return lax.all_to_all(x, axis, 0, 0)  17.7 us
    all_to_all x2, waiting for transfers between devices, exchange(): return lax.all_to_all(x, axis, 0, 0)  13.9 us
    ppermute x2, starting transfers between devices, up(): return lax.ppermute(x, axis, [(i, i + 1) for i in range(count - 1)])  4.97 us
    pallas_call x1, Pallas kernels, on_device(): call(residual_blocks_kernel, [VMEM, VMEM, VMEM, SMEM, VMEM], [pltpu.HBM((...  4.8 us
    pallas_call x1, Pallas kernels, on_device(): call(operated_blocks_kernel, [HBM, HBM] + [VMEM] * 4, [block, shape(GRP,...  3.74 us
    ppermute x2, waiting for transfers between devices, down(): return lax.ppermute(x, axis, [(i + 1, i) for i in range(count - 1)])  3.69 us
    pallas_call x1, Pallas kernels, on_device(): call(residual_kernel, [HBM] * 3, [pltpu.HBM((PEN, 8, 8, 128), F32)], [(BX...  3.54 us
  transfers between devices with their start and end apart: 6, of which 4 were waited for; matrix products, arithmetic and copies ran while one was open for 0% of the time, Pallas kernels for 6%

profile of v6, /device:TPU:1, one launch (start us, length us, event | category | flops | bytes accessed | tf_op | source)
XLA Modules:
  0.0 135.3 jit_solution(4864149528030837524)
XLA Ops:
  0.6 3.5 %shard_map.95 = f32[32,8,8,128]{3,2,1,0:T(8,128)} custom-call(f32[32,16,512]{2,1,0:T(8,128)} %r_ref.3, bf16[512,512]{1,0:T(8,128)(2,1)} %constant.10.clone.ch_hbm.ch_ref, bf16[512,512]{1,0:T(8,128)(2,1)} %constant.11.clone.cl_hbm.cl_ref), custom_call_target="tpu_custom_call" | custom-call | tf_op jit(solution)/shard_map/pallas_call | solution.py:468
  4.2 0.0 copy-start.2
  4.2 0.0 copy-start.4
  4.2 11.3 %all-to-all-start = ((f32[32,8,8,128]{3,2,1,0:T(8,128)}), f32[32,8,8,128]{3,2,1,0:T(8,128)}, u32[]{:S(2)}, u32[]{:S(2)}) async-start(f32[32,8,8,128]{3,2,1,0:T(8,128)} %shard_map.95), calls=%async_computation | async-start | bytes 2097152 | tf_op jit(solution)/shard_map/all_to_all | solution.py:453
  15.5 0.0 copy-done.2
  15.5 0.0 copy-done.4
  15.5 0.0 copy-start.3
  15.5 0.0 copy-start.5
  15.5 0.1 shard_map.98
  15.6 3.7 %collective-permute-start.2 = (f32[32,512]{1,0:T(8,128)S(1)}, f32[32,512]{1,0:T(8,128)S(1)}, u32[]{:S(2)}, u32[]{:S(2)}) collective-permute-start(f32[32,512]{1,0:T(8,128)S(1)} %get-tuple-element.23), channel_id=1, source_target_pairs={{0,1},{1,2},{2,3},{3,4},{4,5},{5,6},{6,7},{7,8},{8,9},{9,10},{10,1... | collective-permute-start | bytes 196616 | tf_op jit(solution)/shard_map/ppermute | solution.py:481
  19.3 1.9 %collective-permute-start.3 = (f32[32,512]{1,0:T(8,128)S(1)}, f32[32,512]{1,0:T(8,128)S(1)}, u32[]{:S(2)}, u32[]{:S(2)}) collective-permute-start(f32[32,512]{1,0:T(8,128)S(1)} %get-tuple-element.24), channel_id=1, source_target_pairs={{1,0},{2,1},{3,2},{4,3},{5,4},{6,5},{7,6},{8,7},{9,8},{10,9},{11,1... | collective-permute-start | bytes 196616 | tf_op jit(solution)/shard_map/ppermute | solution.py:484
  21.2 1.3 collective-permute-start
  22.5 0.0 copy-start
  22.6 0.0 copy-start.1
  22.6 1.4 %collective-permute-start.1 = (f32[1,16,512]{2,1,0:T(8,128)S(1)}, f32[1,16,512]{2,1,0:T(8,128)S(1)}, u32[]{:S(2)}, u32[]{:S(2)}) collective-permute-start(f32[1,16,512]{2,1,0:T(8,128)S(1)} %get-tuple-element.22), channel_id=1, source_target_pairs={{32,0},{64,32},{96,64},{128,96},{160,128},{192,160},{224,192},{256... | collective-permute-start | bytes 98312 | tf_op jit(solution)/shard_map/ppermute | solution.py:484
  24.0 1.4 %shard_map.97 = (f32[32,16,512]{2,1,0:T(8,128)S(1)}, f32[2,8,128]{2,1,0:T(8,128)S(1)}) custom-call(f32[32,16,512]{2,1,0:T(8,128)S(1)} %copy-done.3, f32[32,16,512]{2,1,0:T(8,128)S(1)} %copy-done.2, s32[32,16,512]{2,1,0:T(8,128)S(1)} %copy-done.5), custom_call_target="tpu_custom_call" | custom-call | tf_op jit(solution)/shard_map/pallas_call | solution.py:489
  25.4 0.0 collective-permute-done.xl_ref
  25.4 2.3 %collective-permute-done.1.xh_ref = f32[1,16,512]{2,1,0:T(8,128)S(1)} collective-permute-done((f32[1,16,512]{2,1,0:T(8,128)S(1)}, f32[1,16,512]{2,1,0:T(8,128)S(1)}, u32[]{:S(2)}, u32[]{:S(2)}) %collective-permute-start.1) | collective-permute-done | bytes 32800 | tf_op jit(solution)/shard_map/ppermute | solution.py:484
  27.8 0.0 collective-permute-done.2.yl_ref
  27.8 1.4 %collective-permute-done.3.yh_ref = f32[32,512]{1,0:T(8,128)S(1)} collective-permute-done((f32[32,512]{1,0:T(8,128)S(1)}, f32[32,512]{1,0:T(8,128)S(1)}, u32[]{:S(2)}, u32[]{:S(2)}) %collective-permute-start.3) | collective-permute-done | bytes 65568 | tf_op jit(solution)/shard_map/ppermute | solution.py:484
  29.1 2.4 %shard_map.99 = (f32[32,16,512]{2,1,0:T(8,128)}, f32[32,17,4,128]{3,2,1,0:T(4,128)}) custom-call(f32[32,16,512]{2,1,0:T(8,128)S(1)} %get-tuple-element.19.q_ref, f32[2,8,128]{2,1,0:T(8,128)S(1)} %get-tuple-element.20.sums_ref, f32[32,16,512]{2,1,0:T(8,128)S(1)} %copy-done.2, s32[32,16,512]{2,1,0:T(8,128)S(1)} %copy-done.5, ...), custom_call_target="tpu_custom_call" | custom-call | tf_op jit(solution)/shard_map/pallas_call | solution.py:492
  31.5 1.0 all-to-all-done.recv_ref
  32.5 6.4 %all-to-all-start.1 = ((f32[32,17,4,128]{3,2,1,0:T(4,128)}), f32[32,17,4,128]{3,2,1,0:T(4,128)}, u32[]{:S(2)}, u32[]{:S(2)}) async-start(f32[32,17,4,128]{3,2,1,0:T(4,128)} %get-tuple-element.25), calls=%async_computation.1 | async-start | bytes 2228224 | tf_op jit(solution)/shard_map/all_to_all | solution.py:453
  39.0 4.8 %shard_map.96 = (f32[32,16,512]{2,1,0:T(8,128)}, f32[32,16,512]{2,1,0:T(8,128)}, f32[16,8,1,128]{3,2,1,0:T(1,128)S(1)}, f32[2,16,512]{2,1,0:T(8,128)S(1)}) custom-call(f32[32,8,8,128]{3,2,1,0:T(8,128)} %all-to-all-done.recv_ref, bf16[512,512]{1,0:T(8,128)(2,1)S(1)} %copy-done.1, bf16[512,512]{1,0:T(8,128)(2,1)S(1)} %copy-done, f32[512]{0:T(512)S(1)} %copy-done.8, ...), custom_call_target="tpu_custom_call" | custom-call | tf_op jit(solution)/shard_map/pallas_call | solution.py:500
  43.8 12.9 %all-to-all-done.1.recv_hbm = f32[32,17,4,128]{3,2,1,0:T(4,128)} async-done(((f32[32,17,4,128]{3,2,1,0:T(4,128)}), f32[32,17,4,128]{3,2,1,0:T(4,128)}, u32[]{:S(2)}, u32[]{:S(2)}) %all-to-all-start.1) | async-done | bytes 1114144 | tf_op jit(solution)/shard_map/all_to_all | solution.py:453
  56.7 3.7 %shard_map.100 = (f32[32,16,512]{2,1,0:T(8,128)S(1)}, f32[16,17,1,128]{3,2,1,0:T(1,128)S(1)}) custom-call(f32[32,17,4,128]{3,2,1,0:T(4,128)} %all-to-all-done.1.recv_hbm, f32[32,16,512]{2,1,0:T(8,128)} %get-tuple-element.26.zr_hbm, f32[16,8,1,128]{3,2,1,0:T(1,128)S(1)} %get-tuple-element.27.states_ref, f32[2,16,512]{2,1,0:T(8,128)S(1)} %get-tuple-element.28.table_ref, ...), custom_call_target="tpu_custom_call" | custom-call | tf_op jit(solution)/shard_map/pallas_call | solution.py:511
  60.4 26.3 %all_to_all.25.recv_ref = f32[16,17,1,128]{3,2,1,0:T(1,128)S(1)} all-to-all(f32[16,17,1,128]{3,2,1,0:T(1,128)S(1)} %get-tuple-element.30), channel_id=1, replica_groups=mesh['grp'=16,'pen'=32] {'grp'}, dimensions={0} | all-to-all | bytes 278528 | tf_op jit(solution)/shard_map/all_to_all | solution.py:453
  86.7 0.9 shard_map.101
  87.6 18.3 %all_to_all.26.recv_ref = f32[16,9,1,128]{3,2,1,0:T(1,128)S(1)} all-to-all(f32[16,9,1,128]{3,2,1,0:T(1,128)S(1)} %get-tuple-element.31), channel_id=1, replica_groups=mesh['grp'=16,'pen'=32] {'grp'}, dimensions={0} | all-to-all | bytes 147456 | tf_op jit(solution)/shard_map/all_to_all | solution.py:453
  105.9 2.7 %shard_map.102 = f32[32,17,4,128]{3,2,1,0:T(4,128)S(1)} custom-call(f32[32,16,512]{2,1,0:T(8,128)S(1)} %copy-done.6, f32[32,16,512]{2,1,0:T(8,128)S(1)} %get-tuple-element.29.fq_ref, f32[16,9,1,128]{3,2,1,0:T(1,128)S(1)} %all_to_all.26.recv_ref, f32[3,8,128]{2,1,0:T(8,128)S(1)} %get-tuple-element.32.control_ref, ...), custom_call_target="tpu_custom_call" | custom-call | tf_op jit(solution)/shard_map/pallas_call | solution.py:524
  108.6 24.1 %all_to_all.27.recv_ref = f32[32,17,4,128]{3,2,1,0:T(4,128)S(1)} all-to-all(f32[32,17,4,128]{3,2,1,0:T(4,128)S(1)} %shard_map.102), channel_id=1, replica_groups=mesh['grp'=16,'pen'=32] {'pen'}, dimensions={0} | all-to-all | bytes 2228224 | tf_op jit(solution)/shard_map/all_to_all | solution.py:453
  132.7 2.6 %shard_map.103 = (f32[32,16,512]{2,1,0:T(8,128)}, f32[32,16,512]{2,1,0:T(8,128)}) custom-call(f32[32,17,4,128]{3,2,1,0:T(4,128)S(1)} %all_to_all.27.recv_ref, f32[32,16,512]{2,1,0:T(8,128)S(1)} %copy-done.3, f32[32,16,512]{2,1,0:T(8,128)S(1)} %copy-done.2, f32[32,16,512]{2,1,0:T(8,128)S(1)} %copy-done.7, f32[3,8,128]{2,1,0:T(8,128)S(1)} %get-tuple-element.32.control_ref, ...), custom_call_target="tpu_custom_call" | custom-call | tf_op jit(solution)/shard_map/pallas_call | solution.py:533
  (14 shorter events, 0.0 us)
Async XLA Ops:
  4.2 11.3 %copy-start.2 = (f32[32,16,512]{2,1,0:T(8,128)S(1)}, f32[32,16,512]{2,1,0:T(8,128)}, u32[]{:S(2)}) copy-start(f32[32,16,512]{2,1,0:T(8,128)} %d_ref.7) | copy-start | bytes 3145732
  4.2 11.3 %copy-start.4 = (s32[32,16,512]{2,1,0:T(8,128)S(1)}, s32[32,16,512]{2,1,0:T(8,128)}, u32[]{:S(2)}) copy-start(s32[32,16,512]{2,1,0:T(8,128)} %m_ref.5) | copy-start | bytes 3145732
  4.2 28.3 %all-to-all-start = ((f32[32,8,8,128]{3,2,1,0:T(8,128)}), f32[32,8,8,128]{3,2,1,0:T(8,128)}, u32[]{:S(2)}, u32[]{:S(2)}) async-start(f32[32,8,8,128]{3,2,1,0:T(8,128)} %shard_map.95), calls=%async_computation | async-start | bytes 2097152 | tf_op jit(solution)/shard_map/all_to_all | solution.py:453
  15.5 8.5 %copy-start.3 = (f32[32,16,512]{2,1,0:T(8,128)S(1)}, f32[32,16,512]{2,1,0:T(8,128)}, u32[]{:S(2)}) copy-start(f32[32,16,512]{2,1,0:T(8,128)} %r_ref.3) | copy-start | bytes 3145732
  15.5 8.5 %copy-start.5 = (s32[32,16,512]{2,1,0:T(8,128)S(1)}, s32[32,16,512]{2,1,0:T(8,128)}, u32[]{:S(2)}) copy-start(s32[32,16,512]{2,1,0:T(8,128)} %m_ref.5) | copy-start | bytes 3145732
  15.6 12.1 %collective-permute-start.2 = (f32[32,512]{1,0:T(8,128)S(1)}, f32[32,512]{1,0:T(8,128)S(1)}, u32[]{:S(2)}, u32[]{:S(2)}) collective-permute-start(f32[32,512]{1,0:T(8,128)S(1)} %get-tuple-element.23), channel_id=1, source_target_pairs={{0,1},{1,2},{2,3},{3,4},{4,5},{5,6},{6,7},{7,8},{8,9},{9,10},{10,1... | collective-permute-start | bytes 196616 | tf_op jit(solution)/shard_map/ppermute | solution.py:481
  19.3 9.8 %collective-permute-start.3 = (f32[32,512]{1,0:T(8,128)S(1)}, f32[32,512]{1,0:T(8,128)S(1)}, u32[]{:S(2)}, u32[]{:S(2)}) collective-permute-start(f32[32,512]{1,0:T(8,128)S(1)} %get-tuple-element.24), channel_id=1, source_target_pairs={{1,0},{2,1},{3,2},{4,3},{5,4},{6,5},{7,6},{8,7},{9,8},{10,9},{11,1... | collective-permute-start | bytes 196616 | tf_op jit(solution)/shard_map/ppermute | solution.py:484
  21.2 4.2 %collective-permute-start = (f32[1,16,512]{2,1,0:T(8,128)S(1)}, f32[1,16,512]{2,1,0:T(8,128)S(1)}, u32[]{:S(2)}, u32[]{:S(2)}) collective-permute-start(f32[1,16,512]{2,1,0:T(8,128)S(1)} %get-tuple-element.21), channel_id=1, source_target_pairs={{0,32},{32,64},{64,96},{96,128},{128,160},{160,192},{192,224},{224... | collective-permute-start | bytes 98312 | tf_op jit(solution)/shard_map/ppermute | solution.py:481
  22.5 6.6 %copy-start = (bf16[512,512]{1,0:T(8,128)(2,1)S(1)}, bf16[512,512]{1,0:T(8,128)(2,1)}, u32[]{:S(2)}) copy-start(bf16[512,512]{1,0:T(8,128)(2,1)} %constant.11.clone.cl_hbm.cl_ref) | copy-start | bytes 1572868
  22.6 6.6 %copy-start.1 = (bf16[512,512]{1,0:T(8,128)(2,1)S(1)}, bf16[512,512]{1,0:T(8,128)(2,1)}, u32[]{:S(2)}) copy-start(bf16[512,512]{1,0:T(8,128)(2,1)} %constant.10.clone.ch_hbm.ch_ref) | copy-start | bytes 1572868
  22.6 5.2 %collective-permute-start.1 = (f32[1,16,512]{2,1,0:T(8,128)S(1)}, f32[1,16,512]{2,1,0:T(8,128)S(1)}, u32[]{:S(2)}, u32[]{:S(2)}) collective-permute-start(f32[1,16,512]{2,1,0:T(8,128)S(1)} %get-tuple-element.22), channel_id=1, source_target_pairs={{32,0},{64,32},{96,64},{128,96},{160,128},{192,160},{224,192},{256... | collective-permute-start | bytes 98312 | tf_op jit(solution)/shard_map/ppermute | solution.py:484
  32.5 6.4 %copy-start.8 = (f32[512]{0:T(512)S(1)}, f32[512]{0:T(512)}, u32[]{:S(2)}) copy-start(f32[512]{0:T(512)} %constant.12.clone.ez_ref) | copy-start | bytes 6148
  32.5 6.4 %copy-start.10 = (f32[1,512]{1,0:T(1,128)S(1)}, f32[1,512]{1,0:T(1,128)}, u32[]{:S(2)}) copy-start(f32[1,512]{1,0:T(1,128)} %constant.13.clone.ey_ref) | copy-start | bytes 6148
  32.5 24.1 %all-to-all-start.1 = ((f32[32,17,4,128]{3,2,1,0:T(4,128)}), f32[32,17,4,128]{3,2,1,0:T(4,128)}, u32[]{:S(2)}, u32[]{:S(2)}) async-start(f32[32,17,4,128]{3,2,1,0:T(4,128)} %get-tuple-element.25), calls=%async_computation.1 | async-start | bytes 2228224 | tf_op jit(solution)/shard_map/all_to_all | solution.py:453
  56.7 30.0 %copy-start.9 = (f32[8,128]{1,0:T(8,128)S(1)}, f32[8,128]{1,0:T(8,128)}, u32[]{:S(2)}) copy-start(f32[8,128]{1,0:T(8,128)} %constant.14.clone.ey_ref) | copy-start | bytes 12292
  56.7 49.2 %copy-start.6 = (f32[32,16,512]{2,1,0:T(8,128)S(1)}, f32[32,16,512]{2,1,0:T(8,128)}, u32[]{:S(2)}) copy-start(f32[32,16,512]{2,1,0:T(8,128)} %get-tuple-element.18.fr_ref) | copy-start | bytes 3145732
  108.6 24.1 %copy-start.7 = (f32[32,16,512]{2,1,0:T(8,128)S(1)}, f32[32,16,512]{2,1,0:T(8,128)}, u32[]{:S(2)}) copy-start(f32[32,16,512]{2,1,0:T(8,128)} %get-tuple-element.33.q_ref) | copy-start | bytes 3145732

commit v7 on v6

--- a/solution.py
+++ b/solution.py
@@ -83,11 +83,17 @@
     return jnp.where(material == 1, jnp.float32(SOLID), jnp.float32(1.0))
 
 
-def faces_kernel(d_ref, m_ref, xlo_ref, xhi_ref, ylo_ref, yhi_ref):
+def even_pen():
+    return lax.rem(lax.axis_index("pen"), 2) == 0
+
+
+def faces_kernel(d_ref, m_ref, xlo_ref, xhi_ref, first_ref, second_ref):
     xlo_ref[0] = stiffness_of(m_ref[0]) * d_ref[0]
     xhi_ref[0] = stiffness_of(m_ref[BX - 1]) * d_ref[BX - 1]
-    ylo_ref[...] = stiffness_of(m_ref[:, 0, :]) * d_ref[:, 0, :]
-    yhi_ref[...] = stiffness_of(m_ref[:, BY - 1, :]) * d_ref[:, BY - 1, :]
+    low = stiffness_of(m_ref[:, 0, :]) * d_ref[:, 0, :]
+    high = stiffness_of(m_ref[:, BY - 1, :]) * d_ref[:, BY - 1, :]
+    first_ref[...] = jnp.where(even_pen(), high, low)
+    second_ref[...] = jnp.where(even_pen(), low, high)
 
 
 def start(copies):
@@ -157,14 +163,16 @@
 
 
 def operated_kernel(
-    q_ref, sums_ref, d_ref, m_ref, xl_ref, xh_ref, yl_ref, yh_ref, ch_ref, cl_ref, out_hbm, send_hbm, out_ref, send_ref, sems
+    q_ref, sums_ref, d_ref, m_ref, xl_ref, xh_ref, ya_ref, yb_ref, ch_ref, cl_ref, out_hbm, send_hbm, out_ref, send_ref, sems
 ):
     row = lax.broadcasted_iota(jnp.int32, (8, N), 0)
 
     def low_high(x, total):
-        for first, edge, side_ref in ((0, 0, yl_ref), (8, 7, yh_ref)):
+        ya, yb = ya_ref[pl.ds(x, 1), :], yb_ref[pl.ds(x, 1), :]
+        low, high = jnp.where(even_pen(), yb, ya), jnp.where(even_pen(), ya, yb)
+        for first, edge, side in ((0, 0, low), (8, 7, high)):
             rows = pl.ds(first, 8)
-            add = stiffness_of(m_ref[x, rows]) * jnp.where(row == edge, side_ref[pl.ds(x, 1), :], 0.0)
+            add = stiffness_of(m_ref[x, rows]) * jnp.where(row == edge, side, 0.0)
             out_ref[x, rows] = q_ref[x, rows] - add
             total = total + d_ref[x, rows] * add
         return total
@@ -473,7 +481,7 @@
     )(in_hbm(residual), in_hbm(high), in_hbm(low))
     recv_r = exchange(send, "pen")
 
-    xlo, xhi, ylo, yhi = call(
+    xlo, xhi, first, second = call(
         faces_kernel, [VMEM] * 2, [shape(1, BY, N), shape(1, BY, N), shape(BX, N), shape(BX, N)]
     )(direction, material)
 
@@ -484,7 +492,8 @@
         return lax.ppermute(x, axis, [(i + 1, i) for i in range(count - 1)])
 
     xl, xh = up(xhi, "grp", GRP), down(xlo, "grp", GRP)
-    yl, yh = up(yhi, "pen", PEN), down(ylo, "pen", PEN)
+    ya = lax.ppermute(first, "pen", [(i, i ^ 1) for i in range(PEN)])
+    yb = lax.ppermute(second, "pen", [(i, i + 1 if i % 2 else i - 1) for i in range(1, PEN - 1)])
 
     inner, sums = call(
         inner_kernel, [VMEM] * 3, [block, shape(2, 8, 128)], [(BX + 2, BY, N)]
@@ -494,7 +503,7 @@
         [VMEM] * 10,
         [pltpu.HBM((BX, BY, N), F32), pltpu.HBM((PEN, 17, 4, 128), F32)],
         [(BX, BY, N), (PEN, 17, 4, 128), pltpu.SemaphoreType.DMA((2,))],
-    )(inner, sums, direction, material, xl, xh, yl, yh, high, low)
+    )(inner, sums, direction, material, xl, xh, ya, yb, high, low)
     recv_q = exchange(send, "pen")
 
     field_r, inside_r, states, table = call(

time: 136 us -> 135 us (level)
    ppermute x0 -> x2, starting transfers between devices: none -> 5.74 us  [the longest x1 3.27 us: on_device(): lax.ppermute(second, 'pen', [(i, i + 1 if i % 2 else i - 1) for i in rang...]
    ppermute x2 -> x1, starting transfers between devices: 4.97 us -> 1.29 us  [up(): return lax.ppermute(x, axis, [(i, i + 1) for i in range(count - 1)])]
    ppermute x2 -> x1, starting transfers between devices: 3.34 us -> 1.42 us  [down(): return lax.ppermute(x, axis, [(i + 1, i) for i in range(count - 1)])]
    ppermute x2 -> x1, waiting for transfers between devices: 3.69 us -> 2.31 us  [down(): return lax.ppermute(x, axis, [(i + 1, i) for i in range(count - 1)])]
  transfers between devices with their start and end apart: 6 -> 6, of which waited for: 4 -> 4; matrix products, arithmetic and copies ran while one was open for 0% -> 0% of each run, Pallas kernels for 6% -> 7%
where the time goes in v7:
time: 135 us; the launch traced here: 134 us
  blocking collectives  67.6 us (50%)
  starting transfers between devices  26.2 us (19%)
  Pallas kernels  22.2 us (16%)
  waiting for transfers between devices  17.4 us (13%)
    all_to_all x3, blocking collectives, exchange(): return lax.all_to_all(x, axis, 0, 0)  67.6 us
    all_to_all x2, starting transfers between devices, exchange(): return lax.all_to_all(x, axis, 0, 0)  17.8 us
    all_to_all x2, waiting for transfers between devices, exchange(): return lax.all_to_all(x, axis, 0, 0)  13.8 us
    pallas_call x1, Pallas kernels, on_device(): call(residual_blocks_kernel, [VMEM, VMEM, VMEM, SMEM, VMEM], [pltpu.HBM((...  4.8 us
    pallas_call x1, Pallas kernels, on_device(): call(operated_blocks_kernel, [HBM, HBM] + [VMEM] * 4, [block, shape(GRP,...  3.74 us
    pallas_call x1, Pallas kernels, on_device(): call(residual_kernel, [HBM] * 3, [pltpu.HBM((PEN, 8, 8, 128), F32)], [(BX...  3.54 us
    ppermute x1, starting transfers between devices, on_device(): lax.ppermute(second, 'pen', [(i, i + 1 if i % 2 else i - 1) for i in rang...  3.27 us
  transfers between devices with their start and end apart: 6, of which 4 were waited for; matrix products, arithmetic and copies ran while one was open for 0% of the time, Pallas kernels for 7%

profile of v7, /device:TPU:1, one launch (start us, length us, event | category | flops | bytes accessed | tf_op | source)
XLA Modules:
  0.0 134.3 jit_solution(6454698583105157962)
XLA Ops:
  0.6 3.5 %shard_map.95 = f32[32,8,8,128]{3,2,1,0:T(8,128)} custom-call(f32[32,16,512]{2,1,0:T(8,128)} %r_ref.3, bf16[512,512]{1,0:T(8,128)(2,1)} %constant.10.clone.ch_hbm.ch_ref, bf16[512,512]{1,0:T(8,128)(2,1)} %constant.11.clone.cl_hbm.cl_ref), custom_call_target="tpu_custom_call" | custom-call | tf_op jit(solution)/shard_map/pallas_call | solution.py:476
  4.2 0.0 copy-start.2
  4.2 0.0 copy-start.4
  4.2 11.3 %all-to-all-start = ((f32[32,8,8,128]{3,2,1,0:T(8,128)}), f32[32,8,8,128]{3,2,1,0:T(8,128)}, u32[]{:S(2)}, u32[]{:S(2)}) async-start(f32[32,8,8,128]{3,2,1,0:T(8,128)} %shard_map.95), calls=%async_computation | async-start | bytes 2097152 | tf_op jit(solution)/shard_map/all_to_all | solution.py:461
  15.5 0.0 copy-done.2
  15.5 0.0 copy-done.4
  15.5 0.0 copy-start.3
  15.5 0.0 copy-start.5
  15.5 0.1 shard_map.98
  15.6 2.5 %collective-permute-start.2 = (f32[32,512]{1,0:T(8,128)S(1)}, f32[32,512]{1,0:T(8,128)S(1)}, u32[]{:S(2)}, u32[]{:S(2)}) collective-permute-start(f32[32,512]{1,0:T(8,128)S(1)} %get-tuple-element.23), channel_id=1, source_target_pairs={{0,1},{1,0},{2,3},{3,2},{4,5},{5,4},{6,7},{7,6},{8,9},{9,8},{10,11... | collective-permute-start | bytes 196616 | tf_op jit(solution)/shard_map/ppermute | solution.py:495
  18.1 3.3 %collective-permute-start.3 = (f32[32,512]{1,0:T(8,128)S(1)}, f32[32,512]{1,0:T(8,128)S(1)}, u32[]{:S(2)}, u32[]{:S(2)}) collective-permute-start(f32[32,512]{1,0:T(8,128)S(1)} %get-tuple-element.24), channel_id=1, source_target_pairs={{1,2},{2,1},{3,4},{4,3},{5,6},{6,5},{7,8},{8,7},{9,10},{10,9},{11,... | collective-permute-start | bytes 196616 | tf_op jit(solution)/shard_map/ppermute | solution.py:496
  21.4 1.3 collective-permute-start
  22.7 0.0 copy-start
  22.7 0.0 copy-start.1
  22.7 1.4 %collective-permute-start.1 = (f32[1,16,512]{2,1,0:T(8,128)S(1)}, f32[1,16,512]{2,1,0:T(8,128)S(1)}, u32[]{:S(2)}, u32[]{:S(2)}) collective-permute-start(f32[1,16,512]{2,1,0:T(8,128)S(1)} %get-tuple-element.22), channel_id=1, source_target_pairs={{32,0},{64,32},{96,64},{128,96},{160,128},{192,160},{224,192},{256... | collective-permute-start | bytes 98312 | tf_op jit(solution)/shard_map/ppermute | solution.py:492
  24.2 1.4 %shard_map.97 = (f32[32,16,512]{2,1,0:T(8,128)S(1)}, f32[2,8,128]{2,1,0:T(8,128)S(1)}) custom-call(f32[32,16,512]{2,1,0:T(8,128)S(1)} %copy-done.3, f32[32,16,512]{2,1,0:T(8,128)S(1)} %copy-done.2, s32[32,16,512]{2,1,0:T(8,128)S(1)} %copy-done.5), custom_call_target="tpu_custom_call" | custom-call | tf_op jit(solution)/shard_map/pallas_call | solution.py:498
  25.6 0.0 collective-permute-done.xl_ref
  25.6 2.3 %collective-permute-done.1.xh_ref = f32[1,16,512]{2,1,0:T(8,128)S(1)} collective-permute-done((f32[1,16,512]{2,1,0:T(8,128)S(1)}, f32[1,16,512]{2,1,0:T(8,128)S(1)}, u32[]{:S(2)}, u32[]{:S(2)}) %collective-permute-start.1) | collective-permute-done | bytes 32800 | tf_op jit(solution)/shard_map/ppermute | solution.py:492
  27.9 0.0 collective-permute-done.2.ya_ref
  27.9 1.2 collective-permute-done.3.yb_ref
  29.1 2.4 %shard_map.99 = (f32[32,16,512]{2,1,0:T(8,128)}, f32[32,17,4,128]{3,2,1,0:T(4,128)}) custom-call(f32[32,16,512]{2,1,0:T(8,128)S(1)} %get-tuple-element.19.q_ref, f32[2,8,128]{2,1,0:T(8,128)S(1)} %get-tuple-element.20.sums_ref, f32[32,16,512]{2,1,0:T(8,128)S(1)} %copy-done.2, s32[32,16,512]{2,1,0:T(8,128)S(1)} %copy-done.5, ...), custom_call_target="tpu_custom_call" | custom-call | tf_op jit(solution)/shard_map/pallas_call | solution.py:501
  31.6 0.9 all-to-all-done.recv_ref
  32.5 6.5 %all-to-all-start.1 = ((f32[32,17,4,128]{3,2,1,0:T(4,128)}), f32[32,17,4,128]{3,2,1,0:T(4,128)}, u32[]{:S(2)}, u32[]{:S(2)}) async-start(f32[32,17,4,128]{3,2,1,0:T(4,128)} %get-tuple-element.25), calls=%async_computation.1 | async-start | bytes 2228224 | tf_op jit(solution)/shard_map/all_to_all | solution.py:461
  39.1 4.8 %shard_map.96 = (f32[32,16,512]{2,1,0:T(8,128)}, f32[32,16,512]{2,1,0:T(8,128)}, f32[16,8,1,128]{3,2,1,0:T(1,128)S(1)}, f32[2,16,512]{2,1,0:T(8,128)S(1)}) custom-call(f32[32,8,8,128]{3,2,1,0:T(8,128)} %all-to-all-done.recv_ref, bf16[512,512]{1,0:T(8,128)(2,1)S(1)} %copy-done.1, bf16[512,512]{1,0:T(8,128)(2,1)S(1)} %copy-done, f32[512]{0:T(512)S(1)} %copy-done.8, ...), custom_call_target="tpu_custom_call" | custom-call | tf_op jit(solution)/shard_map/pallas_call | solution.py:509
  43.9 12.9 %all-to-all-done.1.recv_hbm = f32[32,17,4,128]{3,2,1,0:T(4,128)} async-done(((f32[32,17,4,128]{3,2,1,0:T(4,128)}), f32[32,17,4,128]{3,2,1,0:T(4,128)}, u32[]{:S(2)}, u32[]{:S(2)}) %all-to-all-start.1) | async-done | bytes 1114144 | tf_op jit(solution)/shard_map/all_to_all | solution.py:461
  56.7 3.7 %shard_map.100 = (f32[32,16,512]{2,1,0:T(8,128)S(1)}, f32[16,17,1,128]{3,2,1,0:T(1,128)S(1)}) custom-call(f32[32,17,4,128]{3,2,1,0:T(4,128)} %all-to-all-done.1.recv_hbm, f32[32,16,512]{2,1,0:T(8,128)} %get-tuple-element.26.zr_hbm, f32[16,8,1,128]{3,2,1,0:T(1,128)S(1)} %get-tuple-element.27.states_ref, f32[2,16,512]{2,1,0:T(8,128)S(1)} %get-tuple-element.28.table_ref, ...), custom_call_target="tpu_custom_call" | custom-call | tf_op jit(solution)/shard_map/pallas_call | solution.py:520
  60.5 25.2 %all_to_all.25.recv_ref = f32[16,17,1,128]{3,2,1,0:T(1,128)S(1)} all-to-all(f32[16,17,1,128]{3,2,1,0:T(1,128)S(1)} %get-tuple-element.30), channel_id=1, replica_groups=mesh['grp'=16,'pen'=32] {'grp'}, dimensions={0} | all-to-all | bytes 278528 | tf_op jit(solution)/shard_map/all_to_all | solution.py:461
  85.7 0.9 shard_map.101
  86.6 18.3 %all_to_all.26.recv_ref = f32[16,9,1,128]{3,2,1,0:T(1,128)S(1)} all-to-all(f32[16,9,1,128]{3,2,1,0:T(1,128)S(1)} %get-tuple-element.31), channel_id=1, replica_groups=mesh['grp'=16,'pen'=32] {'grp'}, dimensions={0} | all-to-all | bytes 147456 | tf_op jit(solution)/shard_map/all_to_all | solution.py:461
  104.9 2.7 %shard_map.102 = f32[32,17,4,128]{3,2,1,0:T(4,128)S(1)} custom-call(f32[32,16,512]{2,1,0:T(8,128)S(1)} %copy-done.6, f32[32,16,512]{2,1,0:T(8,128)S(1)} %get-tuple-element.29.fq_ref, f32[16,9,1,128]{3,2,1,0:T(1,128)S(1)} %all_to_all.26.recv_ref, f32[3,8,128]{2,1,0:T(8,128)S(1)} %get-tuple-element.32.control_ref, ...), custom_call_target="tpu_custom_call" | custom-call | tf_op jit(solution)/shard_map/pallas_call | solution.py:533
  107.6 24.0 %all_to_all.27.recv_ref = f32[32,17,4,128]{3,2,1,0:T(4,128)S(1)} all-to-all(f32[32,17,4,128]{3,2,1,0:T(4,128)S(1)} %shard_map.102), channel_id=1, replica_groups=mesh['grp'=16,'pen'=32] {'pen'}, dimensions={0} | all-to-all | bytes 2228224 | tf_op jit(solution)/shard_map/all_to_all | solution.py:461
  131.7 2.6 %shard_map.103 = (f32[32,16,512]{2,1,0:T(8,128)}, f32[32,16,512]{2,1,0:T(8,128)}) custom-call(f32[32,17,4,128]{3,2,1,0:T(4,128)S(1)} %all_to_all.27.recv_ref, f32[32,16,512]{2,1,0:T(8,128)S(1)} %copy-done.3, f32[32,16,512]{2,1,0:T(8,128)S(1)} %copy-done.2, f32[32,16,512]{2,1,0:T(8,128)S(1)} %copy-done.7, f32[3,8,128]{2,1,0:T(8,128)S(1)} %get-tuple-element.32.control_ref, ...), custom_call_target="tpu_custom_call" | custom-call | tf_op jit(solution)/shard_map/pallas_call | solution.py:542
  (14 shorter events, 0.0 us)
Async XLA Ops:
  4.2 11.3 %copy-start.2 = (f32[32,16,512]{2,1,0:T(8,128)S(1)}, f32[32,16,512]{2,1,0:T(8,128)}, u32[]{:S(2)}) copy-start(f32[32,16,512]{2,1,0:T(8,128)} %d_ref.7) | copy-start | bytes 3145732
  4.2 11.3 %copy-start.4 = (s32[32,16,512]{2,1,0:T(8,128)S(1)}, s32[32,16,512]{2,1,0:T(8,128)}, u32[]{:S(2)}) copy-start(s32[32,16,512]{2,1,0:T(8,128)} %m_ref.5) | copy-start | bytes 3145732
  4.2 28.3 %all-to-all-start = ((f32[32,8,8,128]{3,2,1,0:T(8,128)}), f32[32,8,8,128]{3,2,1,0:T(8,128)}, u32[]{:S(2)}, u32[]{:S(2)}) async-start(f32[32,8,8,128]{3,2,1,0:T(8,128)} %shard_map.95), calls=%async_computation | async-start | bytes 2097152 | tf_op jit(solution)/shard_map/all_to_all | solution.py:461
  15.5 8.6 %copy-start.3 = (f32[32,16,512]{2,1,0:T(8,128)S(1)}, f32[32,16,512]{2,1,0:T(8,128)}, u32[]{:S(2)}) copy-start(f32[32,16,512]{2,1,0:T(8,128)} %r_ref.3) | copy-start | bytes 3145732
  15.5 8.6 %copy-start.5 = (s32[32,16,512]{2,1,0:T(8,128)S(1)}, s32[32,16,512]{2,1,0:T(8,128)}, u32[]{:S(2)}) copy-start(s32[32,16,512]{2,1,0:T(8,128)} %m_ref.5) | copy-start | bytes 3145732
  15.6 12.3 %collective-permute-start.2 = (f32[32,512]{1,0:T(8,128)S(1)}, f32[32,512]{1,0:T(8,128)S(1)}, u32[]{:S(2)}, u32[]{:S(2)}) collective-permute-start(f32[32,512]{1,0:T(8,128)S(1)} %get-tuple-element.23), channel_id=1, source_target_pairs={{0,1},{1,0},{2,3},{3,2},{4,5},{5,4},{6,7},{7,6},{8,9},{9,8},{10,11... | collective-permute-start | bytes 196616 | tf_op jit(solution)/shard_map/ppermute | solution.py:495
  18.1 11.0 %collective-permute-start.3 = (f32[32,512]{1,0:T(8,128)S(1)}, f32[32,512]{1,0:T(8,128)S(1)}, u32[]{:S(2)}, u32[]{:S(2)}) collective-permute-start(f32[32,512]{1,0:T(8,128)S(1)} %get-tuple-element.24), channel_id=1, source_target_pairs={{1,2},{2,1},{3,4},{4,3},{5,6},{6,5},{7,8},{8,7},{9,10},{10,9},{11,... | collective-permute-start | bytes 196616 | tf_op jit(solution)/shard_map/ppermute | solution.py:496
  21.4 4.2 %collective-permute-start = (f32[1,16,512]{2,1,0:T(8,128)S(1)}, f32[1,16,512]{2,1,0:T(8,128)S(1)}, u32[]{:S(2)}, u32[]{:S(2)}) collective-permute-start(f32[1,16,512]{2,1,0:T(8,128)S(1)} %get-tuple-element.21), channel_id=1, source_target_pairs={{0,32},{32,64},{64,96},{96,128},{128,160},{160,192},{192,224},{224... | collective-permute-start | bytes 98312 | tf_op jit(solution)/shard_map/ppermute | solution.py:489
  22.7 6.5 %copy-start = (bf16[512,512]{1,0:T(8,128)(2,1)S(1)}, bf16[512,512]{1,0:T(8,128)(2,1)}, u32[]{:S(2)}) copy-start(bf16[512,512]{1,0:T(8,128)(2,1)} %constant.11.clone.cl_hbm.cl_ref) | copy-start | bytes 1572868
  22.7 6.5 %copy-start.1 = (bf16[512,512]{1,0:T(8,128)(2,1)S(1)}, bf16[512,512]{1,0:T(8,128)(2,1)}, u32[]{:S(2)}) copy-start(bf16[512,512]{1,0:T(8,128)(2,1)} %constant.10.clone.ch_hbm.ch_ref) | copy-start | bytes 1572868
  22.7 5.2 %collective-permute-start.1 = (f32[1,16,512]{2,1,0:T(8,128)S(1)}, f32[1,16,512]{2,1,0:T(8,128)S(1)}, u32[]{:S(2)}, u32[]{:S(2)}) collective-permute-start(f32[1,16,512]{2,1,0:T(8,128)S(1)} %get-tuple-element.22), channel_id=1, source_target_pairs={{32,0},{64,32},{96,64},{128,96},{160,128},{192,160},{224,192},{256... | collective-permute-start | bytes 98312 | tf_op jit(solution)/shard_map/ppermute | solution.py:492
  32.5 6.5 %copy-start.8 = (f32[512]{0:T(512)S(1)}, f32[512]{0:T(512)}, u32[]{:S(2)}) copy-start(f32[512]{0:T(512)} %constant.12.clone.ez_ref) | copy-start | bytes 6148
  32.5 6.5 %copy-start.10 = (f32[1,512]{1,0:T(1,128)S(1)}, f32[1,512]{1,0:T(1,128)}, u32[]{:S(2)}) copy-start(f32[1,512]{1,0:T(1,128)} %constant.13.clone.ey_ref) | copy-start | bytes 6148
  32.5 24.2 %all-to-all-start.1 = ((f32[32,17,4,128]{3,2,1,0:T(4,128)}), f32[32,17,4,128]{3,2,1,0:T(4,128)}, u32[]{:S(2)}, u32[]{:S(2)}) async-start(f32[32,17,4,128]{3,2,1,0:T(4,128)} %get-tuple-element.25), calls=%async_computation.1 | async-start | bytes 2228224 | tf_op jit(solution)/shard_map/all_to_all | solution.py:461
  56.7 29.0 %copy-start.9 = (f32[8,128]{1,0:T(8,128)S(1)}, f32[8,128]{1,0:T(8,128)}, u32[]{:S(2)}) copy-start(f32[8,128]{1,0:T(8,128)} %constant.14.clone.ey_ref) | copy-start | bytes 12292
  56.7 48.2 %copy-start.6 = (f32[32,16,512]{2,1,0:T(8,128)S(1)}, f32[32,16,512]{2,1,0:T(8,128)}, u32[]{:S(2)}) copy-start(f32[32,16,512]{2,1,0:T(8,128)} %get-tuple-element.18.fr_ref) | copy-start | bytes 3145732
  107.6 24.1 %copy-start.7 = (f32[32,16,512]{2,1,0:T(8,128)S(1)}, f32[32,16,512]{2,1,0:T(8,128)}, u32[]{:S(2)}) copy-start(f32[32,16,512]{2,1,0:T(8,128)} %get-tuple-element.33.q_ref) | copy-start | bytes 3145732

commit v8 on v7

--- a/solution.py
+++ b/solution.py
@@ -163,7 +163,7 @@
 
 
 def operated_kernel(
-    q_ref, sums_ref, d_ref, m_ref, xl_ref, xh_ref, ya_ref, yb_ref, ch_ref, cl_ref, out_hbm, send_hbm, out_ref, send_ref, sems
+    q_ref, sums_ref, d_ref, m_ref, yb_ref, xl_ref, xh_ref, ya_ref, ch_ref, cl_ref, out_hbm, send_hbm, out_ref, send_ref, sems
 ):
     row = lax.broadcasted_iota(jnp.int32, (8, N), 0)
 
@@ -491,10 +491,9 @@
     def down(x, axis, count):
         return lax.ppermute(x, axis, [(i + 1, i) for i in range(count - 1)])
 
+    yb = lax.ppermute(second, "pen", [(i, i + 1 if i % 2 else i - 1) for i in range(1, PEN - 1)])
     xl, xh = up(xhi, "grp", GRP), down(xlo, "grp", GRP)
     ya = lax.ppermute(first, "pen", [(i, i ^ 1) for i in range(PEN)])
-    yb = lax.ppermute(second, "pen", [(i, i + 1 if i % 2 else i - 1) for i in range(1, PEN - 1)])
-
     inner, sums = call(
         inner_kernel, [VMEM] * 3, [block, shape(2, 8, 128)], [(BX + 2, BY, N)]
     )(residual, direction, material)
@@ -503,7 +502,7 @@
         [VMEM] * 10,
         [pltpu.HBM((BX, BY, N), F32), pltpu.HBM((PEN, 17, 4, 128), F32)],
         [(BX, BY, N), (PEN, 17, 4, 128), pltpu.SemaphoreType.DMA((2,))],
-    )(inner, sums, direction, material, xl, xh, ya, yb, high, low)
+    )(inner, sums, direction, material, yb, xl, xh, ya, high, low)
     recv_q = exchange(send, "pen")
 
     field_r, inside_r, states, table = call(

time: 135 us -> 136 us (level)
  transfers between devices with their start and end apart: 6 -> 6, of which waited for: 4 -> 4; matrix products, arithmetic and copies ran while one was open for 0% -> 0% of each run, Pallas kernels for 7% -> 6%
where the time goes in v8:
time: 136 us; the launch traced here: 135 us
  blocking collectives  68.2 us (50%)
  starting transfers between devices  26.1 us (19%)
  Pallas kernels  22.2 us (16%)
  waiting for transfers between devices  17.5 us (13%)
    all_to_all x3, blocking collectives, exchange(): return lax.all_to_all(x, axis, 0, 0)  68.2 us
    all_to_all x2, starting transfers between devices, exchange(): return lax.all_to_all(x, axis, 0, 0)  17.8 us
    all_to_all x2, waiting for transfers between devices, exchange(): return lax.all_to_all(x, axis, 0, 0)  13.8 us
    pallas_call x1, Pallas kernels, on_device(): call(residual_blocks_kernel, [VMEM, VMEM, VMEM, SMEM, VMEM], [pltpu.HBM((...  4.79 us
    pallas_call x1, Pallas kernels, on_device(): call(operated_blocks_kernel, [HBM, HBM] + [VMEM] * 4, [block, shape(GRP,...  3.74 us
    ppermute x1, starting transfers between devices, on_device(): lax.ppermute(second, 'pen', [(i, i + 1 if i % 2 else i - 1) for i in rang...  3.68 us
    pallas_call x1, Pallas kernels, on_device(): call(residual_kernel, [HBM] * 3, [pltpu.HBM((PEN, 8, 8, 128), F32)], [(BX...  3.54 us
  transfers between devices with their start and end apart: 6, of which 4 were waited for; matrix products, arithmetic and copies ran while one was open for 0% of the time, Pallas kernels for 6%

profile of v8, /device:TPU:1, one launch (start us, length us, event | category | flops | bytes accessed | tf_op | source)
XLA Modules:
  0.0 134.9 jit_solution(16307963897906954641)
XLA Ops:
  0.6 3.5 %shard_map.95 = f32[32,8,8,128]{3,2,1,0:T(8,128)} custom-call(f32[32,16,512]{2,1,0:T(8,128)} %r_ref.3, bf16[512,512]{1,0:T(8,128)(2,1)} %constant.10.clone.ch_hbm.ch_ref, bf16[512,512]{1,0:T(8,128)(2,1)} %constant.11.clone.cl_hbm.cl_ref), custom_call_target="tpu_custom_call" | custom-call | tf_op jit(solution)/shard_map/pallas_call | solution.py:476
  4.2 0.0 copy-start.2
  4.2 0.0 copy-start.4
  4.2 11.3 %all-to-all-start = ((f32[32,8,8,128]{3,2,1,0:T(8,128)}), f32[32,8,8,128]{3,2,1,0:T(8,128)}, u32[]{:S(2)}, u32[]{:S(2)}) async-start(f32[32,8,8,128]{3,2,1,0:T(8,128)} %shard_map.95), calls=%async_computation | async-start | bytes 2097152 | tf_op jit(solution)/shard_map/all_to_all | solution.py:461
  15.5 0.0 copy-done.2
  15.5 0.0 copy-done.4
  15.5 0.0 copy-start.3
  15.5 0.0 copy-start.5
  15.5 0.1 shard_map.98
  15.6 3.7 %collective-permute-start = (f32[32,512]{1,0:T(8,128)S(1)}, f32[32,512]{1,0:T(8,128)S(1)}, u32[]{:S(2)}, u32[]{:S(2)}) collective-permute-start(f32[32,512]{1,0:T(8,128)S(1)} %get-tuple-element.21), channel_id=1, source_target_pairs={{1,2},{2,1},{3,4},{4,3},{5,6},{6,5},{7,8},{8,7},{9,10},{10,9},{11,... | collective-permute-start | bytes 196616 | tf_op jit(solution)/shard_map/ppermute | solution.py:494
  19.3 1.9 %collective-permute-start.3 = (f32[32,512]{1,0:T(8,128)S(1)}, f32[32,512]{1,0:T(8,128)S(1)}, u32[]{:S(2)}, u32[]{:S(2)}) collective-permute-start(f32[32,512]{1,0:T(8,128)S(1)} %get-tuple-element.24), channel_id=1, source_target_pairs={{0,1},{1,0},{2,3},{3,2},{4,5},{5,4},{6,7},{7,6},{8,9},{9,8},{10,11... | collective-permute-start | bytes 196616 | tf_op jit(solution)/shard_map/ppermute | solution.py:496
  21.2 1.3 collective-permute-start.1
  22.5 0.0 copy-start
  22.6 0.0 copy-start.1
  22.6 1.4 %collective-permute-start.2 = (f32[1,16,512]{2,1,0:T(8,128)S(1)}, f32[1,16,512]{2,1,0:T(8,128)S(1)}, u32[]{:S(2)}, u32[]{:S(2)}) collective-permute-start(f32[1,16,512]{2,1,0:T(8,128)S(1)} %get-tuple-element.23), channel_id=1, source_target_pairs={{32,0},{64,32},{96,64},{128,96},{160,128},{192,160},{224,192},{256... | collective-permute-start | bytes 98312 | tf_op jit(solution)/shard_map/ppermute | solution.py:492
  24.0 1.4 %shard_map.97 = (f32[32,16,512]{2,1,0:T(8,128)S(1)}, f32[2,8,128]{2,1,0:T(8,128)S(1)}) custom-call(f32[32,16,512]{2,1,0:T(8,128)S(1)} %copy-done.3, f32[32,16,512]{2,1,0:T(8,128)S(1)} %copy-done.2, s32[32,16,512]{2,1,0:T(8,128)S(1)} %copy-done.5), custom_call_target="tpu_custom_call" | custom-call | tf_op jit(solution)/shard_map/pallas_call | solution.py:497
  25.4 0.0 collective-permute-done.1.xl_ref
  25.4 2.3 %collective-permute-done.2.xh_ref = f32[1,16,512]{2,1,0:T(8,128)S(1)} collective-permute-done((f32[1,16,512]{2,1,0:T(8,128)S(1)}, f32[1,16,512]{2,1,0:T(8,128)S(1)}, u32[]{:S(2)}, u32[]{:S(2)}) %collective-permute-start.2) | collective-permute-done | bytes 32800 | tf_op jit(solution)/shard_map/ppermute | solution.py:492
  27.8 1.4 %collective-permute-done.yb_ref = f32[32,512]{1,0:T(8,128)S(1)} collective-permute-done((f32[32,512]{1,0:T(8,128)S(1)}, f32[32,512]{1,0:T(8,128)S(1)}, u32[]{:S(2)}, u32[]{:S(2)}) %collective-permute-start) | collective-permute-done | bytes 65568 | tf_op jit(solution)/shard_map/ppermute | solution.py:494
  29.1 0.0 collective-permute-done.3.ya_ref
  29.2 2.4 %shard_map.99 = (f32[32,16,512]{2,1,0:T(8,128)}, f32[32,17,4,128]{3,2,1,0:T(4,128)}) custom-call(f32[32,16,512]{2,1,0:T(8,128)S(1)} %get-tuple-element.19.q_ref, f32[2,8,128]{2,1,0:T(8,128)S(1)} %get-tuple-element.20.sums_ref, f32[32,16,512]{2,1,0:T(8,128)S(1)} %copy-done.2, s32[32,16,512]{2,1,0:T(8,128)S(1)} %copy-done.5, ...), custom_call_target="tpu_custom_call" | custom-call | tf_op jit(solution)/shard_map/pallas_call | solution.py:500
  31.6 0.9 all-to-all-done.recv_ref
  32.5 6.5 %all-to-all-start.1 = ((f32[32,17,4,128]{3,2,1,0:T(4,128)}), f32[32,17,4,128]{3,2,1,0:T(4,128)}, u32[]{:S(2)}, u32[]{:S(2)}) async-start(f32[32,17,4,128]{3,2,1,0:T(4,128)} %get-tuple-element.25), calls=%async_computation.1 | async-start | bytes 2228224 | tf_op jit(solution)/shard_map/all_to_all | solution.py:461
  39.1 4.8 %shard_map.96 = (f32[32,16,512]{2,1,0:T(8,128)}, f32[32,16,512]{2,1,0:T(8,128)}, f32[16,8,1,128]{3,2,1,0:T(1,128)S(1)}, f32[2,16,512]{2,1,0:T(8,128)S(1)}) custom-call(f32[32,8,8,128]{3,2,1,0:T(8,128)} %all-to-all-done.recv_ref, bf16[512,512]{1,0:T(8,128)(2,1)S(1)} %copy-done.1, bf16[512,512]{1,0:T(8,128)(2,1)S(1)} %copy-done, f32[512]{0:T(512)S(1)} %copy-done.8, ...), custom_call_target="tpu_custom_call" | custom-call | tf_op jit(solution)/shard_map/pallas_call | solution.py:508
  43.9 12.9 %all-to-all-done.1.recv_hbm = f32[32,17,4,128]{3,2,1,0:T(4,128)} async-done(((f32[32,17,4,128]{3,2,1,0:T(4,128)}), f32[32,17,4,128]{3,2,1,0:T(4,128)}, u32[]{:S(2)}, u32[]{:S(2)}) %all-to-all-start.1) | async-done | bytes 1114144 | tf_op jit(solution)/shard_map/all_to_all | solution.py:461
  56.8 3.7 %shard_map.100 = (f32[32,16,512]{2,1,0:T(8,128)S(1)}, f32[16,17,1,128]{3,2,1,0:T(1,128)S(1)}) custom-call(f32[32,17,4,128]{3,2,1,0:T(4,128)} %all-to-all-done.1.recv_hbm, f32[32,16,512]{2,1,0:T(8,128)} %get-tuple-element.26.zr_hbm, f32[16,8,1,128]{3,2,1,0:T(1,128)S(1)} %get-tuple-element.27.states_ref, f32[2,16,512]{2,1,0:T(8,128)S(1)} %get-tuple-element.28.table_ref, ...), custom_call_target="tpu_custom_call" | custom-call | tf_op jit(solution)/shard_map/pallas_call | solution.py:519
  60.5 25.8 %all_to_all.25.recv_ref = f32[16,17,1,128]{3,2,1,0:T(1,128)S(1)} all-to-all(f32[16,17,1,128]{3,2,1,0:T(1,128)S(1)} %get-tuple-element.30), channel_id=1, replica_groups=mesh['grp'=16,'pen'=32] {'grp'}, dimensions={0} | all-to-all | bytes 278528 | tf_op jit(solution)/shard_map/all_to_all | solution.py:461
  86.3 0.9 shard_map.101
  87.2 18.3 %all_to_all.26.recv_ref = f32[16,9,1,128]{3,2,1,0:T(1,128)S(1)} all-to-all(f32[16,9,1,128]{3,2,1,0:T(1,128)S(1)} %get-tuple-element.31), channel_id=1, replica_groups=mesh['grp'=16,'pen'=32] {'grp'}, dimensions={0} | all-to-all | bytes 147456 | tf_op jit(solution)/shard_map/all_to_all | solution.py:461
  105.6 2.7 %shard_map.102 = f32[32,17,4,128]{3,2,1,0:T(4,128)S(1)} custom-call(f32[32,16,512]{2,1,0:T(8,128)S(1)} %copy-done.6, f32[32,16,512]{2,1,0:T(8,128)S(1)} %get-tuple-element.29.fq_ref, f32[16,9,1,128]{3,2,1,0:T(1,128)S(1)} %all_to_all.26.recv_ref, f32[3,8,128]{2,1,0:T(8,128)S(1)} %get-tuple-element.32.control_ref, ...), custom_call_target="tpu_custom_call" | custom-call | tf_op jit(solution)/shard_map/pallas_call | solution.py:532
  108.2 24.0 %all_to_all.27.recv_ref = f32[32,17,4,128]{3,2,1,0:T(4,128)S(1)} all-to-all(f32[32,17,4,128]{3,2,1,0:T(4,128)S(1)} %shard_map.102), channel_id=1, replica_groups=mesh['grp'=16,'pen'=32] {'pen'}, dimensions={0} | all-to-all | bytes 2228224 | tf_op jit(solution)/shard_map/all_to_all | solution.py:461
  132.3 2.6 %shard_map.103 = (f32[32,16,512]{2,1,0:T(8,128)}, f32[32,16,512]{2,1,0:T(8,128)}) custom-call(f32[32,17,4,128]{3,2,1,0:T(4,128)S(1)} %all_to_all.27.recv_ref, f32[32,16,512]{2,1,0:T(8,128)S(1)} %copy-done.3, f32[32,16,512]{2,1,0:T(8,128)S(1)} %copy-done.2, f32[32,16,512]{2,1,0:T(8,128)S(1)} %copy-done.7, f32[3,8,128]{2,1,0:T(8,128)S(1)} %get-tuple-element.32.control_ref, ...), custom_call_target="tpu_custom_call" | custom-call | tf_op jit(solution)/shard_map/pallas_call | solution.py:541
  (14 shorter events, 0.0 us)
Async XLA Ops:
  4.2 11.3 %copy-start.2 = (f32[32,16,512]{2,1,0:T(8,128)S(1)}, f32[32,16,512]{2,1,0:T(8,128)}, u32[]{:S(2)}) copy-start(f32[32,16,512]{2,1,0:T(8,128)} %d_ref.7) | copy-start | bytes 3145732
  4.2 11.3 %copy-start.4 = (s32[32,16,512]{2,1,0:T(8,128)S(1)}, s32[32,16,512]{2,1,0:T(8,128)}, u32[]{:S(2)}) copy-start(s32[32,16,512]{2,1,0:T(8,128)} %m_ref.5) | copy-start | bytes 3145732
  4.2 28.3 %all-to-all-start = ((f32[32,8,8,128]{3,2,1,0:T(8,128)}), f32[32,8,8,128]{3,2,1,0:T(8,128)}, u32[]{:S(2)}, u32[]{:S(2)}) async-start(f32[32,8,8,128]{3,2,1,0:T(8,128)} %shard_map.95), calls=%async_computation | async-start | bytes 2097152 | tf_op jit(solution)/shard_map/all_to_all | solution.py:461
  15.5 8.5 %copy-start.3 = (f32[32,16,512]{2,1,0:T(8,128)S(1)}, f32[32,16,512]{2,1,0:T(8,128)}, u32[]{:S(2)}) copy-start(f32[32,16,512]{2,1,0:T(8,128)} %r_ref.3) | copy-start | bytes 3145732
  15.5 8.5 %copy-start.5 = (s32[32,16,512]{2,1,0:T(8,128)S(1)}, s32[32,16,512]{2,1,0:T(8,128)}, u32[]{:S(2)}) copy-start(s32[32,16,512]{2,1,0:T(8,128)} %m_ref.5) | copy-start | bytes 3145732
  15.6 13.5 %collective-permute-start = (f32[32,512]{1,0:T(8,128)S(1)}, f32[32,512]{1,0:T(8,128)S(1)}, u32[]{:S(2)}, u32[]{:S(2)}) collective-permute-start(f32[32,512]{1,0:T(8,128)S(1)} %get-tuple-element.21), channel_id=1, source_target_pairs={{1,2},{2,1},{3,4},{4,3},{5,6},{6,5},{7,8},{8,7},{9,10},{10,9},{11,... | collective-permute-start | bytes 196616 | tf_op jit(solution)/shard_map/ppermute | solution.py:494
  19.3 9.8 %collective-permute-start.3 = (f32[32,512]{1,0:T(8,128)S(1)}, f32[32,512]{1,0:T(8,128)S(1)}, u32[]{:S(2)}, u32[]{:S(2)}) collective-permute-start(f32[32,512]{1,0:T(8,128)S(1)} %get-tuple-element.24), channel_id=1, source_target_pairs={{0,1},{1,0},{2,3},{3,2},{4,5},{5,4},{6,7},{7,6},{8,9},{9,8},{10,11... | collective-permute-start | bytes 196616 | tf_op jit(solution)/shard_map/ppermute | solution.py:496
  21.2 4.2 %collective-permute-start.1 = (f32[1,16,512]{2,1,0:T(8,128)S(1)}, f32[1,16,512]{2,1,0:T(8,128)S(1)}, u32[]{:S(2)}, u32[]{:S(2)}) collective-permute-start(f32[1,16,512]{2,1,0:T(8,128)S(1)} %get-tuple-element.22), channel_id=1, source_target_pairs={{0,32},{32,64},{64,96},{96,128},{128,160},{160,192},{192,224},{224... | collective-permute-start | bytes 98312 | tf_op jit(solution)/shard_map/ppermute | solution.py:489
  22.5 6.6 %copy-start = (bf16[512,512]{1,0:T(8,128)(2,1)S(1)}, bf16[512,512]{1,0:T(8,128)(2,1)}, u32[]{:S(2)}) copy-start(bf16[512,512]{1,0:T(8,128)(2,1)} %constant.11.clone.cl_hbm.cl_ref) | copy-start | bytes 1572868
  22.6 6.6 %copy-start.1 = (bf16[512,512]{1,0:T(8,128)(2,1)S(1)}, bf16[512,512]{1,0:T(8,128)(2,1)}, u32[]{:S(2)}) copy-start(bf16[512,512]{1,0:T(8,128)(2,1)} %constant.10.clone.ch_hbm.ch_ref) | copy-start | bytes 1572868
  22.6 5.2 %collective-permute-start.2 = (f32[1,16,512]{2,1,0:T(8,128)S(1)}, f32[1,16,512]{2,1,0:T(8,128)S(1)}, u32[]{:S(2)}, u32[]{:S(2)}) collective-permute-start(f32[1,16,512]{2,1,0:T(8,128)S(1)} %get-tuple-element.23), channel_id=1, source_target_pairs={{32,0},{64,32},{96,64},{128,96},{160,128},{192,160},{224,192},{256... | collective-permute-start | bytes 98312 | tf_op jit(solution)/shard_map/ppermute | solution.py:492
  32.5 6.5 %copy-start.8 = (f32[512]{0:T(512)S(1)}, f32[512]{0:T(512)}, u32[]{:S(2)}) copy-start(f32[512]{0:T(512)} %constant.12.clone.ez_ref) | copy-start | bytes 6148
  32.5 6.5 %copy-start.10 = (f32[1,512]{1,0:T(1,128)S(1)}, f32[1,512]{1,0:T(1,128)}, u32[]{:S(2)}) copy-start(f32[1,512]{1,0:T(1,128)} %constant.13.clone.ey_ref) | copy-start | bytes 6148
  32.5 24.2 %all-to-all-start.1 = ((f32[32,17,4,128]{3,2,1,0:T(4,128)}), f32[32,17,4,128]{3,2,1,0:T(4,128)}, u32[]{:S(2)}, u32[]{:S(2)}) async-start(f32[32,17,4,128]{3,2,1,0:T(4,128)} %get-tuple-element.25), calls=%async_computation.1 | async-start | bytes 2228224 | tf_op jit(solution)/shard_map/all_to_all | solution.py:461
  56.7 29.6 %copy-start.9 = (f32[8,128]{1,0:T(8,128)S(1)}, f32[8,128]{1,0:T(8,128)}, u32[]{:S(2)}) copy-start(f32[8,128]{1,0:T(8,128)} %constant.14.clone.ey_ref) | copy-start | bytes 12292
  56.8 48.8 %copy-start.6 = (f32[32,16,512]{2,1,0:T(8,128)S(1)}, f32[32,16,512]{2,1,0:T(8,128)}, u32[]{:S(2)}) copy-start(f32[32,16,512]{2,1,0:T(8,128)} %get-tuple-element.18.fr_ref) | copy-start | bytes 3145732
  108.2 24.1 %copy-start.7 = (f32[32,16,512]{2,1,0:T(8,128)S(1)}, f32[32,16,512]{2,1,0:T(8,128)}, u32[]{:S(2)}) copy-start(f32[32,16,512]{2,1,0:T(8,128)} %get-tuple-element.33.q_ref) | copy-start | bytes 3145732

commit v9 on v8

--- a/solution.py
+++ b/solution.py
@@ -107,30 +107,39 @@
         copy.wait()
 
 
-def third_modes(field_ref, c_refs, put):
-    modes = product(whole(c_refs), halves(field_ref[...].reshape(BX * BY, N)), ((1,), (1,)))
-    for b in range(4):
-        part = modes[:, 128 * b : 128 * b + 128].reshape(PEN, 2, 8, 128)
-        for a in range(2):
-            put(4 * a + b, part[:, a])
+def send_third_modes(field_ref, c_refs, put, send_ref, send_hbm, sems):
+    field = halves(field_ref[...].reshape(BX * BY, N))
+    copies = []
+    for h in range(2):
+        devices = slice(h * PEN // 2, (h + 1) * PEN // 2)
+        rows = slice(h * N // 2, (h + 1) * N // 2)
+        modes = product(tuple(ref[rows] for ref in c_refs), field, ((1,), (1,)))
+        for b in range(4):
+            part = modes[:, 128 * b : 128 * b + 128].reshape(PEN // 2, 2, 8, 128)
+            for a in range(2):
+                put(devices, 4 * a + b, part[:, a])
+        target = pl.ds(h * PEN // 2, PEN // 2)
+        copies += start(
+            [pltpu.make_async_copy(send_ref.at[target], send_hbm.at[target], sems.at[h])]
+        )
+    return copies
 
 
 def residual_kernel(r_hbm, ch_hbm, cl_hbm, send_hbm, r_ref, ch_ref, cl_ref, send_ref, sems):
     wait(
         start(
             [
-                pltpu.make_async_copy(r_hbm, r_ref, sems.at[0]),
-                pltpu.make_async_copy(ch_hbm, ch_ref, sems.at[1]),
-                pltpu.make_async_copy(cl_hbm, cl_ref, sems.at[2]),
+                pltpu.make_async_copy(r_hbm, r_ref, sems.at[2]),
+                pltpu.make_async_copy(ch_hbm, ch_ref, sems.at[3]),
+                pltpu.make_async_copy(cl_hbm, cl_ref, sems.at[4]),
             ]
         )
     )
 
-    def put(tile, x):
-        send_ref[:, tile] = x
-
-    third_modes(r_ref, (ch_ref, cl_ref), put)
-    wait(start([pltpu.make_async_copy(send_ref, send_hbm, sems.at[3])]))
+    def put(devices, tile, x):
+        send_ref[devices, tile] = x
+
+    wait(send_third_modes(r_ref, (ch_ref, cl_ref), put, send_ref, send_hbm, sems))
 
 
 def inner_kernel(r_ref, d_ref, m_ref, q_ref, sums_ref, u_ref):
@@ -188,14 +197,13 @@
     sums = jnp.where(first, fold(fold(curvature, 4), 2), fold(fold(sums_ref[1], 4), 2))
     for j in range(PEN):
         send_ref[j, 16] = sums[:4]
-    copies = start([pltpu.make_async_copy(out_ref, out_hbm, sems.at[0])])
-
-    def put(tile, x):
-        send_ref[:, 2 * tile] = x[:, :4]
-        send_ref[:, 2 * tile + 1] = x[:, 4:]
-
-    third_modes(out_ref, (ch_ref, cl_ref), put)
-    wait(copies + start([pltpu.make_async_copy(send_ref, send_hbm, sems.at[1])]))
+    copies = start([pltpu.make_async_copy(out_ref, out_hbm, sems.at[2])])
+
+    def put(devices, tile, x):
+        send_ref[devices, 2 * tile] = x[:, :4]
+        send_ref[devices, 2 * tile + 1] = x[:, 4:]
+
+    wait(copies + send_third_modes(out_ref, (ch_ref, cl_ref), put, send_ref, send_hbm, sems))
 
 
 def second_modes(get, c_refs, out_ref, y_ref, ready=lambda b: None):
@@ -226,7 +234,21 @@
 
 
 def residual_blocks_kernel(
-    recv_ref, ch_ref, cl_ref, ez_ref, ey_ref, fr_hbm, zr_hbm, states_ref, table_ref, y_ref, fr_ref, zr_ref, sems
+    recv_ref,
+    ch_ref,
+    cl_ref,
+    ez_ref,
+    ey_ref,
+    tile_ref,
+    fr_hbm,
+    zr_hbm,
+    states_ref,
+    table_ref,
+    across_ref,
+    y_ref,
+    fr_ref,
+    zr_ref,
+    sems,
 ):
     second_modes(lambda j, tile: recv_ref[j, tile], (ch_ref, cl_ref), fr_ref, y_ref)
     copies = start([pltpu.make_async_copy(fr_ref, fr_hbm, sems.at[0])])
@@ -251,7 +273,20 @@
         v = lax.fori_loop(0, BX, rise, zero, unroll=4)
         w = lax.fori_loop(0, BX, fall, zero, unroll=4)
         put_states(v, w, h, states_ref, 0)
-    wait(copies + start([pltpu.make_async_copy(zr_ref, zr_hbm, sems.at[1])]))
+    copies += start([pltpu.make_async_copy(zr_ref, zr_hbm, sems.at[1])])
+    ez = ez_ref[lax.axis_index("pen") * BK + lax.axis_index("grp")]
+    rho, factor = decay(ABSORPTION / CONDUCT + ez + tile_ref[...])
+    across = rho
+    for _ in range(5):
+        across = across * across
+    power = jnp.ones((8, 128), F32)
+    for p in range(GRP):
+        across_ref[p] = power
+        power = power * across
+    across_ref[GRP] = power
+    across_ref[GRP + 1] = rho * factor
+    across_ref[GRP + 2] = 1.0 / (1.0 - power * power)
+    wait(copies)
 
 
 def operated_blocks_kernel(
@@ -311,7 +346,7 @@
         send_ref[j, 16] = packed
 
 
-def interface_kernel(recv_ref, ez_ref, ey_ref, send_ref, control_ref):
+def interface_kernel(recv_ref, across_ref, send_ref, control_ref):
     row = lax.broadcasted_iota(jnp.int32, (8, 128), 0)
     group = lax.broadcasted_iota(jnp.int32, (1, 128), 1) // 32
     sums = recv_ref[0, 16]
@@ -323,11 +358,7 @@
 
     curvature, projection, rq, qq = total(0), total(1), total(2), total(3)
     step = projection / curvature
-    ez = ez_ref[lax.axis_index("pen") * BK + lax.axis_index("grp")]
-    rho, factor = decay(ABSORPTION / CONDUCT + ez + ey_ref[...])
-    across = rho
-    for _ in range(5):
-        across = across * across
+    across = across_ref[1]
     others = [recv_ref[p, 8:16].reshape(8, 128) for p in range(GRP)]
     tiles = [recv_ref[p, 0:8].reshape(8, 128) - step * others[p] for p in range(GRP)]
     zero = jnp.zeros((8, 128), F32)
@@ -339,21 +370,17 @@
         falling.append(tiles[p] + across * falling[-1])
     lower = row < 4
     ends = jnp.where(lower, rising[GRP], falling[GRP])
-    powers = [jnp.ones((8, 128), F32)]
-    for p in range(GRP):
-        powers.append(powers[-1] * across)
-    whole = powers[GRP]
-    images = (pltpu.roll(ends, 4, 0) + whole * ends) / (1.0 - whole * whole)
+    images = (pltpu.roll(ends, 4, 0) + across_ref[GRP] * ends) * across_ref[GRP + 2]
     dots = zero
     for p in range(GRP):
         state = jnp.where(
             lower,
-            rising[p] + powers[p] * images,
-            falling[GRP - 1 - p] + powers[GRP - 1 - p] * images,
+            rising[p] + across_ref[p] * images,
+            falling[GRP - 1 - p] + across_ref[GRP - 1 - p] * images,
         )
         send_ref[p, 0:8] = state.reshape(8, 1, 128)
         dots = dots + state * pltpu.roll(others[p], 4, 0)
-    dots = jnp.sum(rho * factor * dots, axis=0, keepdims=True)
+    dots = jnp.sum(across_ref[GRP + 1] * dots, axis=0, keepdims=True)
     for p in range(GRP):
         send_ref[p, 8] = dots
     control_ref[0] = step
@@ -432,10 +459,14 @@
         sums = sums + recv_ref[j, 16]
     conjugacy = jnp.full((8, 128), jnp.sum(sums), F32)
     ratio = (conjugacy / control_ref[1])[0:1, 0:1]
-    modes = halves(g_ref[...].reshape(N, BX * BY))
-    smoothed = product(modes, (ch_ref[...], cl_ref[...]), ((0,), (0,)))
-    nd_ref[...] = smoothed.reshape(BX, BY, N) - ratio * d_ref[...]
-    wait(copies + start([pltpu.make_async_copy(nd_ref, nd_hbm, sems.at[1])]))
+    for h in range(2):
+        part = pl.ds(h * BX // 2, BX // 2)
+        cells = slice(h * BX * BY // 2, (h + 1) * BX * BY // 2)
+        modes = halves(g_ref[:, :, :, cells].reshape(N, BX * BY // 2))
+        smoothed = product(modes, (ch_ref[...], cl_ref[...]), ((0,), (0,)))
+        nd_ref[part] = smoothed.reshape(BX // 2, BY, N) - ratio * d_ref[part]
+        copies += start([pltpu.make_async_copy(nd_ref.at[part], nd_hbm.at[part], sems.at[1 + h])])
+    wait(copies)
 
 
 def shape(*dims):
@@ -477,7 +508,7 @@
         residual_kernel,
         [HBM] * 3,
         [pltpu.HBM((PEN, 8, 8, 128), F32)],
-        [(BX, BY, N), half, half, (PEN, 8, 8, 128), pltpu.SemaphoreType.DMA((4,))],
+        [(BX, BY, N), half, half, (PEN, 8, 8, 128), pltpu.SemaphoreType.DMA((5,))],
     )(in_hbm(residual), in_hbm(high), in_hbm(low))
     recv_r = exchange(send, "pen")
 
@@ -501,21 +532,22 @@
         operated_kernel,
         [VMEM] * 10,
         [pltpu.HBM((BX, BY, N), F32), pltpu.HBM((PEN, 17, 4, 128), F32)],
-        [(BX, BY, N), (PEN, 17, 4, 128), pltpu.SemaphoreType.DMA((2,))],
+        [(BX, BY, N), (PEN, 17, 4, 128), pltpu.SemaphoreType.DMA((3,))],
     )(inner, sums, direction, material, yb, xl, xh, ya, high, low)
     recv_q = exchange(send, "pen")
 
-    field_r, inside_r, states, table = call(
+    field_r, inside_r, states, table, across = call(
         residual_blocks_kernel,
-        [VMEM, VMEM, VMEM, SMEM, VMEM],
+        [VMEM, VMEM, VMEM, SMEM, VMEM, VMEM],
         [
             pltpu.HBM((BX, BK, N), F32),
             pltpu.HBM((BX, BK, N), F32),
             shape(GRP, 8, 1, 128),
             shape(2, BK, N),
+            shape(GRP + 3, 8, 128),
         ],
         [(BX, BK, N)] * 3 + [pltpu.SemaphoreType.DMA((2,))],
-    )(recv_r, high, low, ez, ey_row)
+    )(recv_r, high, low, ez, ey_row, ey_tile)
     field_q, send = call(
         operated_blocks_kernel,
         [HBM, HBM] + [VMEM] * 4,
@@ -525,8 +557,8 @@
 
     recv = exchange(send, "grp")
     send, control = call(
-        interface_kernel, [VMEM, SMEM, VMEM], [shape(GRP, 9, 1, 128), shape(3, 8, 128)]
-    )(recv, ez, ey_tile)
+        interface_kernel, [VMEM, VMEM], [shape(GRP, 9, 1, 128), shape(3, 8, 128)]
+    )(recv, across)
 
     recv = exchange(send, "grp")
     (send,) = call(
@@ -542,7 +574,7 @@
             finish_kernel,
             [VMEM] * 7,
             [pltpu.HBM((BX, BY, N), F32), pltpu.HBM((BX, BY, N), F32)],
-            [(PEN, 2, 8, BX * BY), (BX, BY, N), (BX, BY, N), pltpu.SemaphoreType.DMA((2,))],
+            [(PEN, 2, 8, BX * BY), (BX, BY, N), (BX, BY, N), pltpu.SemaphoreType.DMA((3,))],
         )(recv, residual, direction, operated, control, high, low)
     )
 

time: 136 us -> 135 us (level)
  transfers between devices with their start and end apart: 6 -> 6, of which waited for: 4 -> 4; matrix products, arithmetic and copies ran while one was open for 0% -> 0% of each run, Pallas kernels for 6% -> 7%
where the time goes in v9:
time: 135 us; the launch traced here: 134 us
  blocking collectives  68.2 us (51%)
  starting transfers between devices  26.3 us (19%)
  Pallas kernels  21.4 us (16%)
  waiting for transfers between devices  17.4 us (13%)
    all_to_all x3, blocking collectives, exchange(): return lax.all_to_all(x, axis, 0, 0)  68.2 us
    all_to_all x2, starting transfers between devices, exchange(): return lax.all_to_all(x, axis, 0, 0)  18 us
    all_to_all x2, waiting for transfers between devices, exchange(): return lax.all_to_all(x, axis, 0, 0)  13.7 us
    pallas_call x1, Pallas kernels, on_device(): call(residual_blocks_kernel, [VMEM, VMEM, VMEM, SMEM, VMEM, VMEM], [pltpu...  4.8 us
    pallas_call x1, Pallas kernels, on_device(): call(operated_blocks_kernel, [HBM, HBM] + [VMEM] * 4, [block, shape(GRP,...  3.74 us
    ppermute x1, starting transfers between devices, on_device(): lax.ppermute(second, 'pen', [(i, i + 1 if i % 2 else i - 1) for i in rang...  3.68 us
    pallas_call x1, Pallas kernels, on_device(): call(residual_kernel, [HBM] * 3, [pltpu.HBM((PEN, 8, 8, 128), F32)], [(BX...  3.38 us
  transfers between devices with their start and end apart: 6, of which 4 were waited for; matrix products, arithmetic and copies ran while one was open for 0% of the time, Pallas kernels for 7%

profile of v9, /device:TPU:1, one launch (start us, length us, event | category | flops | bytes accessed | tf_op | source)
XLA Modules:
  0.0 134.3 jit_solution(5173876179351234527)
XLA Ops:
  0.6 3.4 %shard_map.95 = f32[32,8,8,128]{3,2,1,0:T(8,128)} custom-call(f32[32,16,512]{2,1,0:T(8,128)} %r_ref.3, bf16[512,512]{1,0:T(8,128)(2,1)} %constant.10.clone.ch_hbm.ch_ref, bf16[512,512]{1,0:T(8,128)(2,1)} %constant.11.clone.cl_hbm.cl_ref), custom_call_target="tpu_custom_call" | custom-call | tf_op jit(solution)/shard_map/pallas_call | solution.py:507
  4.0 0.0 copy-start.2
  4.0 0.0 copy-start.4
  4.0 11.3 %all-to-all-start = ((f32[32,8,8,128]{3,2,1,0:T(8,128)}), f32[32,8,8,128]{3,2,1,0:T(8,128)}, u32[]{:S(2)}, u32[]{:S(2)}) async-start(f32[32,8,8,128]{3,2,1,0:T(8,128)} %shard_map.95), calls=%async_computation | async-start | bytes 2097152 | tf_op jit(solution)/shard_map/all_to_all | solution.py:492
  15.3 0.0 copy-done.2
  15.3 0.0 copy-start.3
  15.4 0.0 copy-start.5
  15.4 0.1 shard_map.98
  15.5 3.7 %collective-permute-start = (f32[32,512]{1,0:T(8,128)S(1)}, f32[32,512]{1,0:T(8,128)S(1)}, u32[]{:S(2)}, u32[]{:S(2)}) collective-permute-start(f32[32,512]{1,0:T(8,128)S(1)} %get-tuple-element.22), channel_id=1, source_target_pairs={{1,2},{2,1},{3,4},{4,3},{5,6},{6,5},{7,8},{8,7},{9,10},{10,9},{11,... | collective-permute-start | bytes 196616 | tf_op jit(solution)/shard_map/ppermute | solution.py:525
  19.1 1.9 %collective-permute-start.3 = (f32[32,512]{1,0:T(8,128)S(1)}, f32[32,512]{1,0:T(8,128)S(1)}, u32[]{:S(2)}, u32[]{:S(2)}) collective-permute-start(f32[32,512]{1,0:T(8,128)S(1)} %get-tuple-element.25), channel_id=1, source_target_pairs={{0,1},{1,0},{2,3},{3,2},{4,5},{5,4},{6,7},{7,6},{8,9},{9,8},{10,11... | collective-permute-start | bytes 196616 | tf_op jit(solution)/shard_map/ppermute | solution.py:527
  21.1 1.3 collective-permute-start.1
  22.4 0.0 copy-start
  22.4 0.0 copy-start.1
  22.4 1.4 %collective-permute-start.2 = (f32[1,16,512]{2,1,0:T(8,128)S(1)}, f32[1,16,512]{2,1,0:T(8,128)S(1)}, u32[]{:S(2)}, u32[]{:S(2)}) collective-permute-start(f32[1,16,512]{2,1,0:T(8,128)S(1)} %get-tuple-element.24), channel_id=1, source_target_pairs={{32,0},{64,32},{96,64},{128,96},{160,128},{192,160},{224,192},{256... | collective-permute-start | bytes 98312 | tf_op jit(solution)/shard_map/ppermute | solution.py:523
  23.9 1.4 %shard_map.97 = (f32[32,16,512]{2,1,0:T(8,128)S(1)}, f32[2,8,128]{2,1,0:T(8,128)S(1)}) custom-call(f32[32,16,512]{2,1,0:T(8,128)S(1)} %copy-done.3, f32[32,16,512]{2,1,0:T(8,128)S(1)} %copy-done.2, s32[32,16,512]{2,1,0:T(8,128)S(1)} %copy-done.5), custom_call_target="tpu_custom_call" | custom-call | tf_op jit(solution)/shard_map/pallas_call | solution.py:528
  25.3 0.0 collective-permute-done.1.xl_ref
  25.3 2.3 %collective-permute-done.2.xh_ref = f32[1,16,512]{2,1,0:T(8,128)S(1)} collective-permute-done((f32[1,16,512]{2,1,0:T(8,128)S(1)}, f32[1,16,512]{2,1,0:T(8,128)S(1)}, u32[]{:S(2)}, u32[]{:S(2)}) %collective-permute-start.2) | collective-permute-done | bytes 32800 | tf_op jit(solution)/shard_map/ppermute | solution.py:523
  27.6 1.4 %collective-permute-done.yb_ref = f32[32,512]{1,0:T(8,128)S(1)} collective-permute-done((f32[32,512]{1,0:T(8,128)S(1)}, f32[32,512]{1,0:T(8,128)S(1)}, u32[]{:S(2)}, u32[]{:S(2)}) %collective-permute-start) | collective-permute-done | bytes 65568 | tf_op jit(solution)/shard_map/ppermute | solution.py:525
  29.0 0.0 collective-permute-done.3.ya_ref
  29.0 0.0 copy-done.1
  29.0 2.5 %shard_map.99 = (f32[32,16,512]{2,1,0:T(8,128)}, f32[32,17,4,128]{3,2,1,0:T(4,128)}) custom-call(f32[32,16,512]{2,1,0:T(8,128)S(1)} %get-tuple-element.20.q_ref, f32[2,8,128]{2,1,0:T(8,128)S(1)} %get-tuple-element.21.sums_ref, f32[32,16,512]{2,1,0:T(8,128)S(1)} %copy-done.2, s32[32,16,512]{2,1,0:T(8,128)S(1)} %copy-done.5, ...), custom_call_target="tpu_custom_call" | custom-call | tf_op jit(solution)/shard_map/pallas_call | solution.py:531
  31.5 0.9 all-to-all-done.recv_ref
  32.4 6.7 %all-to-all-start.1 = ((f32[32,17,4,128]{3,2,1,0:T(4,128)}), f32[32,17,4,128]{3,2,1,0:T(4,128)}, u32[]{:S(2)}, u32[]{:S(2)}) async-start(f32[32,17,4,128]{3,2,1,0:T(4,128)} %get-tuple-element.26), calls=%async_computation.1 | async-start | bytes 2228224 | tf_op jit(solution)/shard_map/all_to_all | solution.py:492
  39.1 4.8 %shard_map.96 = (f32[32,16,512]{2,1,0:T(8,128)}, f32[32,16,512]{2,1,0:T(8,128)}, f32[16,8,1,128]{3,2,1,0:T(1,128)S(1)}, f32[2,16,512]{2,1,0:T(8,128)S(1)}, f32[19,8,128]{2,1,0:T(8,128)S(1)}) custom-call(f32[32,8,8,128]{3,2,1,0:T(8,128)} %all-to-all-done.recv_ref, bf16[512,512]{1,0:T(8,128)(2,1)S(1)} %copy-done.1, bf16[512,512]{1,0:T(8,128)(2,1)S(1)} %copy-done, ...), custom_call_target="tpu_custom_call" | custom-call | tf_op jit(solution)/shard_map/pallas_call | solution.py:539
  43.9 12.9 %all-to-all-done.1.recv_hbm = f32[32,17,4,128]{3,2,1,0:T(4,128)} async-done(((f32[32,17,4,128]{3,2,1,0:T(4,128)}), f32[32,17,4,128]{3,2,1,0:T(4,128)}, u32[]{:S(2)}, u32[]{:S(2)}) %all-to-all-start.1) | async-done | bytes 1114144 | tf_op jit(solution)/shard_map/all_to_all | solution.py:492
  56.8 3.7 %shard_map.100 = (f32[32,16,512]{2,1,0:T(8,128)S(1)}, f32[16,17,1,128]{3,2,1,0:T(1,128)S(1)}) custom-call(f32[32,17,4,128]{3,2,1,0:T(4,128)} %all-to-all-done.1.recv_hbm, f32[32,16,512]{2,1,0:T(8,128)} %get-tuple-element.27.zr_hbm, f32[16,8,1,128]{3,2,1,0:T(1,128)S(1)} %get-tuple-element.28.states_ref, f32[2,16,512]{2,1,0:T(8,128)S(1)} %get-tuple-element.29.table_ref, ...), custom_call_target="tpu_custom_call" | custom-call | tf_op jit(solution)/shard_map/pallas_call | solution.py:551
  60.5 25.8 %all_to_all.25.recv_ref = f32[16,17,1,128]{3,2,1,0:T(1,128)S(1)} all-to-all(f32[16,17,1,128]{3,2,1,0:T(1,128)S(1)} %get-tuple-element.31), channel_id=1, replica_groups=mesh['grp'=16,'pen'=32] {'grp'}, dimensions={0} | all-to-all | bytes 278528 | tf_op jit(solution)/shard_map/all_to_all | solution.py:492
  86.4 0.3 shard_map.101
  86.7 18.3 %all_to_all.26.recv_ref = f32[16,9,1,128]{3,2,1,0:T(1,128)S(1)} all-to-all(f32[16,9,1,128]{3,2,1,0:T(1,128)S(1)} %get-tuple-element.33), channel_id=1, replica_groups=mesh['grp'=16,'pen'=32] {'grp'}, dimensions={0} | all-to-all | bytes 147456 | tf_op jit(solution)/shard_map/all_to_all | solution.py:492
  105.0 2.7 %shard_map.102 = f32[32,17,4,128]{3,2,1,0:T(4,128)S(1)} custom-call(f32[32,16,512]{2,1,0:T(8,128)S(1)} %copy-done.6, f32[32,16,512]{2,1,0:T(8,128)S(1)} %get-tuple-element.30.fq_ref, f32[16,9,1,128]{3,2,1,0:T(1,128)S(1)} %all_to_all.26.recv_ref, f32[3,8,128]{2,1,0:T(8,128)S(1)} %get-tuple-element.34.control_ref, ...), custom_call_target="tpu_custom_call" | custom-call | tf_op jit(solution)/shard_map/pallas_call | solution.py:564
  107.7 24.1 %all_to_all.27.recv_ref = f32[32,17,4,128]{3,2,1,0:T(4,128)S(1)} all-to-all(f32[32,17,4,128]{3,2,1,0:T(4,128)S(1)} %shard_map.102), channel_id=1, replica_groups=mesh['grp'=16,'pen'=32] {'pen'}, dimensions={0} | all-to-all | bytes 2228224 | tf_op jit(solution)/shard_map/all_to_all | solution.py:492
  131.8 2.5 %shard_map.103 = (f32[32,16,512]{2,1,0:T(8,128)}, f32[32,16,512]{2,1,0:T(8,128)}) custom-call(f32[32,17,4,128]{3,2,1,0:T(4,128)S(1)} %all_to_all.27.recv_ref, f32[32,16,512]{2,1,0:T(8,128)S(1)} %copy-done.3, f32[32,16,512]{2,1,0:T(8,128)S(1)} %copy-done.2, f32[32,16,512]{2,1,0:T(8,128)S(1)} %copy-done.7, f32[3,8,128]{2,1,0:T(8,128)S(1)} %get-tuple-element.34.control_ref, ...), custom_call_target="tpu_custom_call" | custom-call | tf_op jit(solution)/shard_map/pallas_call | solution.py:573
  (14 shorter events, 0.0 us)
Async XLA Ops:
  4.0 11.3 %copy-start.2 = (f32[32,16,512]{2,1,0:T(8,128)S(1)}, f32[32,16,512]{2,1,0:T(8,128)}, u32[]{:S(2)}) copy-start(f32[32,16,512]{2,1,0:T(8,128)} %d_ref.7) | copy-start | bytes 3145732
  4.0 11.3 %copy-start.4 = (s32[32,16,512]{2,1,0:T(8,128)S(1)}, s32[32,16,512]{2,1,0:T(8,128)}, u32[]{:S(2)}) copy-start(s32[32,16,512]{2,1,0:T(8,128)} %m_ref.5) | copy-start | bytes 3145732
  4.0 28.3 %all-to-all-start = ((f32[32,8,8,128]{3,2,1,0:T(8,128)}), f32[32,8,8,128]{3,2,1,0:T(8,128)}, u32[]{:S(2)}, u32[]{:S(2)}) async-start(f32[32,8,8,128]{3,2,1,0:T(8,128)} %shard_map.95), calls=%async_computation | async-start | bytes 2097152 | tf_op jit(solution)/shard_map/all_to_all | solution.py:492
  15.3 8.5 %copy-start.3 = (f32[32,16,512]{2,1,0:T(8,128)S(1)}, f32[32,16,512]{2,1,0:T(8,128)}, u32[]{:S(2)}) copy-start(f32[32,16,512]{2,1,0:T(8,128)} %r_ref.3) | copy-start | bytes 3145732
  15.4 8.5 %copy-start.5 = (s32[32,16,512]{2,1,0:T(8,128)S(1)}, s32[32,16,512]{2,1,0:T(8,128)}, u32[]{:S(2)}) copy-start(s32[32,16,512]{2,1,0:T(8,128)} %m_ref.5) | copy-start | bytes 3145732
  15.5 13.5 %collective-permute-start = (f32[32,512]{1,0:T(8,128)S(1)}, f32[32,512]{1,0:T(8,128)S(1)}, u32[]{:S(2)}, u32[]{:S(2)}) collective-permute-start(f32[32,512]{1,0:T(8,128)S(1)} %get-tuple-element.22), channel_id=1, source_target_pairs={{1,2},{2,1},{3,4},{4,3},{5,6},{6,5},{7,8},{8,7},{9,10},{10,9},{11,... | collective-permute-start | bytes 196616 | tf_op jit(solution)/shard_map/ppermute | solution.py:525
  19.1 9.8 %collective-permute-start.3 = (f32[32,512]{1,0:T(8,128)S(1)}, f32[32,512]{1,0:T(8,128)S(1)}, u32[]{:S(2)}, u32[]{:S(2)}) collective-permute-start(f32[32,512]{1,0:T(8,128)S(1)} %get-tuple-element.25), channel_id=1, source_target_pairs={{0,1},{1,0},{2,3},{3,2},{4,5},{5,4},{6,7},{7,6},{8,9},{9,8},{10,11... | collective-permute-start | bytes 196616 | tf_op jit(solution)/shard_map/ppermute | solution.py:527
  21.1 4.2 %collective-permute-start.1 = (f32[1,16,512]{2,1,0:T(8,128)S(1)}, f32[1,16,512]{2,1,0:T(8,128)S(1)}, u32[]{:S(2)}, u32[]{:S(2)}) collective-permute-start(f32[1,16,512]{2,1,0:T(8,128)S(1)} %get-tuple-element.23), channel_id=1, source_target_pairs={{0,32},{32,64},{64,96},{96,128},{128,160},{160,192},{192,224},{224... | collective-permute-start | bytes 98312 | tf_op jit(solution)/shard_map/ppermute | solution.py:520
  22.4 6.6 %copy-start = (bf16[512,512]{1,0:T(8,128)(2,1)S(1)}, bf16[512,512]{1,0:T(8,128)(2,1)}, u32[]{:S(2)}) copy-start(bf16[512,512]{1,0:T(8,128)(2,1)} %constant.11.clone.cl_hbm.cl_ref) | copy-start | bytes 1572868
  22.4 6.6 %copy-start.1 = (bf16[512,512]{1,0:T(8,128)(2,1)S(1)}, bf16[512,512]{1,0:T(8,128)(2,1)}, u32[]{:S(2)}) copy-start(bf16[512,512]{1,0:T(8,128)(2,1)} %constant.10.clone.ch_hbm.ch_ref) | copy-start | bytes 1572868
  22.4 5.2 %collective-permute-start.2 = (f32[1,16,512]{2,1,0:T(8,128)S(1)}, f32[1,16,512]{2,1,0:T(8,128)S(1)}, u32[]{:S(2)}, u32[]{:S(2)}) collective-permute-start(f32[1,16,512]{2,1,0:T(8,128)S(1)} %get-tuple-element.24), channel_id=1, source_target_pairs={{32,0},{64,32},{96,64},{128,96},{160,128},{192,160},{224,192},{256... | collective-permute-start | bytes 98312 | tf_op jit(solution)/shard_map/ppermute | solution.py:523
  32.4 6.7 %copy-start.8 = (f32[8,128]{1,0:T(8,128)S(1)}, f32[8,128]{1,0:T(8,128)}, u32[]{:S(2)}) copy-start(f32[8,128]{1,0:T(8,128)} %constant.14.clone.tile_ref) | copy-start | bytes 12292
  32.4 6.7 %copy-start.9 = (f32[1,512]{1,0:T(1,128)S(1)}, f32[1,512]{1,0:T(1,128)}, u32[]{:S(2)}) copy-start(f32[1,512]{1,0:T(1,128)} %constant.13.clone.ey_ref) | copy-start | bytes 6148
  32.4 6.7 %copy-start.10 = (f32[512]{0:T(512)S(1)}, f32[512]{0:T(512)}, u32[]{:S(2)}) copy-start(f32[512]{0:T(512)} %constant.12.clone.ez_ref) | copy-start | bytes 6148
  32.4 24.4 %all-to-all-start.1 = ((f32[32,17,4,128]{3,2,1,0:T(4,128)}), f32[32,17,4,128]{3,2,1,0:T(4,128)}, u32[]{:S(2)}, u32[]{:S(2)}) async-start(f32[32,17,4,128]{3,2,1,0:T(4,128)} %get-tuple-element.26), calls=%async_computation.1 | async-start | bytes 2228224 | tf_op jit(solution)/shard_map/all_to_all | solution.py:492
  56.8 48.2 %copy-start.6 = (f32[32,16,512]{2,1,0:T(8,128)S(1)}, f32[32,16,512]{2,1,0:T(8,128)}, u32[]{:S(2)}) copy-start(f32[32,16,512]{2,1,0:T(8,128)} %get-tuple-element.19.fr_ref) | copy-start | bytes 3145732
  107.7 24.1 %copy-start.7 = (f32[32,16,512]{2,1,0:T(8,128)S(1)}, f32[32,16,512]{2,1,0:T(8,128)}, u32[]{:S(2)}) copy-start(f32[32,16,512]{2,1,0:T(8,128)} %get-tuple-element.35.q_ref) | copy-start | bytes 3145732

commit v10 on v9

--- a/solution.py
+++ b/solution.py
@@ -87,13 +87,15 @@
     return lax.rem(lax.axis_index("pen"), 2) == 0
 
 
-def faces_kernel(d_ref, m_ref, xlo_ref, xhi_ref, first_ref, second_ref):
+def faces_kernel(d_ref, m_ref, xlo_ref, xhi_ref, first_ref, second_ref, third_ref):
     xlo_ref[0] = stiffness_of(m_ref[0]) * d_ref[0]
     xhi_ref[0] = stiffness_of(m_ref[BX - 1]) * d_ref[BX - 1]
     low = stiffness_of(m_ref[:, 0, :]) * d_ref[:, 0, :]
     high = stiffness_of(m_ref[:, BY - 1, :]) * d_ref[:, BY - 1, :]
     first_ref[...] = jnp.where(even_pen(), high, low)
-    second_ref[...] = jnp.where(even_pen(), low, high)
+    second = jnp.where(even_pen(), low, high)
+    second_ref[...] = second[: BX // 2]
+    third_ref[...] = second[BX // 2 :]
 
 
 def start(copies):
@@ -172,12 +174,15 @@
 
 
 def operated_kernel(
-    q_ref, sums_ref, d_ref, m_ref, yb_ref, xl_ref, xh_ref, ya_ref, ch_ref, cl_ref, out_hbm, send_hbm, out_ref, send_ref, sems
+    q_ref, sums_ref, d_ref, m_ref, yb_ref, yc_ref, xl_ref, xh_ref, ya_ref, ch_ref, cl_ref, out_hbm, send_hbm, out_ref, send_ref, y_ref, sems
 ):
     row = lax.broadcasted_iota(jnp.int32, (8, N), 0)
 
+    y_ref[: BX // 2] = yb_ref[...]
+    y_ref[BX // 2 :] = yc_ref[...]
+
     def low_high(x, total):
-        ya, yb = ya_ref[pl.ds(x, 1), :], yb_ref[pl.ds(x, 1), :]
+        ya, yb = ya_ref[pl.ds(x, 1), :], y_ref[pl.ds(x, 1), :]
         low, high = jnp.where(even_pen(), yb, ya), jnp.where(even_pen(), ya, yb)
         for first, edge, side in ((0, 0, low), (8, 7, high)):
             rows = pl.ds(first, 8)
@@ -512,8 +517,8 @@
     )(in_hbm(residual), in_hbm(high), in_hbm(low))
     recv_r = exchange(send, "pen")
 
-    xlo, xhi, first, second = call(
-        faces_kernel, [VMEM] * 2, [shape(1, BY, N), shape(1, BY, N), shape(BX, N), shape(BX, N)]
+    xlo, xhi, first, second, third = call(
+        faces_kernel, [VMEM] * 2, [shape(1, BY, N)] * 2 + [shape(BX, N)] + [shape(BX // 2, N)] * 2
     )(direction, material)
 
     def up(x, axis, count):
@@ -522,7 +527,9 @@
     def down(x, axis, count):
         return lax.ppermute(x, axis, [(i + 1, i) for i in range(count - 1)])
 
-    yb = lax.ppermute(second, "pen", [(i, i + 1 if i % 2 else i - 1) for i in range(1, PEN - 1)])
+    across_chips = [(i, i + 1 if i % 2 else i - 1) for i in range(1, PEN - 1)]
+    yb = lax.ppermute(second, "pen", across_chips)
+    yc = lax.ppermute(third, "pen", across_chips)
     xl, xh = up(xhi, "grp", GRP), down(xlo, "grp", GRP)
     ya = lax.ppermute(first, "pen", [(i, i ^ 1) for i in range(PEN)])
     inner, sums = call(
@@ -530,10 +537,10 @@
     )(residual, direction, material)
     operated, send = call(
         operated_kernel,
-        [VMEM] * 10,
+        [VMEM] * 11,
         [pltpu.HBM((BX, BY, N), F32), pltpu.HBM((PEN, 17, 4, 128), F32)],
-        [(BX, BY, N), (PEN, 17, 4, 128), pltpu.SemaphoreType.DMA((3,))],
-    )(inner, sums, direction, material, yb, xl, xh, ya, high, low)
+        [(BX, BY, N), (PEN, 17, 4, 128), (BX, N), pltpu.SemaphoreType.DMA((3,))],
+    )(inner, sums, direction, material, yb, yc, xl, xh, ya, high, low)
     recv_q = exchange(send, "pen")
 
     field_r, inside_r, states, table, across = call(

time: 135 us -> 138 us (1.022)
  starting transfers between devices: 26.3 us -> 30.8 us
  waiting for transfers between devices: 17.4 us -> 15.2 us
    all_to_all x2, starting transfers between devices: 18 us -> 20.1 us  [exchange(): return lax.all_to_all(x, axis, 0, 0)]
    ppermute x1 -> x2, starting transfers between devices: 3.68 us -> 5.56 us  [the longest x1 3.27 us: on_device(): yb = lax.ppermute(second, 'pen', across_chips)]
    ppermute x1, waiting for transfers between devices: 2.31 us -> 0.84 us  [down(): return lax.ppermute(x, axis, [(i + 1, i) for i in range(count - 1)])]
  transfers between devices with their start and end apart: 6 -> 7, of which waited for: 4 -> 3; matrix products, arithmetic and copies ran while one was open for 0% -> 0% of each run, Pallas kernels for 7% -> 6%
where the time goes in v10:
time: 138 us; the launch traced here: 137 us
  blocking collectives  68.7 us (50%)
  starting transfers between devices  30.8 us (22%)
  Pallas kernels  21.4 us (16%)
  waiting for transfers between devices  15.2 us (11%)
    all_to_all x3, blocking collectives, exchange(): return lax.all_to_all(x, axis, 0, 0)  68.7 us
    all_to_all x2, starting transfers between devices, exchange(): return lax.all_to_all(x, axis, 0, 0)  20.1 us
    all_to_all x2, waiting for transfers between devices, exchange(): return lax.all_to_all(x, axis, 0, 0)  12.9 us
    pallas_call x1, Pallas kernels, on_device(): call(residual_blocks_kernel, [VMEM, VMEM, VMEM, SMEM, VMEM, VMEM], [pltpu...  4.8 us
    pallas_call x1, Pallas kernels, on_device(): call(operated_blocks_kernel, [HBM, HBM] + [VMEM] * 4, [block, shape(GRP,...  3.74 us
    pallas_call x1, Pallas kernels, on_device(): call(residual_kernel, [HBM] * 3, [pltpu.HBM((PEN, 8, 8, 128), F32)], [(BX...  3.38 us
    ppermute x1, starting transfers between devices, on_device(): yb = lax.ppermute(second, 'pen', across_chips)  3.27 us
  transfers between devices with their start and end apart: 7, of which 3 were waited for; matrix products, arithmetic and copies ran while one was open for 0% of the time, Pallas kernels for 6%

profile of v10, /device:TPU:1, one launch (start us, length us, event | category | flops | bytes accessed | tf_op | source)
XLA Modules:
  0.0 137.1 jit_solution(5839640758593637128)
XLA Ops:
  0.6 3.4 %shard_map.95 = f32[32,8,8,128]{3,2,1,0:T(8,128)} custom-call(f32[32,16,512]{2,1,0:T(8,128)} %r_ref.3, bf16[512,512]{1,0:T(8,128)(2,1)} %constant.10.clone.ch_hbm.ch_ref, bf16[512,512]{1,0:T(8,128)(2,1)} %constant.11.clone.cl_hbm.cl_ref), custom_call_target="tpu_custom_call" | custom-call | tf_op jit(solution)/shard_map/pallas_call | solution.py:512
  4.0 0.0 copy-start.2
  4.0 0.0 copy-start.4
  4.0 11.3 %all-to-all-start = ((f32[32,8,8,128]{3,2,1,0:T(8,128)}), f32[32,8,8,128]{3,2,1,0:T(8,128)}, u32[]{:S(2)}, u32[]{:S(2)}) async-start(f32[32,8,8,128]{3,2,1,0:T(8,128)} %shard_map.95), calls=%async_computation | async-start | bytes 2097152 | tf_op jit(solution)/shard_map/all_to_all | solution.py:497
  15.3 0.0 copy-start.3
  15.3 0.0 copy-start.5
  15.4 0.1 shard_map.98
  15.4 2.5 %collective-permute-start.4 = (f32[32,512]{1,0:T(8,128)S(1)}, f32[32,512]{1,0:T(8,128)S(1)}, u32[]{:S(2)}, u32[]{:S(2)}) collective-permute-start(f32[32,512]{1,0:T(8,128)S(1)} %get-tuple-element.27), channel_id=1, source_target_pairs={{0,1},{1,0},{2,3},{3,2},{4,5},{5,4},{6,7},{7,6},{8,9},{9,8},{10,11... | collective-permute-start | bytes 196616 | tf_op jit(solution)/shard_map/ppermute | solution.py:534
  17.9 3.3 %collective-permute-start = (f32[16,512]{1,0:T(8,128)S(1)}, f32[16,512]{1,0:T(8,128)S(1)}, u32[]{:S(2)}, u32[]{:S(2)}) collective-permute-start(f32[16,512]{1,0:T(8,128)S(1)} %get-tuple-element.23), channel_id=1, source_target_pairs={{1,2},{2,1},{3,4},{4,3},{5,6},{6,5},{7,8},{8,7},{9,10},{10,9},{11,... | collective-permute-start | bytes 98312 | tf_op jit(solution)/shard_map/ppermute | solution.py:531
  21.2 2.3 %collective-permute-start.1 = (f32[16,512]{1,0:T(8,128)S(1)}, f32[16,512]{1,0:T(8,128)S(1)}, u32[]{:S(2)}, u32[]{:S(2)}) collective-permute-start(f32[16,512]{1,0:T(8,128)S(1)} %get-tuple-element.24), channel_id=1, source_target_pairs={{1,2},{2,1},{3,4},{4,3},{5,6},{6,5},{7,8},{8,7},{9,10},{10,9},{11,... | collective-permute-start | bytes 98312 | tf_op jit(solution)/shard_map/ppermute | solution.py:532
  23.5 1.3 collective-permute-start.2
  24.8 0.0 copy-start
  24.8 0.0 copy-start.1
  24.8 1.4 %collective-permute-start.3 = (f32[1,16,512]{2,1,0:T(8,128)S(1)}, f32[1,16,512]{2,1,0:T(8,128)S(1)}, u32[]{:S(2)}, u32[]{:S(2)}) collective-permute-start(f32[1,16,512]{2,1,0:T(8,128)S(1)} %get-tuple-element.26), channel_id=1, source_target_pairs={{32,0},{64,32},{96,64},{128,96},{160,128},{192,160},{224,192},{256... | collective-permute-start | bytes 98312 | tf_op jit(solution)/shard_map/ppermute | solution.py:528
  26.3 1.4 %shard_map.97 = (f32[32,16,512]{2,1,0:T(8,128)S(1)}, f32[2,8,128]{2,1,0:T(8,128)S(1)}) custom-call(f32[32,16,512]{2,1,0:T(8,128)S(1)} %copy-done.3, f32[32,16,512]{2,1,0:T(8,128)S(1)} %copy-done.2, s32[32,16,512]{2,1,0:T(8,128)S(1)} %copy-done.5), custom_call_target="tpu_custom_call" | custom-call | tf_op jit(solution)/shard_map/pallas_call | solution.py:535
  27.7 0.0 collective-permute-done.yb_ref
  27.7 1.5 %collective-permute-done.1.yc_ref = f32[16,512]{1,0:T(8,128)S(1)} collective-permute-done((f32[16,512]{1,0:T(8,128)S(1)}, f32[16,512]{1,0:T(8,128)S(1)}, u32[]{:S(2)}, u32[]{:S(2)}) %collective-permute-start.1) | collective-permute-done | bytes 32800 | tf_op jit(solution)/shard_map/ppermute | solution.py:532
  29.2 0.8 collective-permute-done.3.xh_ref
  30.0 2.5 %shard_map.99 = (f32[32,16,512]{2,1,0:T(8,128)}, f32[32,17,4,128]{3,2,1,0:T(4,128)}) custom-call(f32[32,16,512]{2,1,0:T(8,128)S(1)} %get-tuple-element.21.q_ref, f32[2,8,128]{2,1,0:T(8,128)S(1)} %get-tuple-element.22.sums_ref, f32[32,16,512]{2,1,0:T(8,128)S(1)} %copy-done.2, s32[32,16,512]{2,1,0:T(8,128)S(1)} %copy-done.5, ...), custom_call_target="tpu_custom_call" | custom-call | tf_op jit(solution)/shard_map/pallas_call | solution.py:538
  32.6 0.0 copy-start.8
  32.6 0.0 copy-start.9
  32.6 0.0 copy-start.10
  32.6 8.8 %all-to-all-start.1 = ((f32[32,17,4,128]{3,2,1,0:T(4,128)}), f32[32,17,4,128]{3,2,1,0:T(4,128)}, u32[]{:S(2)}, u32[]{:S(2)}) async-start(f32[32,17,4,128]{3,2,1,0:T(4,128)} %get-tuple-element.28), calls=%async_computation.1 | async-start | bytes 2228224 | tf_op jit(solution)/shard_map/all_to_all | solution.py:497
  41.4 4.8 %shard_map.96 = (f32[32,16,512]{2,1,0:T(8,128)}, f32[32,16,512]{2,1,0:T(8,128)}, f32[16,8,1,128]{3,2,1,0:T(1,128)S(1)}, f32[2,16,512]{2,1,0:T(8,128)S(1)}, f32[19,8,128]{2,1,0:T(8,128)S(1)}) custom-call(f32[32,8,8,128]{3,2,1,0:T(8,128)} %all-to-all-done.recv_ref, bf16[512,512]{1,0:T(8,128)(2,1)S(1)} %copy-done.1, bf16[512,512]{1,0:T(8,128)(2,1)S(1)} %copy-done, ...), custom_call_target="tpu_custom_call" | custom-call | tf_op jit(solution)/shard_map/pallas_call | solution.py:546
  46.2 12.9 %all-to-all-done.1.recv_hbm = f32[32,17,4,128]{3,2,1,0:T(4,128)} async-done(((f32[32,17,4,128]{3,2,1,0:T(4,128)}), f32[32,17,4,128]{3,2,1,0:T(4,128)}, u32[]{:S(2)}, u32[]{:S(2)}) %all-to-all-start.1) | async-done | bytes 1114144 | tf_op jit(solution)/shard_map/all_to_all | solution.py:497
  59.1 3.7 %shard_map.100 = (f32[32,16,512]{2,1,0:T(8,128)S(1)}, f32[16,17,1,128]{3,2,1,0:T(1,128)S(1)}) custom-call(f32[32,17,4,128]{3,2,1,0:T(4,128)} %all-to-all-done.1.recv_hbm, f32[32,16,512]{2,1,0:T(8,128)} %get-tuple-element.29.zr_hbm, f32[16,8,1,128]{3,2,1,0:T(1,128)S(1)} %get-tuple-element.30.states_ref, f32[2,16,512]{2,1,0:T(8,128)S(1)} %get-tuple-element.31.table_ref, ...), custom_call_target="tpu_custom_call" | custom-call | tf_op jit(solution)/shard_map/pallas_call | solution.py:558
  62.9 26.4 %all_to_all.25.recv_ref = f32[16,17,1,128]{3,2,1,0:T(1,128)S(1)} all-to-all(f32[16,17,1,128]{3,2,1,0:T(1,128)S(1)} %get-tuple-element.33), channel_id=1, replica_groups=mesh['grp'=16,'pen'=32] {'grp'}, dimensions={0} | all-to-all | bytes 278528 | tf_op jit(solution)/shard_map/all_to_all | solution.py:497
  89.2 0.3 shard_map.101
  89.6 18.3 %all_to_all.26.recv_ref = f32[16,9,1,128]{3,2,1,0:T(1,128)S(1)} all-to-all(f32[16,9,1,128]{3,2,1,0:T(1,128)S(1)} %get-tuple-element.35), channel_id=1, replica_groups=mesh['grp'=16,'pen'=32] {'grp'}, dimensions={0} | all-to-all | bytes 147456 | tf_op jit(solution)/shard_map/all_to_all | solution.py:497
  107.9 2.7 %shard_map.102 = f32[32,17,4,128]{3,2,1,0:T(4,128)S(1)} custom-call(f32[32,16,512]{2,1,0:T(8,128)S(1)} %copy-done.6, f32[32,16,512]{2,1,0:T(8,128)S(1)} %get-tuple-element.32.fq_ref, f32[16,9,1,128]{3,2,1,0:T(1,128)S(1)} %all_to_all.26.recv_ref, f32[3,8,128]{2,1,0:T(8,128)S(1)} %get-tuple-element.36.control_ref, ...), custom_call_target="tpu_custom_call" | custom-call | tf_op jit(solution)/shard_map/pallas_call | solution.py:571
  110.6 24.1 %all_to_all.27.recv_ref = f32[32,17,4,128]{3,2,1,0:T(4,128)S(1)} all-to-all(f32[32,17,4,128]{3,2,1,0:T(4,128)S(1)} %shard_map.102), channel_id=1, replica_groups=mesh['grp'=16,'pen'=32] {'pen'}, dimensions={0} | all-to-all | bytes 2228224 | tf_op jit(solution)/shard_map/all_to_all | solution.py:497
  134.6 2.5 %shard_map.103 = (f32[32,16,512]{2,1,0:T(8,128)}, f32[32,16,512]{2,1,0:T(8,128)}) custom-call(f32[32,17,4,128]{3,2,1,0:T(4,128)S(1)} %all_to_all.27.recv_ref, f32[32,16,512]{2,1,0:T(8,128)S(1)} %copy-done.3, f32[32,16,512]{2,1,0:T(8,128)S(1)} %copy-done.2, f32[32,16,512]{2,1,0:T(8,128)S(1)} %copy-done.7, f32[3,8,128]{2,1,0:T(8,128)S(1)} %get-tuple-element.36.control_ref, ...), custom_call_target="tpu_custom_call" | custom-call | tf_op jit(solution)/shard_map/pallas_call | solution.py:580
  (16 shorter events, 0.0 us)
Async XLA Ops:
  4.0 11.3 %copy-start.2 = (f32[32,16,512]{2,1,0:T(8,128)S(1)}, f32[32,16,512]{2,1,0:T(8,128)}, u32[]{:S(2)}) copy-start(f32[32,16,512]{2,1,0:T(8,128)} %d_ref.7) | copy-start | bytes 3145732
  4.0 11.3 %copy-start.4 = (s32[32,16,512]{2,1,0:T(8,128)S(1)}, s32[32,16,512]{2,1,0:T(8,128)}, u32[]{:S(2)}) copy-start(s32[32,16,512]{2,1,0:T(8,128)} %m_ref.5) | copy-start | bytes 3145732
  4.0 28.5 %all-to-all-start = ((f32[32,8,8,128]{3,2,1,0:T(8,128)}), f32[32,8,8,128]{3,2,1,0:T(8,128)}, u32[]{:S(2)}, u32[]{:S(2)}) async-start(f32[32,8,8,128]{3,2,1,0:T(8,128)} %shard_map.95), calls=%async_computation | async-start | bytes 2097152 | tf_op jit(solution)/shard_map/all_to_all | solution.py:497
  15.3 10.9 %copy-start.3 = (f32[32,16,512]{2,1,0:T(8,128)S(1)}, f32[32,16,512]{2,1,0:T(8,128)}, u32[]{:S(2)}) copy-start(f32[32,16,512]{2,1,0:T(8,128)} %r_ref.3) | copy-start | bytes 3145732
  15.3 10.9 %copy-start.5 = (s32[32,16,512]{2,1,0:T(8,128)S(1)}, s32[32,16,512]{2,1,0:T(8,128)}, u32[]{:S(2)}) copy-start(s32[32,16,512]{2,1,0:T(8,128)} %m_ref.5) | copy-start | bytes 3145732
  15.4 14.6 %collective-permute-start.4 = (f32[32,512]{1,0:T(8,128)S(1)}, f32[32,512]{1,0:T(8,128)S(1)}, u32[]{:S(2)}, u32[]{:S(2)}) collective-permute-start(f32[32,512]{1,0:T(8,128)S(1)} %get-tuple-element.27), channel_id=1, source_target_pairs={{0,1},{1,0},{2,3},{3,2},{4,5},{5,4},{6,7},{7,6},{8,9},{9,8},{10,11... | collective-permute-start | bytes 196616 | tf_op jit(solution)/shard_map/ppermute | solution.py:534
  17.9 9.8 %collective-permute-start = (f32[16,512]{1,0:T(8,128)S(1)}, f32[16,512]{1,0:T(8,128)S(1)}, u32[]{:S(2)}, u32[]{:S(2)}) collective-permute-start(f32[16,512]{1,0:T(8,128)S(1)} %get-tuple-element.23), channel_id=1, source_target_pairs={{1,2},{2,1},{3,4},{4,3},{5,6},{6,5},{7,8},{8,7},{9,10},{10,9},{11,... | collective-permute-start | bytes 98312 | tf_op jit(solution)/shard_map/ppermute | solution.py:531
  21.2 8.0 %collective-permute-start.1 = (f32[16,512]{1,0:T(8,128)S(1)}, f32[16,512]{1,0:T(8,128)S(1)}, u32[]{:S(2)}, u32[]{:S(2)}) collective-permute-start(f32[16,512]{1,0:T(8,128)S(1)} %get-tuple-element.24), channel_id=1, source_target_pairs={{1,2},{2,1},{3,4},{4,3},{5,6},{6,5},{7,8},{8,7},{9,10},{10,9},{11,... | collective-permute-start | bytes 98312 | tf_op jit(solution)/shard_map/ppermute | solution.py:532
  23.5 5.7 %collective-permute-start.2 = (f32[1,16,512]{2,1,0:T(8,128)S(1)}, f32[1,16,512]{2,1,0:T(8,128)S(1)}, u32[]{:S(2)}, u32[]{:S(2)}) collective-permute-start(f32[1,16,512]{2,1,0:T(8,128)S(1)} %get-tuple-element.25), channel_id=1, source_target_pairs={{0,32},{32,64},{64,96},{96,128},{128,160},{160,192},{192,224},{224... | collective-permute-start | bytes 98312 | tf_op jit(solution)/shard_map/ppermute | solution.py:525
  24.8 5.2 %copy-start = (bf16[512,512]{1,0:T(8,128)(2,1)S(1)}, bf16[512,512]{1,0:T(8,128)(2,1)}, u32[]{:S(2)}) copy-start(bf16[512,512]{1,0:T(8,128)(2,1)} %constant.11.clone.cl_hbm.cl_ref) | copy-start | bytes 1572868
  24.8 5.2 %copy-start.1 = (bf16[512,512]{1,0:T(8,128)(2,1)S(1)}, bf16[512,512]{1,0:T(8,128)(2,1)}, u32[]{:S(2)}) copy-start(bf16[512,512]{1,0:T(8,128)(2,1)} %constant.10.clone.ch_hbm.ch_ref) | copy-start | bytes 1572868
  24.8 5.2 %collective-permute-start.3 = (f32[1,16,512]{2,1,0:T(8,128)S(1)}, f32[1,16,512]{2,1,0:T(8,128)S(1)}, u32[]{:S(2)}, u32[]{:S(2)}) collective-permute-start(f32[1,16,512]{2,1,0:T(8,128)S(1)} %get-tuple-element.26), channel_id=1, source_target_pairs={{32,0},{64,32},{96,64},{128,96},{160,128},{192,160},{224,192},{256... | collective-permute-start | bytes 98312 | tf_op jit(solution)/shard_map/ppermute | solution.py:528
  32.6 8.9 %copy-start.8 = (f32[8,128]{1,0:T(8,128)S(1)}, f32[8,128]{1,0:T(8,128)}, u32[]{:S(2)}) copy-start(f32[8,128]{1,0:T(8,128)} %constant.14.clone.tile_ref) | copy-start | bytes 12292
  32.6 8.9 %copy-start.9 = (f32[1,512]{1,0:T(1,128)S(1)}, f32[1,512]{1,0:T(1,128)}, u32[]{:S(2)}) copy-start(f32[1,512]{1,0:T(1,128)} %constant.13.clone.ey_ref) | copy-start | bytes 6148
  32.6 8.9 %copy-start.10 = (f32[512]{0:T(512)S(1)}, f32[512]{0:T(512)}, u32[]{:S(2)}) copy-start(f32[512]{0:T(512)} %constant.12.clone.ez_ref) | copy-start | bytes 6148
  32.6 26.5 %all-to-all-start.1 = ((f32[32,17,4,128]{3,2,1,0:T(4,128)}), f32[32,17,4,128]{3,2,1,0:T(4,128)}, u32[]{:S(2)}, u32[]{:S(2)}) async-start(f32[32,17,4,128]{3,2,1,0:T(4,128)} %get-tuple-element.28), calls=%async_computation.1 | async-start | bytes 2228224 | tf_op jit(solution)/shard_map/all_to_all | solution.py:497
  59.1 48.8 %copy-start.6 = (f32[32,16,512]{2,1,0:T(8,128)S(1)}, f32[32,16,512]{2,1,0:T(8,128)}, u32[]{:S(2)}) copy-start(f32[32,16,512]{2,1,0:T(8,128)} %get-tuple-element.20.fr_ref) | copy-start | bytes 3145732
  110.6 24.1 %copy-start.7 = (f32[32,16,512]{2,1,0:T(8,128)S(1)}, f32[32,16,512]{2,1,0:T(8,128)}, u32[]{:S(2)}) copy-start(f32[32,16,512]{2,1,0:T(8,128)} %get-tuple-element.37.q_ref) | copy-start | bytes 3145732

commit v11 on v9

--- a/solution.py
+++ b/solution.py
@@ -83,17 +83,19 @@
     return jnp.where(material == 1, jnp.float32(SOLID), jnp.float32(1.0))
 
 
-def even_pen():
-    return lax.rem(lax.axis_index("pen"), 2) == 0
-
-
-def faces_kernel(d_ref, m_ref, xlo_ref, xhi_ref, first_ref, second_ref):
-    xlo_ref[0] = stiffness_of(m_ref[0]) * d_ref[0]
-    xhi_ref[0] = stiffness_of(m_ref[BX - 1]) * d_ref[BX - 1]
+def even(axis):
+    return lax.rem(lax.axis_index(axis), 2) == 0
+
+
+def faces_kernel(d_ref, m_ref, x_first_ref, x_second_ref, first_ref, second_ref):
+    low = stiffness_of(m_ref[0]) * d_ref[0]
+    high = stiffness_of(m_ref[BX - 1]) * d_ref[BX - 1]
+    x_first_ref[0] = jnp.where(even("grp"), high, low)
+    x_second_ref[0] = jnp.where(even("grp"), low, high)
     low = stiffness_of(m_ref[:, 0, :]) * d_ref[:, 0, :]
     high = stiffness_of(m_ref[:, BY - 1, :]) * d_ref[:, BY - 1, :]
-    first_ref[...] = jnp.where(even_pen(), high, low)
-    second_ref[...] = jnp.where(even_pen(), low, high)
+    first_ref[...] = jnp.where(even("pen"), high, low)
+    second_ref[...] = jnp.where(even("pen"), low, high)
 
 
 def start(copies):
@@ -172,13 +174,13 @@
 
 
 def operated_kernel(
-    q_ref, sums_ref, d_ref, m_ref, yb_ref, xl_ref, xh_ref, ya_ref, ch_ref, cl_ref, out_hbm, send_hbm, out_ref, send_ref, sems
+    q_ref, sums_ref, d_ref, m_ref, yb_ref, xa_ref, xb_ref, ya_ref, ch_ref, cl_ref, out_hbm, send_hbm, out_ref, send_ref, sems
 ):
     row = lax.broadcasted_iota(jnp.int32, (8, N), 0)
 
     def low_high(x, total):
         ya, yb = ya_ref[pl.ds(x, 1), :], yb_ref[pl.ds(x, 1), :]
-        low, high = jnp.where(even_pen(), yb, ya), jnp.where(even_pen(), ya, yb)
+        low, high = jnp.where(even("pen"), yb, ya), jnp.where(even("pen"), ya, yb)
         for first, edge, side in ((0, 0, low), (8, 7, high)):
             rows = pl.ds(first, 8)
             add = stiffness_of(m_ref[x, rows]) * jnp.where(row == edge, side, 0.0)
@@ -188,8 +190,10 @@
 
     total = lax.fori_loop(0, BX, low_high, jnp.zeros((8, N), F32), unroll=4)
     total = jnp.concatenate([total, jnp.zeros((8, N), F32)], axis=0)
-    for x, side_ref in ((0, xl_ref), (BX - 1, xh_ref)):
-        add = stiffness_of(m_ref[x]) * side_ref[0]
+    xa, xb = xa_ref[0], xb_ref[0]
+    low, high = jnp.where(even("grp"), xb, xa), jnp.where(even("grp"), xa, xb)
+    for x, side in ((0, low), (BX - 1, high)):
+        add = stiffness_of(m_ref[x]) * side
         out_ref[x] = out_ref[x] - add
         total = total + d_ref[x] * add
     curvature = sums_ref[0] - to_tile(total)
@@ -512,19 +516,19 @@
     )(in_hbm(residual), in_hbm(high), in_hbm(low))
     recv_r = exchange(send, "pen")
 
-    xlo, xhi, first, second = call(
+    x_first, x_second, first, second = call(
         faces_kernel, [VMEM] * 2, [shape(1, BY, N), shape(1, BY, N), shape(BX, N), shape(BX, N)]
     )(direction, material)
 
-    def up(x, axis, count):
-        return lax.ppermute(x, axis, [(i, i + 1) for i in range(count - 1)])
-
-    def down(x, axis, count):
-        return lax.ppermute(x, axis, [(i + 1, i) for i in range(count - 1)])
-
-    yb = lax.ppermute(second, "pen", [(i, i + 1 if i % 2 else i - 1) for i in range(1, PEN - 1)])
-    xl, xh = up(xhi, "grp", GRP), down(xlo, "grp", GRP)
-    ya = lax.ppermute(first, "pen", [(i, i ^ 1) for i in range(PEN)])
+    def swap_pairs(x, axis, count):
+        return lax.ppermute(x, axis, [(i, i ^ 1) for i in range(count)])
+
+    def swap_between(x, axis, count):
+        return lax.ppermute(x, axis, [(i, i + 1 if i % 2 else i - 1) for i in range(1, count - 1)])
+
+    xa, xb = swap_pairs(x_first, "grp", GRP), swap_between(x_second, "grp", GRP)
+    ya, yb = swap_pairs(first, "pen", PEN), swap_between(second, "pen", PEN)
+
     inner, sums = call(
         inner_kernel, [VMEM] * 3, [block, shape(2, 8, 128)], [(BX + 2, BY, N)]
     )(residual, direction, material)
@@ -533,7 +537,7 @@
         [VMEM] * 10,
         [pltpu.HBM((BX, BY, N), F32), pltpu.HBM((PEN, 17, 4, 128), F32)],
         [(BX, BY, N), (PEN, 17, 4, 128), pltpu.SemaphoreType.DMA((3,))],
-    )(inner, sums, direction, material, yb, xl, xh, ya, high, low)
+    )(inner, sums, direction, material, yb, xa, xb, ya, high, low)
     recv_q = exchange(send, "pen")
 
     field_r, inside_r, states, table, across = call(

time: 135 us -> 135 us (level)
  no operation moved by 1% of the time
where the time goes in v11:
time: 135 us
  blocking collectives  68.6 us (51%)
  starting transfers between devices  26.3 us (19%)
  Pallas kernels  21.4 us (16%)
  waiting for transfers between devices  17.4 us (13%)
    all_to_all x3, blocking collectives, exchange(): return lax.all_to_all(x, axis, 0, 0)  68.6 us
    all_to_all x2, starting transfers between devices, exchange(): return lax.all_to_all(x, axis, 0, 0)  18 us
    all_to_all x2, waiting for transfers between devices, exchange(): return lax.all_to_all(x, axis, 0, 0)  13.7 us
    pallas_call x1, Pallas kernels, on_device(): call(residual_blocks_kernel, [VMEM, VMEM, VMEM, SMEM, VMEM, VMEM], [pltpu...  4.8 us
    ppermute x2, starting transfers between devices, swap_between(): lax.ppermute(x, axis, [(i, i + 1 if i % 2 else i - 1) for i in range(1, c...  4.47 us
    ppermute x2, starting transfers between devices, swap_pairs(): return lax.ppermute(x, axis, [(i, i ^ 1) for i in range(count)])  3.84 us
    pallas_call x1, Pallas kernels, on_device(): call(operated_blocks_kernel, [HBM, HBM] + [VMEM] * 4, [block, shape(GRP,...  3.74 us
    pallas_call x1, Pallas kernels, on_device(): call(residual_kernel, [HBM] * 3, [pltpu.HBM((PEN, 8, 8, 128), F32)], [(BX...  3.38 us
  transfers between devices with their start and end apart: 6, of which 4 were waited for; matrix products, arithmetic and copies ran while one was open for 0% of the time, Pallas kernels for 7%

profile of v11, /device:TPU:1, one launch (start us, length us, event | category | flops | bytes accessed | tf_op | source)
XLA Modules:
  0.0 134.7 jit_solution(5000674327292932287)
XLA Ops:
  0.6 3.4 %shard_map.95 = f32[32,8,8,128]{3,2,1,0:T(8,128)} custom-call(f32[32,16,512]{2,1,0:T(8,128)} %r_ref.3, bf16[512,512]{1,0:T(8,128)(2,1)} %constant.10.clone.ch_hbm.ch_ref, bf16[512,512]{1,0:T(8,128)(2,1)} %constant.11.clone.cl_hbm.cl_ref), custom_call_target="tpu_custom_call" | custom-call | tf_op jit(solution)/shard_map/pallas_call | solution.py:511
  4.0 0.0 copy-start.2
  4.0 0.0 copy-start.4
  4.0 11.3 %all-to-all-start = ((f32[32,8,8,128]{3,2,1,0:T(8,128)}), f32[32,8,8,128]{3,2,1,0:T(8,128)}, u32[]{:S(2)}, u32[]{:S(2)}) async-start(f32[32,8,8,128]{3,2,1,0:T(8,128)} %shard_map.95), calls=%async_computation | async-start | bytes 2097152 | tf_op jit(solution)/shard_map/all_to_all | solution.py:496
  15.3 0.0 copy-done.2
  15.3 0.0 copy-done.4
  15.3 0.0 copy-start.3
  15.4 0.0 copy-start.5
  15.4 0.1 shard_map.98
  15.5 3.7 %collective-permute-start = (f32[32,512]{1,0:T(8,128)S(1)}, f32[32,512]{1,0:T(8,128)S(1)}, u32[]{:S(2)}, u32[]{:S(2)}) collective-permute-start(f32[32,512]{1,0:T(8,128)S(1)} %get-tuple-element.22), channel_id=1, source_target_pairs={{1,2},{2,1},{3,4},{4,3},{5,6},{6,5},{7,8},{8,7},{9,10},{10,9},{11,... | collective-permute-start | bytes 196616 | tf_op jit(solution)/shard_map/ppermute | solution.py:527
  19.1 1.9 %collective-permute-start.3 = (f32[32,512]{1,0:T(8,128)S(1)}, f32[32,512]{1,0:T(8,128)S(1)}, u32[]{:S(2)}, u32[]{:S(2)}) collective-permute-start(f32[32,512]{1,0:T(8,128)S(1)} %get-tuple-element.25), channel_id=1, source_target_pairs={{0,1},{1,0},{2,3},{3,2},{4,5},{5,4},{6,7},{7,6},{8,9},{9,8},{10,11... | collective-permute-start | bytes 196616 | tf_op jit(solution)/shard_map/ppermute | solution.py:524
  21.1 1.9 %collective-permute-start.1 = (f32[1,16,512]{2,1,0:T(8,128)S(1)}, f32[1,16,512]{2,1,0:T(8,128)S(1)}, u32[]{:S(2)}, u32[]{:S(2)}) collective-permute-start(f32[1,16,512]{2,1,0:T(8,128)S(1)} %get-tuple-element.23), channel_id=1, source_target_pairs={{0,32},{32,0},{64,96},{96,64},{128,160},{160,128},{192,224},{224,1... | collective-permute-start | bytes 98312 | tf_op jit(solution)/shard_map/ppermute | solution.py:524
  23.0 0.0 copy-start
  23.0 0.0 copy-start.1
  23.0 0.8 collective-permute-start.2
  23.9 1.4 %shard_map.97 = (f32[32,16,512]{2,1,0:T(8,128)S(1)}, f32[2,8,128]{2,1,0:T(8,128)S(1)}) custom-call(f32[32,16,512]{2,1,0:T(8,128)S(1)} %copy-done.3, f32[32,16,512]{2,1,0:T(8,128)S(1)} %copy-done.2, s32[32,16,512]{2,1,0:T(8,128)S(1)} %copy-done.5), custom_call_target="tpu_custom_call" | custom-call | tf_op jit(solution)/shard_map/pallas_call | solution.py:532
  25.3 0.9 collective-permute-done.1.xa_ref
  26.1 0.0 collective-permute-done.2.xb_ref
  26.1 2.8 %collective-permute-done.yb_ref = f32[32,512]{1,0:T(8,128)S(1)} collective-permute-done((f32[32,512]{1,0:T(8,128)S(1)}, f32[32,512]{1,0:T(8,128)S(1)}, u32[]{:S(2)}, u32[]{:S(2)}) %collective-permute-start) | collective-permute-done | bytes 65568 | tf_op jit(solution)/shard_map/ppermute | solution.py:527
  29.0 0.0 collective-permute-done.3.ya_ref
  29.0 2.5 %shard_map.99 = (f32[32,16,512]{2,1,0:T(8,128)}, f32[32,17,4,128]{3,2,1,0:T(4,128)}) custom-call(f32[32,16,512]{2,1,0:T(8,128)S(1)} %get-tuple-element.20.q_ref, f32[2,8,128]{2,1,0:T(8,128)S(1)} %get-tuple-element.21.sums_ref, f32[32,16,512]{2,1,0:T(8,128)S(1)} %copy-done.2, s32[32,16,512]{2,1,0:T(8,128)S(1)} %copy-done.5, ...), custom_call_target="tpu_custom_call" | custom-call | tf_op jit(solution)/shard_map/pallas_call | solution.py:535
  31.5 0.9 all-to-all-done.recv_ref
  32.4 6.7 %all-to-all-start.1 = ((f32[32,17,4,128]{3,2,1,0:T(4,128)}), f32[32,17,4,128]{3,2,1,0:T(4,128)}, u32[]{:S(2)}, u32[]{:S(2)}) async-start(f32[32,17,4,128]{3,2,1,0:T(4,128)} %get-tuple-element.26), calls=%async_computation.1 | async-start | bytes 2228224 | tf_op jit(solution)/shard_map/all_to_all | solution.py:496
  39.1 4.8 %shard_map.96 = (f32[32,16,512]{2,1,0:T(8,128)}, f32[32,16,512]{2,1,0:T(8,128)}, f32[16,8,1,128]{3,2,1,0:T(1,128)S(1)}, f32[2,16,512]{2,1,0:T(8,128)S(1)}, f32[19,8,128]{2,1,0:T(8,128)S(1)}) custom-call(f32[32,8,8,128]{3,2,1,0:T(8,128)} %all-to-all-done.recv_ref, bf16[512,512]{1,0:T(8,128)(2,1)S(1)} %copy-done.1, bf16[512,512]{1,0:T(8,128)(2,1)S(1)} %copy-done, ...), custom_call_target="tpu_custom_call" | custom-call | tf_op jit(solution)/shard_map/pallas_call | solution.py:543
  43.9 12.9 %all-to-all-done.1.recv_hbm = f32[32,17,4,128]{3,2,1,0:T(4,128)} async-done(((f32[32,17,4,128]{3,2,1,0:T(4,128)}), f32[32,17,4,128]{3,2,1,0:T(4,128)}, u32[]{:S(2)}, u32[]{:S(2)}) %all-to-all-start.1) | async-done | bytes 1114144 | tf_op jit(solution)/shard_map/all_to_all | solution.py:496
  56.8 3.7 %shard_map.100 = (f32[32,16,512]{2,1,0:T(8,128)S(1)}, f32[16,17,1,128]{3,2,1,0:T(1,128)S(1)}) custom-call(f32[32,17,4,128]{3,2,1,0:T(4,128)} %all-to-all-done.1.recv_hbm, f32[32,16,512]{2,1,0:T(8,128)} %get-tuple-element.27.zr_hbm, f32[16,8,1,128]{3,2,1,0:T(1,128)S(1)} %get-tuple-element.28.states_ref, f32[2,16,512]{2,1,0:T(8,128)S(1)} %get-tuple-element.29.table_ref, ...), custom_call_target="tpu_custom_call" | custom-call | tf_op jit(solution)/shard_map/pallas_call | solution.py:555
  60.5 26.3 %all_to_all.25.recv_ref = f32[16,17,1,128]{3,2,1,0:T(1,128)S(1)} all-to-all(f32[16,17,1,128]{3,2,1,0:T(1,128)S(1)} %get-tuple-element.31), channel_id=1, replica_groups=mesh['grp'=16,'pen'=32] {'grp'}, dimensions={0} | all-to-all | bytes 278528 | tf_op jit(solution)/shard_map/all_to_all | solution.py:496
  86.8 0.3 shard_map.101
  87.1 18.3 %all_to_all.26.recv_ref = f32[16,9,1,128]{3,2,1,0:T(1,128)S(1)} all-to-all(f32[16,9,1,128]{3,2,1,0:T(1,128)S(1)} %get-tuple-element.33), channel_id=1, replica_groups=mesh['grp'=16,'pen'=32] {'grp'}, dimensions={0} | all-to-all | bytes 147456 | tf_op jit(solution)/shard_map/all_to_all | solution.py:496
  105.5 2.7 %shard_map.102 = f32[32,17,4,128]{3,2,1,0:T(4,128)S(1)} custom-call(f32[32,16,512]{2,1,0:T(8,128)S(1)} %copy-done.6, f32[32,16,512]{2,1,0:T(8,128)S(1)} %get-tuple-element.30.fq_ref, f32[16,9,1,128]{3,2,1,0:T(1,128)S(1)} %all_to_all.26.recv_ref, f32[3,8,128]{2,1,0:T(8,128)S(1)} %get-tuple-element.34.control_ref, ...), custom_call_target="tpu_custom_call" | custom-call | tf_op jit(solution)/shard_map/pallas_call | solution.py:568
  108.1 24.1 %all_to_all.27.recv_ref = f32[32,17,4,128]{3,2,1,0:T(4,128)S(1)} all-to-all(f32[32,17,4,128]{3,2,1,0:T(4,128)S(1)} %shard_map.102), channel_id=1, replica_groups=mesh['grp'=16,'pen'=32] {'pen'}, dimensions={0} | all-to-all | bytes 2228224 | tf_op jit(solution)/shard_map/all_to_all | solution.py:496
  132.2 2.5 %shard_map.103 = (f32[32,16,512]{2,1,0:T(8,128)}, f32[32,16,512]{2,1,0:T(8,128)}) custom-call(f32[32,17,4,128]{3,2,1,0:T(4,128)S(1)} %all_to_all.27.recv_ref, f32[32,16,512]{2,1,0:T(8,128)S(1)} %copy-done.3, f32[32,16,512]{2,1,0:T(8,128)S(1)} %copy-done.2, f32[32,16,512]{2,1,0:T(8,128)S(1)} %copy-done.7, f32[3,8,128]{2,1,0:T(8,128)S(1)} %get-tuple-element.34.control_ref, ...), custom_call_target="tpu_custom_call" | custom-call | tf_op jit(solution)/shard_map/pallas_call | solution.py:577
  (14 shorter events, 0.0 us)
Async XLA Ops:
  4.0 11.3 %copy-start.2 = (f32[32,16,512]{2,1,0:T(8,128)S(1)}, f32[32,16,512]{2,1,0:T(8,128)}, u32[]{:S(2)}) copy-start(f32[32,16,512]{2,1,0:T(8,128)} %d_ref.7) | copy-start | bytes 3145732
  4.0 11.3 %copy-start.4 = (s32[32,16,512]{2,1,0:T(8,128)S(1)}, s32[32,16,512]{2,1,0:T(8,128)}, u32[]{:S(2)}) copy-start(s32[32,16,512]{2,1,0:T(8,128)} %m_ref.5) | copy-start | bytes 3145732
  4.0 28.3 %all-to-all-start = ((f32[32,8,8,128]{3,2,1,0:T(8,128)}), f32[32,8,8,128]{3,2,1,0:T(8,128)}, u32[]{:S(2)}, u32[]{:S(2)}) async-start(f32[32,8,8,128]{3,2,1,0:T(8,128)} %shard_map.95), calls=%async_computation | async-start | bytes 2097152 | tf_op jit(solution)/shard_map/all_to_all | solution.py:496
  15.3 8.5 %copy-start.3 = (f32[32,16,512]{2,1,0:T(8,128)S(1)}, f32[32,16,512]{2,1,0:T(8,128)}, u32[]{:S(2)}) copy-start(f32[32,16,512]{2,1,0:T(8,128)} %r_ref.3) | copy-start | bytes 3145732
  15.4 8.5 %copy-start.5 = (s32[32,16,512]{2,1,0:T(8,128)S(1)}, s32[32,16,512]{2,1,0:T(8,128)}, u32[]{:S(2)}) copy-start(s32[32,16,512]{2,1,0:T(8,128)} %m_ref.5) | copy-start | bytes 3145732
  15.5 13.5 %collective-permute-start = (f32[32,512]{1,0:T(8,128)S(1)}, f32[32,512]{1,0:T(8,128)S(1)}, u32[]{:S(2)}, u32[]{:S(2)}) collective-permute-start(f32[32,512]{1,0:T(8,128)S(1)} %get-tuple-element.22), channel_id=1, source_target_pairs={{1,2},{2,1},{3,4},{4,3},{5,6},{6,5},{7,8},{8,7},{9,10},{10,9},{11,... | collective-permute-start | bytes 196616 | tf_op jit(solution)/shard_map/ppermute | solution.py:527
  19.1 9.8 %collective-permute-start.3 = (f32[32,512]{1,0:T(8,128)S(1)}, f32[32,512]{1,0:T(8,128)S(1)}, u32[]{:S(2)}, u32[]{:S(2)}) collective-permute-start(f32[32,512]{1,0:T(8,128)S(1)} %get-tuple-element.25), channel_id=1, source_target_pairs={{0,1},{1,0},{2,3},{3,2},{4,5},{5,4},{6,7},{7,6},{8,9},{9,8},{10,11... | collective-permute-start | bytes 196616 | tf_op jit(solution)/shard_map/ppermute | solution.py:524
  21.1 5.1 %collective-permute-start.1 = (f32[1,16,512]{2,1,0:T(8,128)S(1)}, f32[1,16,512]{2,1,0:T(8,128)S(1)}, u32[]{:S(2)}, u32[]{:S(2)}) collective-permute-start(f32[1,16,512]{2,1,0:T(8,128)S(1)} %get-tuple-element.23), channel_id=1, source_target_pairs={{0,32},{32,0},{64,96},{96,64},{128,160},{160,128},{192,224},{224,1... | collective-permute-start | bytes 98312 | tf_op jit(solution)/shard_map/ppermute | solution.py:524
  23.0 6.0 %copy-start = (bf16[512,512]{1,0:T(8,128)(2,1)S(1)}, bf16[512,512]{1,0:T(8,128)(2,1)}, u32[]{:S(2)}) copy-start(bf16[512,512]{1,0:T(8,128)(2,1)} %constant.11.clone.cl_hbm.cl_ref) | copy-start | bytes 1572868
  23.0 6.0 %copy-start.1 = (bf16[512,512]{1,0:T(8,128)(2,1)S(1)}, bf16[512,512]{1,0:T(8,128)(2,1)}, u32[]{:S(2)}) copy-start(bf16[512,512]{1,0:T(8,128)(2,1)} %constant.10.clone.ch_hbm.ch_ref) | copy-start | bytes 1572868
  23.0 3.1 %collective-permute-start.2 = (f32[1,16,512]{2,1,0:T(8,128)S(1)}, f32[1,16,512]{2,1,0:T(8,128)S(1)}, u32[]{:S(2)}, u32[]{:S(2)}) collective-permute-start(f32[1,16,512]{2,1,0:T(8,128)S(1)} %get-tuple-element.24), channel_id=1, source_target_pairs={{32,64},{64,32},{96,128},{128,96},{160,192},{192,160},{224,256},{2... | collective-permute-start | bytes 98312 | tf_op jit(solution)/shard_map/ppermute | solution.py:527
  32.4 6.7 %copy-start.8 = (f32[8,128]{1,0:T(8,128)S(1)}, f32[8,128]{1,0:T(8,128)}, u32[]{:S(2)}) copy-start(f32[8,128]{1,0:T(8,128)} %constant.14.clone.tile_ref) | copy-start | bytes 12292
  32.4 6.7 %copy-start.9 = (f32[1,512]{1,0:T(1,128)S(1)}, f32[1,512]{1,0:T(1,128)}, u32[]{:S(2)}) copy-start(f32[1,512]{1,0:T(1,128)} %constant.13.clone.ey_ref) | copy-start | bytes 6148
  32.4 6.7 %copy-start.10 = (f32[512]{0:T(512)S(1)}, f32[512]{0:T(512)}, u32[]{:S(2)}) copy-start(f32[512]{0:T(512)} %constant.12.clone.ez_ref) | copy-start | bytes 6148
  32.4 24.4 %all-to-all-start.1 = ((f32[32,17,4,128]{3,2,1,0:T(4,128)}), f32[32,17,4,128]{3,2,1,0:T(4,128)}, u32[]{:S(2)}, u32[]{:S(2)}) async-start(f32[32,17,4,128]{3,2,1,0:T(4,128)} %get-tuple-element.26), calls=%async_computation.1 | async-start | bytes 2228224 | tf_op jit(solution)/shard_map/all_to_all | solution.py:496
  56.8 48.7 %copy-start.6 = (f32[32,16,512]{2,1,0:T(8,128)S(1)}, f32[32,16,512]{2,1,0:T(8,128)}, u32[]{:S(2)}) copy-start(f32[32,16,512]{2,1,0:T(8,128)} %get-tuple-element.19.fr_ref) | copy-start | bytes 3145732
  108.1 24.1 %copy-start.7 = (f32[32,16,512]{2,1,0:T(8,128)S(1)}, f32[32,16,512]{2,1,0:T(8,128)}, u32[]{:S(2)}) copy-start(f32[32,16,512]{2,1,0:T(8,128)} %get-tuple-element.35.q_ref) | copy-start | bytes 3145732

commit v12 on v9

--- a/solution.py
+++ b/solution.py
@@ -305,6 +305,7 @@
         [
             pltpu.make_async_copy(recv_hbm.at[:, 16], recv_ref.at[:, 16], sems.at[2, 0]),
             pltpu.make_async_copy(zr_hbm, zr_ref, sems.at[2, 1]),
+            pltpu.make_async_copy(states_ref, send_ref.at[:, pl.ds(0, 8)], sems.at[2, 2]),
         ]
     )
 
@@ -342,7 +343,6 @@
         x = x + pltpu.roll(x, 64, 1)
         packed = jnp.where(group == i, x + pltpu.roll(x, 32, 1), packed)
     for j in range(GRP):
-        send_ref[j, 0:8] = states_ref[j]
         send_ref[j, 16] = packed
 
 

time: 135 us -> 135 us (level)
  no operation moved by 1% of the time
where the time goes in v12:
time: 135 us; the launch traced here: 134 us
  blocking collectives  68.2 us (51%)
  starting transfers between devices  26.3 us (19%)
  Pallas kernels  21.4 us (16%)
  waiting for transfers between devices  17.4 us (13%)
    all_to_all x3, blocking collectives, exchange(): return lax.all_to_all(x, axis, 0, 0)  68.2 us
    all_to_all x2, starting transfers between devices, exchange(): return lax.all_to_all(x, axis, 0, 0)  18 us
    all_to_all x2, waiting for transfers between devices, exchange(): return lax.all_to_all(x, axis, 0, 0)  13.7 us
    pallas_call x1, Pallas kernels, on_device(): call(residual_blocks_kernel, [VMEM, VMEM, VMEM, SMEM, VMEM, VMEM], [pltpu...  4.8 us
    pallas_call x1, Pallas kernels, on_device(): call(operated_blocks_kernel, [HBM, HBM] + [VMEM] * 4, [block, shape(GRP,...  3.74 us
    ppermute x1, starting transfers between devices, on_device(): lax.ppermute(second, 'pen', [(i, i + 1 if i % 2 else i - 1) for i in rang...  3.68 us
    pallas_call x1, Pallas kernels, on_device(): call(residual_kernel, [HBM] * 3, [pltpu.HBM((PEN, 8, 8, 128), F32)], [(BX...  3.38 us
  transfers between devices with their start and end apart: 6, of which 4 were waited for; matrix products, arithmetic and copies ran while one was open for 0% of the time, Pallas kernels for 7%

profile of v12, /device:TPU:1, one launch (start us, length us, event | category | flops | bytes accessed | tf_op | source)
XLA Modules:
  0.0 134.3 jit_solution(8110183232145558607)
XLA Ops:
  0.6 3.4 %shard_map.95 = f32[32,8,8,128]{3,2,1,0:T(8,128)} custom-call(f32[32,16,512]{2,1,0:T(8,128)} %r_ref.3, bf16[512,512]{1,0:T(8,128)(2,1)} %constant.10.clone.ch_hbm.ch_ref, bf16[512,512]{1,0:T(8,128)(2,1)} %constant.11.clone.cl_hbm.cl_ref), custom_call_target="tpu_custom_call" | custom-call | tf_op jit(solution)/shard_map/pallas_call | solution.py:507
  4.0 0.0 copy-start.2
  4.0 0.0 copy-start.4
  4.0 11.3 %all-to-all-start = ((f32[32,8,8,128]{3,2,1,0:T(8,128)}), f32[32,8,8,128]{3,2,1,0:T(8,128)}, u32[]{:S(2)}, u32[]{:S(2)}) async-start(f32[32,8,8,128]{3,2,1,0:T(8,128)} %shard_map.95), calls=%async_computation | async-start | bytes 2097152 | tf_op jit(solution)/shard_map/all_to_all | solution.py:492
  15.3 0.0 copy-start.3
  15.4 0.0 copy-start.5
  15.4 0.1 shard_map.98
  15.5 3.7 %collective-permute-start = (f32[32,512]{1,0:T(8,128)S(1)}, f32[32,512]{1,0:T(8,128)S(1)}, u32[]{:S(2)}, u32[]{:S(2)}) collective-permute-start(f32[32,512]{1,0:T(8,128)S(1)} %get-tuple-element.22), channel_id=1, source_target_pairs={{1,2},{2,1},{3,4},{4,3},{5,6},{6,5},{7,8},{8,7},{9,10},{10,9},{11,... | collective-permute-start | bytes 196616 | tf_op jit(solution)/shard_map/ppermute | solution.py:525
  19.1 1.9 %collective-permute-start.3 = (f32[32,512]{1,0:T(8,128)S(1)}, f32[32,512]{1,0:T(8,128)S(1)}, u32[]{:S(2)}, u32[]{:S(2)}) collective-permute-start(f32[32,512]{1,0:T(8,128)S(1)} %get-tuple-element.25), channel_id=1, source_target_pairs={{0,1},{1,0},{2,3},{3,2},{4,5},{5,4},{6,7},{7,6},{8,9},{9,8},{10,11... | collective-permute-start | bytes 196616 | tf_op jit(solution)/shard_map/ppermute | solution.py:527
  21.1 1.3 collective-permute-start.1
  22.4 0.0 copy-start
  22.4 0.0 copy-start.1
  22.4 1.4 %collective-permute-start.2 = (f32[1,16,512]{2,1,0:T(8,128)S(1)}, f32[1,16,512]{2,1,0:T(8,128)S(1)}, u32[]{:S(2)}, u32[]{:S(2)}) collective-permute-start(f32[1,16,512]{2,1,0:T(8,128)S(1)} %get-tuple-element.24), channel_id=1, source_target_pairs={{32,0},{64,32},{96,64},{128,96},{160,128},{192,160},{224,192},{256... | collective-permute-start | bytes 98312 | tf_op jit(solution)/shard_map/ppermute | solution.py:523
  23.9 1.4 %shard_map.97 = (f32[32,16,512]{2,1,0:T(8,128)S(1)}, f32[2,8,128]{2,1,0:T(8,128)S(1)}) custom-call(f32[32,16,512]{2,1,0:T(8,128)S(1)} %copy-done.3, f32[32,16,512]{2,1,0:T(8,128)S(1)} %copy-done.2, s32[32,16,512]{2,1,0:T(8,128)S(1)} %copy-done.5), custom_call_target="tpu_custom_call" | custom-call | tf_op jit(solution)/shard_map/pallas_call | solution.py:528
  25.3 0.0 collective-permute-done.1.xl_ref
  25.3 2.3 %collective-permute-done.2.xh_ref = f32[1,16,512]{2,1,0:T(8,128)S(1)} collective-permute-done((f32[1,16,512]{2,1,0:T(8,128)S(1)}, f32[1,16,512]{2,1,0:T(8,128)S(1)}, u32[]{:S(2)}, u32[]{:S(2)}) %collective-permute-start.2) | collective-permute-done | bytes 32800 | tf_op jit(solution)/shard_map/ppermute | solution.py:523
  27.6 1.4 %collective-permute-done.yb_ref = f32[32,512]{1,0:T(8,128)S(1)} collective-permute-done((f32[32,512]{1,0:T(8,128)S(1)}, f32[32,512]{1,0:T(8,128)S(1)}, u32[]{:S(2)}, u32[]{:S(2)}) %collective-permute-start) | collective-permute-done | bytes 65568 | tf_op jit(solution)/shard_map/ppermute | solution.py:525
  29.0 0.0 collective-permute-done.3.ya_ref
  29.0 0.0 copy-done.1
  29.0 2.5 %shard_map.99 = (f32[32,16,512]{2,1,0:T(8,128)}, f32[32,17,4,128]{3,2,1,0:T(4,128)}) custom-call(f32[32,16,512]{2,1,0:T(8,128)S(1)} %get-tuple-element.20.q_ref, f32[2,8,128]{2,1,0:T(8,128)S(1)} %get-tuple-element.21.sums_ref, f32[32,16,512]{2,1,0:T(8,128)S(1)} %copy-done.2, s32[32,16,512]{2,1,0:T(8,128)S(1)} %copy-done.5, ...), custom_call_target="tpu_custom_call" | custom-call | tf_op jit(solution)/shard_map/pallas_call | solution.py:531
  31.5 0.9 all-to-all-done.recv_ref
  32.4 6.7 %all-to-all-start.1 = ((f32[32,17,4,128]{3,2,1,0:T(4,128)}), f32[32,17,4,128]{3,2,1,0:T(4,128)}, u32[]{:S(2)}, u32[]{:S(2)}) async-start(f32[32,17,4,128]{3,2,1,0:T(4,128)} %get-tuple-element.26), calls=%async_computation.1 | async-start | bytes 2228224 | tf_op jit(solution)/shard_map/all_to_all | solution.py:492
  39.1 4.8 %shard_map.96 = (f32[32,16,512]{2,1,0:T(8,128)}, f32[32,16,512]{2,1,0:T(8,128)}, f32[16,8,1,128]{3,2,1,0:T(1,128)S(1)}, f32[2,16,512]{2,1,0:T(8,128)S(1)}, f32[19,8,128]{2,1,0:T(8,128)S(1)}) custom-call(f32[32,8,8,128]{3,2,1,0:T(8,128)} %all-to-all-done.recv_ref, bf16[512,512]{1,0:T(8,128)(2,1)S(1)} %copy-done.1, bf16[512,512]{1,0:T(8,128)(2,1)S(1)} %copy-done, ...), custom_call_target="tpu_custom_call" | custom-call | tf_op jit(solution)/shard_map/pallas_call | solution.py:539
  43.9 12.9 %all-to-all-done.1.recv_hbm = f32[32,17,4,128]{3,2,1,0:T(4,128)} async-done(((f32[32,17,4,128]{3,2,1,0:T(4,128)}), f32[32,17,4,128]{3,2,1,0:T(4,128)}, u32[]{:S(2)}, u32[]{:S(2)}) %all-to-all-start.1) | async-done | bytes 1114144 | tf_op jit(solution)/shard_map/all_to_all | solution.py:492
  56.8 3.7 %shard_map.100 = (f32[32,16,512]{2,1,0:T(8,128)S(1)}, f32[16,17,1,128]{3,2,1,0:T(1,128)S(1)}) custom-call(f32[32,17,4,128]{3,2,1,0:T(4,128)} %all-to-all-done.1.recv_hbm, f32[32,16,512]{2,1,0:T(8,128)} %get-tuple-element.27.zr_hbm, f32[16,8,1,128]{3,2,1,0:T(1,128)S(1)} %get-tuple-element.28.states_ref, f32[2,16,512]{2,1,0:T(8,128)S(1)} %get-tuple-element.29.table_ref, ...), custom_call_target="tpu_custom_call" | custom-call | tf_op jit(solution)/shard_map/pallas_call | solution.py:551
  60.5 25.8 %all_to_all.25.recv_ref = f32[16,17,1,128]{3,2,1,0:T(1,128)S(1)} all-to-all(f32[16,17,1,128]{3,2,1,0:T(1,128)S(1)} %get-tuple-element.31), channel_id=1, replica_groups=mesh['grp'=16,'pen'=32] {'grp'}, dimensions={0} | all-to-all | bytes 278528 | tf_op jit(solution)/shard_map/all_to_all | solution.py:492
  86.4 0.3 shard_map.101
  86.7 18.3 %all_to_all.26.recv_ref = f32[16,9,1,128]{3,2,1,0:T(1,128)S(1)} all-to-all(f32[16,9,1,128]{3,2,1,0:T(1,128)S(1)} %get-tuple-element.33), channel_id=1, replica_groups=mesh['grp'=16,'pen'=32] {'grp'}, dimensions={0} | all-to-all | bytes 147456 | tf_op jit(solution)/shard_map/all_to_all | solution.py:492
  105.0 0.0 copy-done.6
  105.0 2.7 %shard_map.102 = f32[32,17,4,128]{3,2,1,0:T(4,128)S(1)} custom-call(f32[32,16,512]{2,1,0:T(8,128)S(1)} %copy-done.6, f32[32,16,512]{2,1,0:T(8,128)S(1)} %get-tuple-element.30.fq_ref, f32[16,9,1,128]{3,2,1,0:T(1,128)S(1)} %all_to_all.26.recv_ref, f32[3,8,128]{2,1,0:T(8,128)S(1)} %get-tuple-element.34.control_ref, ...), custom_call_target="tpu_custom_call" | custom-call | tf_op jit(solution)/shard_map/pallas_call | solution.py:564
  107.7 24.0 %all_to_all.27.recv_ref = f32[32,17,4,128]{3,2,1,0:T(4,128)S(1)} all-to-all(f32[32,17,4,128]{3,2,1,0:T(4,128)S(1)} %shard_map.102), channel_id=1, replica_groups=mesh['grp'=16,'pen'=32] {'pen'}, dimensions={0} | all-to-all | bytes 2228224 | tf_op jit(solution)/shard_map/all_to_all | solution.py:492
  131.8 2.5 %shard_map.103 = (f32[32,16,512]{2,1,0:T(8,128)}, f32[32,16,512]{2,1,0:T(8,128)}) custom-call(f32[32,17,4,128]{3,2,1,0:T(4,128)S(1)} %all_to_all.27.recv_ref, f32[32,16,512]{2,1,0:T(8,128)S(1)} %copy-done.3, f32[32,16,512]{2,1,0:T(8,128)S(1)} %copy-done.2, f32[32,16,512]{2,1,0:T(8,128)S(1)} %copy-done.7, f32[3,8,128]{2,1,0:T(8,128)S(1)} %get-tuple-element.34.control_ref, ...), custom_call_target="tpu_custom_call" | custom-call | tf_op jit(solution)/shard_map/pallas_call | solution.py:573
  (14 shorter events, 0.0 us)
Async XLA Ops:
  4.0 11.3 %copy-start.2 = (f32[32,16,512]{2,1,0:T(8,128)S(1)}, f32[32,16,512]{2,1,0:T(8,128)}, u32[]{:S(2)}) copy-start(f32[32,16,512]{2,1,0:T(8,128)} %d_ref.7) | copy-start | bytes 3145732
  4.0 11.3 %copy-start.4 = (s32[32,16,512]{2,1,0:T(8,128)S(1)}, s32[32,16,512]{2,1,0:T(8,128)}, u32[]{:S(2)}) copy-start(s32[32,16,512]{2,1,0:T(8,128)} %m_ref.5) | copy-start | bytes 3145732
  4.0 28.3 %all-to-all-start = ((f32[32,8,8,128]{3,2,1,0:T(8,128)}), f32[32,8,8,128]{3,2,1,0:T(8,128)}, u32[]{:S(2)}, u32[]{:S(2)}) async-start(f32[32,8,8,128]{3,2,1,0:T(8,128)} %shard_map.95), calls=%async_computation | async-start | bytes 2097152 | tf_op jit(solution)/shard_map/all_to_all | solution.py:492
  15.3 8.5 %copy-start.3 = (f32[32,16,512]{2,1,0:T(8,128)S(1)}, f32[32,16,512]{2,1,0:T(8,128)}, u32[]{:S(2)}) copy-start(f32[32,16,512]{2,1,0:T(8,128)} %r_ref.3) | copy-start | bytes 3145732
  15.4 8.5 %copy-start.5 = (s32[32,16,512]{2,1,0:T(8,128)S(1)}, s32[32,16,512]{2,1,0:T(8,128)}, u32[]{:S(2)}) copy-start(s32[32,16,512]{2,1,0:T(8,128)} %m_ref.5) | copy-start | bytes 3145732
  15.5 13.5 %collective-permute-start = (f32[32,512]{1,0:T(8,128)S(1)}, f32[32,512]{1,0:T(8,128)S(1)}, u32[]{:S(2)}, u32[]{:S(2)}) collective-permute-start(f32[32,512]{1,0:T(8,128)S(1)} %get-tuple-element.22), channel_id=1, source_target_pairs={{1,2},{2,1},{3,4},{4,3},{5,6},{6,5},{7,8},{8,7},{9,10},{10,9},{11,... | collective-permute-start | bytes 196616 | tf_op jit(solution)/shard_map/ppermute | solution.py:525
  19.1 9.8 %collective-permute-start.3 = (f32[32,512]{1,0:T(8,128)S(1)}, f32[32,512]{1,0:T(8,128)S(1)}, u32[]{:S(2)}, u32[]{:S(2)}) collective-permute-start(f32[32,512]{1,0:T(8,128)S(1)} %get-tuple-element.25), channel_id=1, source_target_pairs={{0,1},{1,0},{2,3},{3,2},{4,5},{5,4},{6,7},{7,6},{8,9},{9,8},{10,11... | collective-permute-start | bytes 196616 | tf_op jit(solution)/shard_map/ppermute | solution.py:527
  21.1 4.2 %collective-permute-start.1 = (f32[1,16,512]{2,1,0:T(8,128)S(1)}, f32[1,16,512]{2,1,0:T(8,128)S(1)}, u32[]{:S(2)}, u32[]{:S(2)}) collective-permute-start(f32[1,16,512]{2,1,0:T(8,128)S(1)} %get-tuple-element.23), channel_id=1, source_target_pairs={{0,32},{32,64},{64,96},{96,128},{128,160},{160,192},{192,224},{224... | collective-permute-start | bytes 98312 | tf_op jit(solution)/shard_map/ppermute | solution.py:520
  22.4 6.6 %copy-start = (bf16[512,512]{1,0:T(8,128)(2,1)S(1)}, bf16[512,512]{1,0:T(8,128)(2,1)}, u32[]{:S(2)}) copy-start(bf16[512,512]{1,0:T(8,128)(2,1)} %constant.11.clone.cl_hbm.cl_ref) | copy-start | bytes 1572868
  22.4 6.6 %copy-start.1 = (bf16[512,512]{1,0:T(8,128)(2,1)S(1)}, bf16[512,512]{1,0:T(8,128)(2,1)}, u32[]{:S(2)}) copy-start(bf16[512,512]{1,0:T(8,128)(2,1)} %constant.10.clone.ch_hbm.ch_ref) | copy-start | bytes 1572868
  22.4 5.2 %collective-permute-start.2 = (f32[1,16,512]{2,1,0:T(8,128)S(1)}, f32[1,16,512]{2,1,0:T(8,128)S(1)}, u32[]{:S(2)}, u32[]{:S(2)}) collective-permute-start(f32[1,16,512]{2,1,0:T(8,128)S(1)} %get-tuple-element.24), channel_id=1, source_target_pairs={{32,0},{64,32},{96,64},{128,96},{160,128},{192,160},{224,192},{256... | collective-permute-start | bytes 98312 | tf_op jit(solution)/shard_map/ppermute | solution.py:523
  32.4 6.7 %copy-start.8 = (f32[8,128]{1,0:T(8,128)S(1)}, f32[8,128]{1,0:T(8,128)}, u32[]{:S(2)}) copy-start(f32[8,128]{1,0:T(8,128)} %constant.14.clone.tile_ref) | copy-start | bytes 12292
  32.4 6.7 %copy-start.9 = (f32[1,512]{1,0:T(1,128)S(1)}, f32[1,512]{1,0:T(1,128)}, u32[]{:S(2)}) copy-start(f32[1,512]{1,0:T(1,128)} %constant.13.clone.ey_ref) | copy-start | bytes 6148
  32.4 6.7 %copy-start.10 = (f32[512]{0:T(512)S(1)}, f32[512]{0:T(512)}, u32[]{:S(2)}) copy-start(f32[512]{0:T(512)} %constant.12.clone.ez_ref) | copy-start | bytes 6148
  32.4 24.4 %all-to-all-start.1 = ((f32[32,17,4,128]{3,2,1,0:T(4,128)}), f32[32,17,4,128]{3,2,1,0:T(4,128)}, u32[]{:S(2)}, u32[]{:S(2)}) async-start(f32[32,17,4,128]{3,2,1,0:T(4,128)} %get-tuple-element.26), calls=%async_computation.1 | async-start | bytes 2228224 | tf_op jit(solution)/shard_map/all_to_all | solution.py:492
  56.8 48.2 %copy-start.6 = (f32[32,16,512]{2,1,0:T(8,128)S(1)}, f32[32,16,512]{2,1,0:T(8,128)}, u32[]{:S(2)}) copy-start(f32[32,16,512]{2,1,0:T(8,128)} %get-tuple-element.19.fr_ref) | copy-start | bytes 3145732
  107.7 24.1 %copy-start.7 = (f32[32,16,512]{2,1,0:T(8,128)S(1)}, f32[32,16,512]{2,1,0:T(8,128)}, u32[]{:S(2)}) copy-start(f32[32,16,512]{2,1,0:T(8,128)} %get-tuple-element.35.q_ref) | copy-start | bytes 3145732
